TPU v7x, 32 devices: a whole 2x2x4 slice. The times are simulated.
32 devices in a mesh: rows: 8 (over z, y), mem: 4 (over x, core).
Axes of the slice: x: 2, y: 2, z: 4, core: 2. Of those that a mesh axis runs over, the one named last changes fastest.
Arguments:
- state: float32 [2048, 5120], P('rows', 'mem')
- member_level: int32 [5120], P('mem'), may hold values from 0 to 3, as said below
- level_weight: float32 [4], replicated, may hold values from 0.3 to 3
- obs_row: int32 [128], replicated, may hold values from 0 to 2047
- state_coords: int32 [2, 2048], replicated, may hold values from 0 to 63, as said below
- weights: float32 [128, 5120], P('rows', 'mem'), may hold values from -6 to 6
Outputs:
- increment: float32 [2048, 5120], P('rows', 'mem')
Inputs may be any that keep to these rules, and one draw needn't show every extreme that they name: `member_level`: every one of the 4 levels holds at least 2 members. `state_coords`: the first coordinate of row i lies within 2 of i // 64.
All inputs are finite; a program needn't handle non-finite values.
Results may differ from a plain program's by a relative error of at most 0.000073.
Values sent between devices are 32-bit elements; how exact they have to be, the bound alone decides.
No kernel may reach another device: no remote copies, remote signals or barrier semaphores. Data moves between devices by JAX's collectives and lax.ppermute only.
A program may use at most 64 MiB of HBM per device.

v0:
```python
import jax
import jax.numpy as jnp
from jax import lax
from jax.sharding import PartitionSpec as P

LEVELS = 4
XCOL_DEV = 4


def taper_rows(state_coords, obs_row, row_first, row_total, radius):
    state_xy = lax.dynamic_slice_in_dim(state_coords, row_first, row_total, 1)
    observed_xy = jnp.take(state_coords, obs_row, axis=1)
    offset_x = state_xy[0][:, None] - observed_xy[0][None, :]
    offset_y = state_xy[1][:, None] - observed_xy[1][None, :]
    distance = offset_x * offset_x + offset_y * offset_y
    reach = jnp.maximum(0.0, 1.0 - distance.astype(jnp.float32) / float(radius * radius))
    return reach * reach


def on_device(state, member_level, level_weight, obs_row, state_coords, weights):
    highest = lax.Precision.HIGHEST
    radius = XCOL_DEV * lax.axis_size("rows")
    row_count = state.shape[0]
    row_first = lax.axis_index("rows") * row_count
    onehot = (member_level[:, None] == jnp.arange(LEVELS, dtype=jnp.int32)[None, :]).astype(
        jnp.float32
    )
    part_sums = jnp.dot(state, onehot, precision=highest, preferred_element_type=jnp.float32)
    part_counts = jnp.sum(onehot, axis=0)
    sums, counts = lax.psum((part_sums, part_counts), "mem")
    means = sums / counts[None, :]
    anomaly = state - jnp.take(means, member_level, axis=1)
    level_scale = level_weight / (counts - 1.0)
    scaled = anomaly * jnp.take(level_scale, member_level)[None, :]
    wanted = obs_row - row_first
    inside = (wanted >= 0) & (wanted < row_count)
    picked = jnp.take(anomaly, jnp.clip(wanted, 0, row_count - 1), axis=0)
    observed = lax.psum(jnp.where(inside[:, None], picked, 0.0), "rows")
    cross = jnp.dot(scaled, observed.T, precision=highest, preferred_element_type=jnp.float32)
    summed = lax.psum(cross, "mem")
    tapered = summed * taper_rows(state_coords, obs_row, row_first, row_count, radius)
    all_weights = lax.all_gather(weights, "rows", axis=0, tiled=True)
    return jnp.dot(tapered, all_weights, precision=highest, preferred_element_type=jnp.float32)


def solution(mesh):
    in_specs = (P("rows", "mem"), P("mem"), P(), P(), P(), P("rows", "mem"))
    out_specs = P("rows", "mem")
    return jax.shard_map(
        on_device, mesh=mesh, in_specs=in_specs, out_specs=out_specs, check_vma=False
    )
```

profile of v0, /device:TPU:0, one launch (start us, length us, event | category | flops | bytes accessed | tf_op | source)
XLA Modules:
  0.0 149.0 jit_solution(10090916671518667911)
XLA Ops:
  6.5 0.0 all-reduce.4.cloned.1.call-start
  6.5 0.9 convert_reduce_fusion
  7.5 0.7 compare_select_fusion
  8.2 2.0 %convolution_bitcast_fusion = f32[256,4]{0,1:T(4,128)S(1)} fusion(f32[256,1280]{1,0:T(8,128)} %param.6, s32[1280]{0:T(1024)} %param.7), kind=kOutput, calls=%fused_computation.6 | convolution fusion | flops 15733760 | bytes 1319936 | tf_op jit(solution)/shard_map/dot_general | solution.py:28
  10.2 0.0 copy-done
  10.2 0.1 copy-start.1
  10.2 0.0 copy-start.4
  10.2 1.5 copy.13
  11.8 8.5 %all-reduce = (f32[256,4]{0,1:T(4,128)S(1)}, f32[4]{0:T(128)S(1)}) all-reduce(f32[256,4]{0,1:T(4,128)S(1)} %convolution_bitcast_fusion, f32[4]{0:T(128)S(1)} %convert_reduce_fusion), channel_id=1, replica_groups=mesh['rows'=8,'mem'=4] {'mem'}, use_global_device_ids=true, to_apply=%region_0.0 | all-reduce | flops 1028 | bytes 8224 | tf_op jit(solution)/shard_map/psum | solution.py:30
  20.3 0.1 broadcast_divide_fusion
  20.3 3.2 %gather_fusion = f32[1280,256]{1,0:T(8,128)S(1)} fusion(f32[256,4]{0,1:T(4,128)S(1)} %broadcast_divide_fusion, s32[2048]{0:T(1024)S(1)} %pad_clamp_fusion), kind=kCustom, calls=%fused_computation | custom fusion | bytes 2626560 | tf_op jit(solution)/shard_map/jit(_take)/gather | solution.py:32
  23.5 1.6 %bitcast_subtract_fusion = f32[256,1280]{0,1:T(8,128)S(1)} fusion(f32[256,1280]{0,1:T(8,128)} %copy.13, f32[1280,256]{1,0:T(8,128)S(1)} %gather_fusion, pred[1280]{0:T(1024)(128)(4,1)S(1)} %compare_and_fusion), kind=kLoop, calls=%fused_computation.3 | loop fusion | flops 655360 | bytes 3933440 | tf_op jit(solution)/shard_map/sub | solution.py:32
  25.1 0.4 copy.14
  25.5 0.9 gather_fusion.1
  26.4 0.0 copy-start.5
  26.4 0.0 copy-start.3
  26.4 1.0 select_select_fusion
  27.4 0.0 all-reduce.4.cloned.1.call-update
  27.4 0.0 all-reduce.6.cloned.1.call-start
  27.5 0.4 copy.15
  27.9 0.6 gather_fusion.2
  28.5 0.1 select_bitcast_fusion
  28.6 0.6 fusion.26
  29.2 0.2 slice_reduce_fusion.1
  29.4 2.5 %select_select_fusion.1 = f32[1280]{0:T(1024)S(1)} fusion(f32[]{:T(128)} %bitcast.2, f32[]{:T(128)} %bitcast.3, f32[]{:T(128)} %bitcast.4, f32[]{:T(128)} %bitcast.5, s32[1280]{0:T(1024)S(1)} %copy-done.1), kind=kLoop, calls=%fused_computation.36 | loop fusion | flops 16640 | bytes 10256 | tf_op jit(solution)/shard_map/jit(_take)/select_n | solution.py:34
  31.9 32.5 %all_gather.3 = f32[128,1280]{1,0:T(8,128)S(1)} all-gather(f32[16,1280]{1,0:T(8,128)S(1)} %copy-done.2), channel_id=1, replica_groups=mesh['rows'=8,'mem'=4] {'rows'}, dimensions={0}, use_global_device_ids=true | all-gather | bytes 737280 | tf_op jit(solution)/shard_map/all_gather | solution.py:42
  64.4 39.5 %all-reduce.4.cloned.1.call-done = f32[128,1280]{1,0:T(8,128)} async-done(((f32[128,1280]{1,0:T(8,128)}), f32[128,1280]{1,0:T(8,128)}) %all-reduce.4.cloned.1.call-update) | async-done | bytes 655376 | tf_op jit(solution)/shard_map/psum | solution.py:38
  103.9 4.1 %fusion = f32[256,128]{1,0:T(8,128)} fusion(f32[128,1280]{1,0:T(8,128)} %all-reduce.4.cloned.1.call-done, f32[256,1280]{0,1:T(8,128)S(1)} %bitcast_subtract_fusion, f32[1280]{0:T(1024)S(1)} %select_select_fusion.1), kind=kOutput, calls=%fused_computation.4 | convolution fusion | flops 503644160 | bytes 2102272 | tf_op jit(solution)/shard_map/dot_general | solution.py:39
  108.1 0.0 all-reduce.6.cloned.1.call-update
  108.1 0.1 constant_dynamic-slice_fusion
  108.2 30.8 %all-reduce.6.cloned.1.call-done = f32[256,128]{1,0:T(8,128)} async-done(((f32[256,128]{1,0:T(8,128)}), f32[256,128]{1,0:T(8,128)}) %all-reduce.6.cloned.1.call-update) | async-done | bytes 131088 | tf_op jit(solution)/shard_map/psum | solution.py:40
  139.0 3.2 %fusion.3 = f32[256,1280]{1,0:T(8,128)} fusion(f32[128,1280]{1,0:T(8,128)S(1)} %all_gather.3, f32[256,128]{1,0:T(8,128)} %all-reduce.6.cloned.1.call-done, s32[128]{0:T(128)S(1)} %get-tuple-element.6, s32[256]{0:T(256)S(1)} %bitcast.16, s32[128]{0:T(128)S(1)} %get-tuple-element.5, s32[256]{0:T(256)S(1)} %bitcast.15), kind=kOutput, calls=%fused_computation.9 | convolution fusion | flops 503676928 | bytes 2100224 | tf_op jit(solution)/shard_map/dot_general | solution.py:43
  (14 shorter events, 0.1 us)
Async XLA Ops:
  6.5 3.6 %copy-start = (f32[256,1280]{1,0:T(8,128)S(1)}, f32[256,1280]{1,0:T(8,128)}, u32[]{:S(2)}) copy-start(f32[256,1280]{1,0:T(8,128)} %param.6) | copy-start | bytes 3932164
  6.5 97.4 %all-reduce.4.cloned.1.call-start = ((), (), s32[]{:S(2)}) async-start(), calls=%async_computation | async-start | bytes 1310720 | tf_op jit(solution)/shard_map/psum | solution.py:38
  10.2 1.5 %copy-start.1 = (s32[1280]{0:T(1024)S(1)}, s32[1280]{0:T(1024)}, u32[]{:S(2)}) copy-start(s32[1280]{0:T(1024)} %param.7) | copy-start | bytes 15364
  10.2 1.5 %copy-start.4 = (s32[128]{0:T(128)S(1)}, s32[128]{0:T(128)}, u32[]{:S(2)}) copy-start(s32[128]{0:T(128)} %param.9) | copy-start | bytes 1540
  26.4 1.1 copy-start.5
  26.4 1.1 copy-start.3
  27.4 4.5 %copy-start.2 = (f32[16,1280]{1,0:T(8,128)S(1)}, f32[16,1280]{1,0:T(8,128)}, u32[]{:S(2)}) copy-start(f32[16,1280]{1,0:T(8,128)} %param.11) | copy-start | bytes 245764
  27.4 111.6 %all-reduce.6.cloned.1.call-start = ((), (), s32[]{:S(2)}) async-start(), calls=%async_computation.1 | async-start | bytes 262144 | tf_op jit(solution)/shard_map/psum | solution.py:40
Sparse Core Ops, SparseCore 0:
  27.5 76.3 all-reduce.3
  108.2 30.6 all-reduce.5
where the time goes:
time: 149 us
  waiting for transfers between devices  70.3 us (47%)
  blocking collectives  41 us (28%)
  between operations  13.6 us (9%)
  matrix products  9.34 us (6%)
  local copies, waits for them, and re-layouts  7.88 us (5%)
  other arithmetic  6.83 us (5%)
    psum x1, waiting for transfers between devices, on_device(): observed = lax.psum(jnp.where(inside[:, None], picked, 0.0), 'rows')  39.5 us
    all_gather x1, blocking collectives, on_device(): all_weights = lax.all_gather(weights, 'rows', axis=0, tiled=True)  32.5 us
    psum x1, waiting for transfers between devices, on_device(): summed = lax.psum(cross, 'mem')  30.8 us
    psum x1, blocking collectives, on_device(): sums, counts = lax.psum((part_sums, part_counts), 'mem')  8.48 us
    dot_general x1, matrix products, on_device(): jnp.dot(scaled, observed.T, precision=highest, preferred_element_type=jnp...  4.14 us
    dot_general x1, matrix products, on_device(): jnp.dot(tapered, all_weights, precision=highest, preferred_element_type=j...  3.2 us
    gather x1, local copies, waits for them, and re-layouts, on_device(): anomaly = state - jnp.take(means, member_level, axis=1)  3.15 us
  transfers between devices with their start and end apart: 2, of which 2 were waited for; matrix products, arithmetic and copies ran while one was open for 3% of the time, Pallas kernels for 0%

commit v1 on v0

v1 whole, which is shorter than its diff:
```python
import functools
import math

import jax
import jax.numpy as jnp
from jax import lax
from jax.experimental import pallas as pl
from jax.experimental.pallas import tpu as pltpu
from jax.sharding import PartitionSpec as P

LEVELS = 4
XCOL_DEV = 4
SUB = 8
VMEM_LIMIT = 48 * 1024 * 1024
F32 = jnp.float32
BF16 = jnp.bfloat16
LANES_BOTH = (((1,), (1,)), ((), ()))
ROWS_BOTH = (((0,), (0,)), ((), ()))
PLAIN = (((1,), (0,)), ((), ()))


def dot(a, b, dims):
    return lax.dot_general(a, b, dims, preferred_element_type=F32)


def split(x, parts):
    pieces = []
    for _ in range(parts - 1):
        piece = x.astype(BF16)
        pieces.append(piece)
        x = x - piece.astype(F32)
    pieces.append(x.astype(BF16))
    return pieces


def level_onehot(level_row):
    levels = lax.broadcasted_iota(jnp.int32, (SUB, level_row.shape[1]), 0)
    return (level_row == levels).astype(F32)


def by_level(level_row, columns):
    picked = jnp.where(level_row == 1, columns[1], columns[0])
    for level in range(2, LEVELS):
        picked = jnp.where(level_row == level, columns[level], picked)
    return picked


def pick_kernel(obs_ref, skip_ref, state_ref, out_ref):
    rows = state_ref.shape[0]
    slots = out_ref.shape[0]
    row_first = lax.axis_index("rows") * rows
    skip = skip_ref[0]

    def visit(j, rank):
        row = obs_ref[j] - row_first
        mine = (row >= 0) & (row < rows)
        slot = rank - skip

        @pl.when(mine & (slot >= 0) & (slot < slots))
        def _():
            out_ref[pl.ds(slot, 1), :] = state_ref[pl.ds(row, 1), :]

        return rank + mine.astype(jnp.int32)

    total = lax.fori_loop(0, obs_ref.shape[0], visit, 0, unroll=8)

    def clear(slot, carry):
        out_ref[pl.ds(slot, 1), :] = jnp.zeros((1, out_ref.shape[1]), F32)
        return carry

    lax.fori_loop(jnp.clip(total - skip, 0, slots), slots, clear, 0)


def pick(obs_row, skip, state, slots):
    smem = pl.BlockSpec(memory_space=pltpu.SMEM)
    vmem = pl.BlockSpec(memory_space=pltpu.VMEM)
    return pl.pallas_call(
        pick_kernel,
        out_shape=jax.ShapeDtypeStruct((slots, state.shape[1]), F32),
        in_specs=[smem, smem, vmem],
        out_specs=vmem,
        compiler_params=pltpu.CompilerParams(vmem_limit_bytes=VMEM_LIMIT),
        name="pick",
    )(obs_row, skip, state)


def center_kernel(level_ref, state_ref, sums_ref, high_ref, low_ref):
    level_row = level_ref[...]
    onehot = level_onehot(level_row)
    counts = jnp.sum(onehot, axis=1, keepdims=True)
    state = state_ref[...]
    hot = onehot.astype(BF16)
    sums = sum(dot(hot, piece, LANES_BOTH) for piece in split(state, 3))
    sums_ref[0:LEVELS, :] = sums[0:LEVELS, :]
    sums_ref[LEVELS:SUB, :] = jnp.broadcast_to(counts[0:LEVELS, :], (LEVELS, sums.shape[1]))
    means = jnp.transpose(sums / jnp.maximum(counts, 1.0))
    columns = [means[:, level : level + 1] for level in range(LEVELS)]
    high, low = split(state - by_level(level_row, columns), 2)
    high_ref[...] = high
    low_ref[...] = low


def center(level_row, state):
    rows, members = state.shape
    vmem = pl.BlockSpec(memory_space=pltpu.VMEM)
    return pl.pallas_call(
        center_kernel,
        out_shape=(
            jax.ShapeDtypeStruct((SUB, rows), F32),
            jax.ShapeDtypeStruct((rows, members), BF16),
            jax.ShapeDtypeStruct((rows, members), BF16),
        ),
        in_specs=[vmem, vmem],
        out_specs=(vmem, vmem, vmem),
        compiler_params=pltpu.CompilerParams(vmem_limit_bytes=VMEM_LIMIT),
        name="center",
    )(level_row, state)


def cross_kernel(number, slots, weight_ref, skip_ref, level_ref, counts_ref, place_ref, high_ref, low_ref, before_ref, *refs):
    blocks, out_ref = refs[: len(number)], refs[len(number)]
    o_high, o_low, p_ref, m_ref = refs[len(number) + 1 :]
    rows = high_ref.shape[0]
    me = lax.axis_index("rows")
    skip = skip_ref[0]
    level_row = level_ref[...]
    onehot = level_onehot(level_row)
    counts = jnp.maximum(jnp.sum(onehot, axis=1, keepdims=True), 1.0)
    total = jnp.sum(counts_ref[...], axis=0)
    scales = [weight_ref[level] / (total[level, 0] - 1.0) for level in range(LEVELS)]
    member_scale = by_level(level_row, scales)
    owner, rank = place_ref[0:1, :], place_ref[1:2, :]
    padded = o_high.shape[0] // len(number)
    m_ref[...] = jnp.zeros_like(m_ref)
    for n, block_ref in enumerate(blocks):
        at = n * padded
        block = block_ref[...]
        columns = []
        for level in range(LEVELS):
            member = jnp.where(level_row == level, block, 0.0)
            columns.append(jnp.sum(member, axis=1, keepdims=True) / counts[level : level + 1, :])
            m_ref[at : at + slots, level : level + 1] = columns[level]
        high, low = split((block - by_level(level_row, columns)) * member_scale, 2)
        o_high[at : at + slots, :] = high
        o_low[at : at + slots, :] = low
        slot = lax.broadcasted_iota(jnp.int32, (slots, owner.shape[1]), 0)
        hit = (owner == (me ^ number[n])) & (rank - skip == slot)
        p_ref[at : at + slots, :] = hit.astype(BF16)
    by_slot = dot(high_ref[...], o_high[...], LANES_BOTH)
    by_slot += dot(high_ref[...], o_low[...], LANES_BOTH)
    by_slot += dot(low_ref[...], o_high[...], LANES_BOTH)
    place = p_ref[...]
    cross = sum(dot(piece, place, PLAIN) for piece in split(by_slot, 3))
    out_ref[0:rows, :] = before_ref[0:rows, :] + cross
    means = sum(dot(piece, place, ROWS_BOTH) for piece in split(m_ref[...], 3))
    out_ref[rows : rows + SUB, :] = before_ref[rows : rows + SUB, :] + means


def cross_part(level_weight, skip, level_row, counts, place, high, low, before, blocks, number):
    rows, members = high.shape
    slots = blocks[0].shape[0]
    smem = pl.BlockSpec(memory_space=pltpu.SMEM)
    vmem = pl.BlockSpec(memory_space=pltpu.VMEM)
    held = len(number) * slots
    return pl.pallas_call(
        functools.partial(cross_kernel, number, slots),
        out_shape=jax.ShapeDtypeStruct(before.shape, F32),
        in_specs=[smem, smem] + [vmem] * (6 + len(number)),
        out_specs=vmem,
        scratch_shapes=[
            pltpu.VMEM((held, members), BF16),
            pltpu.VMEM((held, members), BF16),
            pltpu.VMEM((held, before.shape[1]), BF16),
            pltpu.VMEM((held, SUB), F32),
        ],
        compiler_params=pltpu.CompilerParams(vmem_limit_bytes=VMEM_LIMIT),
        name="cross_part",
    )(level_weight, skip, level_row, counts, place, high, low, before, *blocks)


def final_kernel(number, weight_ref, parts_ref, sums_ref, taper_ref, *refs):
    blocks, out_ref = refs[: len(number)], refs[len(number)]
    t_high, t_low, w_high, w_low = refs[len(number) + 1 :]
    step = pl.program_id(0)
    rows = taper_ref.shape[0]
    me = lax.axis_index("rows")
    mem = parts_ref.shape[0]

    @pl.when(step == 0)
    def _():
        cross = sum(parts_ref[d, 0:rows, :] for d in range(mem))
        counts = [sums_ref[d, LEVELS:SUB, :] for d in range(mem)]
        sums = [sums_ref[d, 0:LEVELS, :] for d in range(mem)]
        total = sum(counts)
        mean = sum(sums) / total
        level = lax.broadcasted_iota(jnp.int32, (LEVELS, 1), 0)
        scale = by_level(level, [weight_ref[k] for k in range(LEVELS)]) / (total - 1.0)
        me_mem = lax.axis_index("mem")
        seen = [parts_ref[me_mem ^ d, rows : rows + LEVELS, :] for d in range(mem)]
        seen_counts = [c[:, 0:1] for c in counts]
        seen_mean = sum(c * s for c, s in zip(seen_counts, seen)) / total[:, 0:1]
        left, right = [], []
        for d in range(mem):
            left.append(scale * (sums[d] - counts[d] * mean))
            right.append(jnp.where(seen_counts[d] > 0.0, seen[d] - seen_mean, 0.0))
        left = split(jnp.concatenate(left, axis=0), 2)
        right = split(jnp.concatenate(right, axis=0), 2)
        cross += dot(left[0], right[0], ROWS_BOTH)
        cross += dot(left[0], right[1], ROWS_BOTH)
        cross += dot(left[1], right[0], ROWS_BOTH)
        high, low = split(cross * taper_ref[...], 2)
        t_high[...] = high
        t_low[...] = low

    for n, block_ref in enumerate(blocks):
        length = block_ref.shape[0]
        at = pl.multiple_of((me ^ number[n]) * length, length)
        high, low = split(block_ref[...], 2)
        w_high[pl.ds(at, length), :] = high
        w_low[pl.ds(at, length), :] = low
    out = dot(t_high[...], w_high[...], PLAIN)
    out += dot(t_high[...], w_low[...], PLAIN)
    out += dot(t_low[...], w_high[...], PLAIN)
    out_ref[...] = out


def final(level_weight, parts, sums, taper, blocks, number):
    rows, observed = taper.shape
    length, members = blocks[0].shape
    width = math.gcd(members, 256)
    smem = pl.BlockSpec(memory_space=pltpu.SMEM)
    vmem = pl.BlockSpec(memory_space=pltpu.VMEM)
    return pl.pallas_call(
        functools.partial(final_kernel, number),
        out_shape=jax.ShapeDtypeStruct((rows, members), F32),
        grid=(members // width,),
        in_specs=[smem, vmem, vmem, vmem] + [pl.BlockSpec((length, width), lambda i: (0, i))] * len(number),
        out_specs=pl.BlockSpec((rows, width), lambda i: (0, i)),
        scratch_shapes=[
            pltpu.VMEM((rows, observed), BF16),
            pltpu.VMEM((rows, observed), BF16),
            pltpu.VMEM((observed, width), BF16),
            pltpu.VMEM((observed, width), BF16),
        ],
        compiler_params=pltpu.CompilerParams(vmem_limit_bytes=VMEM_LIMIT),
        name="final",
    )(level_weight, parts, sums, taper, *blocks)


def across(x, axis, bits):
    count = lax.axis_size(axis)
    return lax.ppermute(x, axis, [(i, i ^ bits) for i in range(count)])


def line_order(count):
    line = [2 * s for s in range(1, count // 2)]
    return [0] + sorted(line, key=lambda b: (b != 4, b))


def gather_line(x, order):
    return [x] + [across(x, "rows", b) for b in order[1:]]


def taper_rows(state_coords, obs_row, row_first, row_total, radius):
    state_xy = lax.dynamic_slice_in_dim(state_coords, row_first, row_total, 1)
    observed_xy = jnp.take(state_coords, obs_row, axis=1)
    offset_x = state_xy[0][:, None] - observed_xy[0][None, :]
    offset_y = state_xy[1][:, None] - observed_xy[1][None, :]
    distance = offset_x * offset_x + offset_y * offset_y
    reach = jnp.maximum(0.0, 1.0 - distance.astype(F32) / float(radius * radius))
    return reach * reach


def on_device(state, member_level, level_weight, obs_row, state_coords, weights):
    groups = lax.axis_size("rows")
    radius = XCOL_DEV * groups
    row_count = state.shape[0]
    observed = obs_row.shape[0]
    row_first = lax.axis_index("rows") * row_count
    order = line_order(groups)
    pair = [b ^ 1 for b in order]
    slots = min(observed, 16 * (-(-2 * observed // groups) // 16))

    none = jnp.zeros((1,), jnp.int32)
    level_row = member_level[None, :]
    own = pick(obs_row, none, state, slots)
    line = gather_line(own, order)
    other = [across(x, "rows", 1) for x in line]

    sums, high, low = center(level_row, state)
    all_sums = jnp.stack([sums] + [across(sums, "mem", b) for b in range(1, lax.axis_size("mem"))])
    counts = all_sums[:, LEVELS:, 0:128]

    owner = obs_row // row_count
    same = owner[:, None] == owner[None, :]
    earlier = lax.broadcasted_iota(jnp.int32, same.shape, 1) < lax.broadcasted_iota(jnp.int32, same.shape, 0)
    rank = jnp.sum((same & earlier).astype(jnp.int32), axis=1)
    place = jnp.stack([owner, rank])
    rounds = jnp.max(rank) // slots + 1

    cross = functools.partial(cross_part, level_weight)
    empty = jnp.zeros((row_count + SUB, observed), F32)

    def more(carry):
        return carry[0] < rounds

    def another(carry):
        turn, part = carry
        skip = (turn * slots)[None]
        block = pick(obs_row, skip, state, slots)
        near = gather_line(block, order)
        far = [across(x, "rows", 1) for x in near]
        part = cross(skip, level_row, counts, place, high, low, part, near + far, order + pair)
        return turn + 1, part

    _, part = lax.while_loop(more, another, (jnp.int32(1), empty))
    part = cross(none, level_row, counts, place, high, low, part, line, order)
    part = cross(none, level_row, counts, place, high, low, part, other, pair)

    weights_line = gather_line(weights, order)
    weights_other = [across(x, "rows", 1) for x in weights_line]
    taper = taper_rows(state_coords, obs_row, row_first, row_count, radius)

    parts = lax.all_gather(part, "mem", axis=0)
    return final(level_weight, parts, all_sums, taper, weights_line + weights_other, order + pair)


def solution(mesh):
    in_specs = (P("rows", "mem"), P("mem"), P(), P(), P(), P("rows", "mem"))
    out_specs = P("rows", "mem")
    return jax.shard_map(
        on_device, mesh=mesh, in_specs=in_specs, out_specs=out_specs, check_vma=False
    )
```

time: 149 us -> 64 us (0.43)
  waiting for transfers between devices: 70.3 us -> 11.4 us
  blocking collectives: 41 us -> 7.25 us
  starting transfers between devices: 0.04 us -> 23.3 us
  Pallas kernels: 0 us -> 13.6 us
  between operations: 13.6 us -> 2.8 us
  matrix products: 9.34 us -> 0 us
  other arithmetic: 6.83 us -> 1.06 us
  local copies, waits for them, and re-layouts: 7.88 us -> 4.32 us
    psum x2 -> x0, waiting for transfers between devices: 70.3 us -> none  [the longest x1 39.5 us: on_device(): observed = lax.psum(jnp.where(inside[:, None], picked, 0.0), 'rows')]
    all_gather x1, blocking collectives: 32.5 us -> 7.25 us  [on_device(): parts = lax.all_gather(part, 'mem', axis=0)]
    ppermute x0 -> x17, starting transfers between devices: none -> 23.3 us  [across(): return lax.ppermute(x, axis, [(i, i ^ bits) for i in range(count)])]
    pallas_call x0 -> x5, Pallas kernels: none -> 13.6 us  [the longest x1 3.88 us: final(): pl.pallas_call(functools.partial(final_kernel, number), out_shape=jax.Sha...]
    ppermute x0 -> x17, waiting for transfers between devices: none -> 11.4 us  [across(): return lax.ppermute(x, axis, [(i, i ^ bits) for i in range(count)])]
    dot_general x3 -> x0, matrix products: 9.34 us -> none  [the longest x1 4.14 us: on_device(): jnp.dot(scaled, observed.T, precision=highest, preferred_element_type=jnp...]
    psum x1 -> x0, blocking collectives: 8.48 us -> none  [on_device(): sums, counts = lax.psum((part_sums, part_counts), 'mem')]
    gather x3 -> x0, local copies, waits for them, and re-layouts: 4.66 us -> none  [the longest x1 3.15 us: on_device(): anomaly = state - jnp.take(means, member_level, axis=1)]
  transfers between devices with their start and end apart: 2 -> 17, of which waited for: 2 -> 4; matrix products, arithmetic and copies ran while one was open for 3% -> 7% of each run, Pallas kernels for 0% -> 10%
where the time goes in v1:
time: 64 us; the launch traced here: 63.8 us
  starting transfers between devices  23.3 us (36%)
  Pallas kernels  13.6 us (21%)
  waiting for transfers between devices  11.4 us (18%)
  blocking collectives  7.25 us (11%)
  local copies, waits for them, and re-layouts  4.32 us (7%)
  between operations  2.8 us (4%)
  other arithmetic  1.06 us (2%)
    ppermute x17, starting transfers between devices, across(): return lax.ppermute(x, axis, [(i, i ^ bits) for i in range(count)])  23.3 us
    ppermute x17, waiting for transfers between devices, across(): return lax.ppermute(x, axis, [(i, i ^ bits) for i in range(count)])  11.4 us
    all_gather x1, blocking collectives, on_device(): parts = lax.all_gather(part, 'mem', axis=0)  7.25 us
    pallas_call x1, Pallas kernels, final(): pl.pallas_call(functools.partial(final_kernel, number), out_shape=jax.Sha...  3.88 us
    pallas_call x2, Pallas kernels, cross_part(): pl.pallas_call(functools.partial(cross_kernel, number, slots), out_shape=...  3.76 us
    pallas_call x1, Pallas kernels, center(): pl.pallas_call(center_kernel, out_shape=(jax.ShapeDtypeStruct((SUB, rows)...  3.58 us
    pallas_call x1, Pallas kernels, pick(): pl.pallas_call(pick_kernel, out_shape=jax.ShapeDtypeStruct((slots, state....  2.37 us
    gather x1, local copies, waits for them, and re-layouts, taper_rows(): observed_xy = jnp.take(state_coords, obs_row, axis=1)  1.87 us
  transfers between devices with their start and end apart: 17, of which 4 were waited for; matrix products, arithmetic and copies ran while one was open for 7% of the time, Pallas kernels for 10%

profile of v1, /device:TPU:0, one launch (start us, length us, event | category | flops | bytes accessed | tf_op | source)
XLA Modules:
  0.0 63.8 jit_solution(15614886519948982382)
XLA Ops:
  0.0 0.8 %broadcast_in_dim.23.level_ref = s32[1,1280]{1,0:T(1,128)S(1)} reshape(s32[1280]{0:T(1024)} %param.9) | data formatting | bytes 10240 | tf_op jit(solution)/shard_map/broadcast_in_dim | solution.py:285
  0.8 3.6 %center.1 = (f32[8,256]{1,0:T(8,128)S(1)}, bf16[256,1280]{1,0:T(8,128)(2,1)}, bf16[256,1280]{1,0:T(8,128)(2,1)}) custom-call(s32[1,1280]{1,0:T(1,128)S(1)} %broadcast_in_dim.23.level_ref, f32[256,1280]{1,0:T(8,128)} %state_ref.3), custom_call_target="tpu_custom_call" | custom-call | tf_op jit(solution)/shard_map/center/pallas_call | solution.py:106
  4.4 0.5 collective-permute-start.7
  4.8 2.5 %collective-permute-start.8 = (f32[8,256]{1,0:T(8,128)S(1)}, f32[8,256]{1,0:T(8,128)S(1)}, u32[]{:S(2)}, u32[]{:S(2)}) collective-permute-start(f32[8,256]{1,0:T(8,128)S(1)} %get-tuple-element.66), channel_id=1, source_target_pairs={{0,2},{1,3},{2,0},{3,1},{4,6},{5,7},{6,4},{7,5},{8,10},{9,11},{10,... | collective-permute-start | bytes 24584 | tf_op jit(solution)/shard_map/ppermute | solution.py:252
  7.3 0.1 collective-permute-start.9
  7.5 2.4 %pick.2.refs_0_ = f32[32,1280]{1,0:T(8,128)S(1)} custom-call(s32[128]{0:T(128)S(1)} %copy-done.6, s32[1]{0:T(128)} %constant.52.clone.1.skip_ref, f32[256,1280]{1,0:T(8,128)S(1)} %copy-done.1), custom_call_target="tpu_custom_call" | custom-call | tf_op jit(solution)/shard_map/pick/pallas_call | solution.py:77
  9.9 2.9 %collective-permute-start.10 = (f32[32,1280]{1,0:T(8,128)S(1)}, f32[32,1280]{1,0:T(8,128)S(1)}, u32[]{:S(2)}, u32[]{:S(2)}) collective-permute-start(f32[32,1280]{1,0:T(8,128)S(1)} %pick.2.refs_0_), channel_id=1, source_target_pairs={{0,16},{4,20},{8,24},{12,28},{16,0},{20,4},{24,8},{28,12},{1,17},{... | collective-permute-start | bytes 491528 | tf_op jit(solution)/shard_map/ppermute | solution.py:252
  12.7 0.2 convert_reduce_fusion
  12.9 0.6 %reduce_max.9 = s32[]{:T(128)} reduce(s32[128]{0:T(128)S(1)} %convert_reduce_fusion, s32[]{:T(128)} %constant.59.clone.1), dimensions={0}, to_apply=%region_1.2 | reduce | flops 127 | bytes 520 | tf_op jit(solution)/shard_map/reduce_max | solution.py:299
  16.3 1.6 %collective-permute-start.11 = (f32[32,1280]{1,0:T(8,128)S(1)}, f32[32,1280]{1,0:T(8,128)S(1)}, u32[]{:S(2)}, u32[]{:S(2)}) collective-permute-start(f32[32,1280]{1,0:T(8,128)S(1)} %pick.2.refs_0_), channel_id=1, source_target_pairs={{0,8},{4,12},{8,0},{12,4},{16,24},{20,28},{24,16},{28,20},{1,9},{5... | collective-permute-start | bytes 491528 | tf_op jit(solution)/shard_map/ppermute | solution.py:252
  18.0 1.9 %collective-permute-start.17 = (f32[16,1280]{1,0:T(8,128)S(1)}, f32[16,1280]{1,0:T(8,128)S(1)}, u32[]{:S(2)}, u32[]{:S(2)}) collective-permute-start(f32[16,1280]{1,0:T(8,128)S(1)} %copy-done), channel_id=1, source_target_pairs={{0,16},{4,20},{8,24},{12,28},{16,0},{20,4},{24,8},{28,12},{1,17},{... | collective-permute-start | bytes 245768 | tf_op jit(solution)/shard_map/ppermute | solution.py:252
  19.9 1.3 %copy.9 = s32[2,2048]{0,1:T(8,128)} copy(s32[2,2048]{1,0:T(2,128)S(1)} %copy-done.5) | data formatting | bytes 32768 | tf_op args[4]
  21.3 1.9 %gather_fusion = s32[128,2]{1,0:T(8,128)S(1)} fusion(s32[2,2048]{0,1:T(8,128)} %copy.9, s32[1024]{0:T(1024)S(1)} %pad_clamp_fusion), kind=kCustom, calls=%fused_computation | custom fusion | bytes 2560 | tf_op jit(solution)/shard_map/jit(_take)/gather | solution.py:266
  23.2 0.2 slice_reduce_fusion.1
  23.4 2.5 %collective-permute-start.18 = (f32[16,1280]{1,0:T(8,128)S(1)}, f32[16,1280]{1,0:T(8,128)S(1)}, u32[]{:S(2)}, u32[]{:S(2)}) collective-permute-start(f32[16,1280]{1,0:T(8,128)S(1)} %copy-done), channel_id=1, source_target_pairs={{0,8},{4,12},{8,0},{12,4},{16,24},{20,28},{24,16},{28,20},{1,9},{5... | collective-permute-start | bytes 245768 | tf_op jit(solution)/shard_map/ppermute | solution.py:252
  26.0 5.4 %collective-permute-done.17.refs_1_ = f32[16,1280]{1,0:T(8,128)S(1)} collective-permute-done((f32[16,1280]{1,0:T(8,128)S(1)}, f32[16,1280]{1,0:T(8,128)S(1)}, u32[]{:S(2)}, u32[]{:S(2)}) %collective-permute-start.17) | collective-permute-done | bytes 81952 | tf_op jit(solution)/shard_map/ppermute | solution.py:252
  31.4 1.6 %collective-permute-start.13 = (f32[32,1280]{1,0:T(8,128)S(1)}, f32[32,1280]{1,0:T(8,128)S(1)}, u32[]{:S(2)}, u32[]{:S(2)}) collective-permute-start(f32[32,1280]{1,0:T(8,128)S(1)} %pick.2.refs_0_), channel_id=1, source_target_pairs={{0,4},{4,0},{8,12},{12,8},{16,20},{20,16},{24,28},{28,24},{1,5},{5... | collective-permute-start | bytes 491528 | tf_op jit(solution)/shard_map/ppermute | solution.py:252
  33.0 3.5 %collective-permute-start.19 = (f32[16,1280]{1,0:T(8,128)S(1)}, f32[16,1280]{1,0:T(8,128)S(1)}, u32[]{:S(2)}, u32[]{:S(2)}) collective-permute-start(f32[16,1280]{1,0:T(8,128)S(1)} %copy-done), channel_id=1, source_target_pairs={{0,24},{4,28},{8,16},{12,20},{16,8},{20,12},{24,0},{28,4},{1,25},{... | collective-permute-start | bytes 245768 | tf_op jit(solution)/shard_map/ppermute | solution.py:252
  36.6 0.5 collective-permute-start.14
  37.0 1.5 %collective-permute-start.15 = (f32[32,1280]{1,0:T(8,128)S(1)}, f32[32,1280]{1,0:T(8,128)S(1)}, u32[]{:S(2)}, u32[]{:S(2)}) collective-permute-start(f32[32,1280]{1,0:T(8,128)S(1)} %collective-permute-done.11.refs_2_), channel_id=1, source_target_pairs={{0,4},{4,0},{8,12},{12,8},{16,20},{20,16},{24,28},{28,24},{1,5},{5... | collective-permute-start | bytes 491528 | tf_op jit(solution)/shard_map/ppermute | solution.py:252
  38.6 0.5 collective-permute-start.16
  39.2 1.9 %cross_part.3.before_ref = f32[264,128]{1,0:T(8,128)S(1)} custom-call(f32[4]{0:T(128)S(1)} %get-tuple-element.255, s32[1]{0:T(128)} %constant.52.clone.1.skip_ref, s32[1,1280]{1,0:T(1,128)S(1)} %get-tuple-element.253, f32[4,4,128]{2,1,0:T(4,128)S(1)} %get-tuple-element.252, s32[2,128]{1,0:T(2,128)S(1)} %get-tuple-element.254, ...), custom_call_target="tpu_custom_call" | custom-call | tf_op jit(solution)/shard_map/cross_part/pallas_call | solution.py:165
  41.1 1.6 %collective-permute-start.20 = (f32[16,1280]{1,0:T(8,128)S(1)}, f32[16,1280]{1,0:T(8,128)S(1)}, u32[]{:S(2)}, u32[]{:S(2)}) collective-permute-start(f32[16,1280]{1,0:T(8,128)S(1)} %copy-done), channel_id=1, source_target_pairs={{0,4},{4,0},{8,12},{12,8},{16,20},{20,16},{24,28},{28,24},{1,5},{5... | collective-permute-start | bytes 245768 | tf_op jit(solution)/shard_map/ppermute | solution.py:252
  42.7 0.5 collective-permute-start.21
  43.2 0.5 collective-permute-done.14.refs_1_
  43.7 1.0 %collective-permute-start.22 = (f32[16,1280]{1,0:T(8,128)S(1)}, f32[16,1280]{1,0:T(8,128)S(1)}, u32[]{:S(2)}, u32[]{:S(2)}) collective-permute-start(f32[16,1280]{1,0:T(8,128)S(1)} %collective-permute-done.18.refs_2_), channel_id=1, source_target_pairs={{0,4},{4,0},{8,12},{12,8},{16,20},{20,16},{24,28},{28,24},{1,5},{5... | collective-permute-start | bytes 245768 | tf_op jit(solution)/shard_map/ppermute | solution.py:252
  44.7 2.5 %collective-permute-done.15.refs_2_ = f32[32,1280]{1,0:T(8,128)S(1)} collective-permute-done((f32[32,1280]{1,0:T(8,128)S(1)}, f32[32,1280]{1,0:T(8,128)S(1)}, u32[]{:S(2)}, u32[]{:S(2)}) %collective-permute-start.15) | collective-permute-done | bytes 163872 | tf_op jit(solution)/shard_map/ppermute | solution.py:252
  47.2 0.5 collective-permute-start.23
  47.7 3.0 %collective-permute-done.16.refs_3_ = f32[32,1280]{1,0:T(8,128)S(1)} collective-permute-done((f32[32,1280]{1,0:T(8,128)S(1)}, f32[32,1280]{1,0:T(8,128)S(1)}, u32[]{:S(2)}, u32[]{:S(2)}) %collective-permute-start.16) | collective-permute-done | bytes 163872 | tf_op jit(solution)/shard_map/ppermute | solution.py:252
  50.7 1.9 %cross_part.4 = f32[264,128]{1,0:T(8,128)S(1)} custom-call(f32[4]{0:T(128)S(1)} %get-tuple-element.255, s32[1]{0:T(128)} %constant.52.clone.1.skip_ref, s32[1,1280]{1,0:T(1,128)S(1)} %get-tuple-element.253, f32[4,4,128]{2,1,0:T(4,128)S(1)} %get-tuple-element.252, s32[2,128]{1,0:T(2,128)S(1)} %get-tuple-element.254, bf16[256,1280]{1,0:T(8,128)(2,1)S(1)} %copy-done.2, ...), custom_call_target="tpu_custom_call" | custom-call | tf_op jit(solution)/shard_map/cross_part/pallas_call | solution.py:165
  52.6 7.3 %all-gather = f32[1056,128]{1,0:T(8,128)S(1)} all-gather(f32[264,128]{1,0:T(8,128)S(1)} %cross_part.4), channel_id=2, replica_groups=mesh['rows'=8,'mem'=4] {'mem'}, dimensions={0}, use_global_device_ids=true | all-gather | bytes 675840 | tf_op jit(solution)/shard_map/all_gather | solution.py:324
  59.9 3.9 %final.1 = f32[256,1280]{1,0:T(8,128)} custom-call(f32[4]{0:T(128)S(1)} %get-tuple-element.255, f32[4,264,128]{2,1,0:T(8,128)S(1)} %bitcast.14, f32[4,8,256]{2,1,0:T(8,128)S(1)} %pad_maximum_fusion.sums_ref, f32[256,128]{1,0:T(8,128)S(1)} %maximum_multiply_fusion.taper_ref, f32[16,1280]{1,0:T(8,128)S(1)} %copy-done, ...), custom_call_target="tpu_custom_call" | custom-call | tf_op jit(solution)/shard_map/final/pallas_call | solution.py:233
  (39 shorter events, 0.4 us)
Async XLA Ops:
  0.0 7.5 %copy-start.1 = (f32[256,1280]{1,0:T(8,128)S(1)}, f32[256,1280]{1,0:T(8,128)}, u32[]{:S(2)}) copy-start(f32[256,1280]{1,0:T(8,128)} %state_ref.3) | copy-start | bytes 3932164
  0.0 7.5 %copy-start.6 = (s32[128]{0:T(128)S(1)}, s32[128]{0:T(128)}, u32[]{:S(2)}) copy-start(s32[128]{0:T(128)} %obs_ref.1) | copy-start | bytes 1540
  0.8 15.4 %copy-start.4 = (f32[4]{0:T(128)S(1)}, f32[4]{0:T(128)}, u32[]{:S(2)}) copy-start(f32[4]{0:T(128)} %weight_ref.5) | copy-start | bytes 52
  4.4 11.8 %collective-permute-start.7 = (f32[8,256]{1,0:T(8,128)S(1)}, f32[8,256]{1,0:T(8,128)S(1)}, u32[]{:S(2)}, u32[]{:S(2)}) collective-permute-start(f32[8,256]{1,0:T(8,128)S(1)} %get-tuple-element.66), channel_id=1, source_target_pairs={{0,1},{1,0},{2,3},{3,2},{4,5},{5,4},{6,7},{7,6},{8,9},{9,8},{10,11... | collective-permute-start | bytes 24584 | tf_op jit(solution)/shard_map/ppermute | solution.py:252
  4.8 11.3 %collective-permute-start.8 = (f32[8,256]{1,0:T(8,128)S(1)}, f32[8,256]{1,0:T(8,128)S(1)}, u32[]{:S(2)}, u32[]{:S(2)}) collective-permute-start(f32[8,256]{1,0:T(8,128)S(1)} %get-tuple-element.66), channel_id=1, source_target_pairs={{0,2},{1,3},{2,0},{3,1},{4,6},{5,7},{6,4},{7,5},{8,10},{9,11},{10,... | collective-permute-start | bytes 24584 | tf_op jit(solution)/shard_map/ppermute | solution.py:252
  7.3 8.9 %collective-permute-start.9 = (f32[8,256]{1,0:T(8,128)S(1)}, f32[8,256]{1,0:T(8,128)S(1)}, u32[]{:S(2)}, u32[]{:S(2)}) collective-permute-start(f32[8,256]{1,0:T(8,128)S(1)} %get-tuple-element.66), channel_id=1, source_target_pairs={{0,3},{1,2},{2,1},{3,0},{4,7},{5,6},{6,5},{7,4},{8,11},{9,10},{10,... | collective-permute-start | bytes 24584 | tf_op jit(solution)/shard_map/ppermute | solution.py:252
  9.9 26.7 %collective-permute-start.10 = (f32[32,1280]{1,0:T(8,128)S(1)}, f32[32,1280]{1,0:T(8,128)S(1)}, u32[]{:S(2)}, u32[]{:S(2)}) collective-permute-start(f32[32,1280]{1,0:T(8,128)S(1)} %pick.2.refs_0_), channel_id=1, source_target_pairs={{0,16},{4,20},{8,24},{12,28},{16,0},{20,4},{24,8},{28,12},{1,17},{... | collective-permute-start | bytes 491528 | tf_op jit(solution)/shard_map/ppermute | solution.py:252
  16.3 1.7 %copy-start = (f32[16,1280]{1,0:T(8,128)S(1)}, f32[16,1280]{1,0:T(8,128)}, u32[]{:S(2)}) copy-start(f32[16,1280]{1,0:T(8,128)} %refs_0_.1) | copy-start | bytes 245764
  16.3 3.6 %copy-start.5 = (s32[2,2048]{1,0:T(2,128)S(1)}, s32[2,2048]{1,0:T(2,128)}, u32[]{:S(2)}) copy-start(s32[2,2048]{1,0:T(2,128)} %param.12) | copy-start | bytes 49156
  16.3 22.9 %copy-start.2 = (bf16[256,1280]{1,0:T(8,128)(2,1)S(1)}, bf16[256,1280]{1,0:T(8,128)(2,1)}, u32[]{:S(2)}) copy-start(bf16[256,1280]{1,0:T(8,128)(2,1)} %get-tuple-element.250) | copy-start | bytes 1966084
  16.3 22.9 %copy-start.3 = (bf16[256,1280]{1,0:T(8,128)(2,1)S(1)}, bf16[256,1280]{1,0:T(8,128)(2,1)}, u32[]{:S(2)}) copy-start(bf16[256,1280]{1,0:T(8,128)(2,1)} %get-tuple-element.251) | copy-start | bytes 1966084
  16.3 20.7 %collective-permute-start.11 = (f32[32,1280]{1,0:T(8,128)S(1)}, f32[32,1280]{1,0:T(8,128)S(1)}, u32[]{:S(2)}, u32[]{:S(2)}) collective-permute-start(f32[32,1280]{1,0:T(8,128)S(1)} %pick.2.refs_0_), channel_id=1, source_target_pairs={{0,8},{4,12},{8,0},{12,4},{16,24},{20,28},{24,16},{28,20},{1,9},{5... | collective-permute-start | bytes 491528 | tf_op jit(solution)/shard_map/ppermute | solution.py:252
  18.0 20.6 %collective-permute-start.12 = (f32[32,1280]{1,0:T(8,128)S(1)}, f32[32,1280]{1,0:T(8,128)S(1)}, u32[]{:S(2)}, u32[]{:S(2)}) collective-permute-start(f32[32,1280]{1,0:T(8,128)S(1)} %pick.2.refs_0_), channel_id=1, source_target_pairs={{0,24},{4,28},{8,16},{12,20},{16,8},{20,12},{24,0},{28,4},{1,25},{... | collective-permute-start | bytes 491528 | tf_op jit(solution)/shard_map/ppermute | solution.py:252
  18.0 13.4 %collective-permute-start.17 = (f32[16,1280]{1,0:T(8,128)S(1)}, f32[16,1280]{1,0:T(8,128)S(1)}, u32[]{:S(2)}, u32[]{:S(2)}) collective-permute-start(f32[16,1280]{1,0:T(8,128)S(1)} %copy-done), channel_id=1, source_target_pairs={{0,16},{4,20},{8,24},{12,28},{16,0},{20,4},{24,8},{28,12},{1,17},{... | collective-permute-start | bytes 245768 | tf_op jit(solution)/shard_map/ppermute | solution.py:252
  23.4 9.6 %collective-permute-start.18 = (f32[16,1280]{1,0:T(8,128)S(1)}, f32[16,1280]{1,0:T(8,128)S(1)}, u32[]{:S(2)}, u32[]{:S(2)}) collective-permute-start(f32[16,1280]{1,0:T(8,128)S(1)} %copy-done), channel_id=1, source_target_pairs={{0,8},{4,12},{8,0},{12,4},{16,24},{20,28},{24,16},{28,20},{1,9},{5... | collective-permute-start | bytes 245768 | tf_op jit(solution)/shard_map/ppermute | solution.py:252
  31.4 11.3 %collective-permute-start.13 = (f32[32,1280]{1,0:T(8,128)S(1)}, f32[32,1280]{1,0:T(8,128)S(1)}, u32[]{:S(2)}, u32[]{:S(2)}) collective-permute-start(f32[32,1280]{1,0:T(8,128)S(1)} %pick.2.refs_0_), channel_id=1, source_target_pairs={{0,4},{4,0},{8,12},{12,8},{16,20},{20,16},{24,28},{28,24},{1,5},{5... | collective-permute-start | bytes 491528 | tf_op jit(solution)/shard_map/ppermute | solution.py:252
  33.0 8.1 %collective-permute-start.19 = (f32[16,1280]{1,0:T(8,128)S(1)}, f32[16,1280]{1,0:T(8,128)S(1)}, u32[]{:S(2)}, u32[]{:S(2)}) collective-permute-start(f32[16,1280]{1,0:T(8,128)S(1)} %copy-done), channel_id=1, source_target_pairs={{0,24},{4,28},{8,16},{12,20},{16,8},{20,12},{24,0},{28,4},{1,25},{... | collective-permute-start | bytes 245768 | tf_op jit(solution)/shard_map/ppermute | solution.py:252
  36.6 7.1 %collective-permute-start.14 = (f32[32,1280]{1,0:T(8,128)S(1)}, f32[32,1280]{1,0:T(8,128)S(1)}, u32[]{:S(2)}, u32[]{:S(2)}) collective-permute-start(f32[32,1280]{1,0:T(8,128)S(1)} %collective-permute-done.10.refs_1_), channel_id=1, source_target_pairs={{0,4},{4,0},{8,12},{12,8},{16,20},{20,16},{24,28},{28,24},{1,5},{5... | collective-permute-start | bytes 491528 | tf_op jit(solution)/shard_map/ppermute | solution.py:252
  37.0 10.2 %collective-permute-start.15 = (f32[32,1280]{1,0:T(8,128)S(1)}, f32[32,1280]{1,0:T(8,128)S(1)}, u32[]{:S(2)}, u32[]{:S(2)}) collective-permute-start(f32[32,1280]{1,0:T(8,128)S(1)} %collective-permute-done.11.refs_2_), channel_id=1, source_target_pairs={{0,4},{4,0},{8,12},{12,8},{16,20},{20,16},{24,28},{28,24},{1,5},{5... | collective-permute-start | bytes 491528 | tf_op jit(solution)/shard_map/ppermute | solution.py:252
  38.6 12.1 %collective-permute-start.16 = (f32[32,1280]{1,0:T(8,128)S(1)}, f32[32,1280]{1,0:T(8,128)S(1)}, u32[]{:S(2)}, u32[]{:S(2)}) collective-permute-start(f32[32,1280]{1,0:T(8,128)S(1)} %collective-permute-done.12.refs_3_), channel_id=1, source_target_pairs={{0,4},{4,0},{8,12},{12,8},{16,20},{20,16},{24,28},{28,24},{1,5},{5... | collective-permute-start | bytes 491528 | tf_op jit(solution)/shard_map/ppermute | solution.py:252
  41.1 18.7 %collective-permute-start.20 = (f32[16,1280]{1,0:T(8,128)S(1)}, f32[16,1280]{1,0:T(8,128)S(1)}, u32[]{:S(2)}, u32[]{:S(2)}) collective-permute-start(f32[16,1280]{1,0:T(8,128)S(1)} %copy-done), channel_id=1, source_target_pairs={{0,4},{4,0},{8,12},{12,8},{16,20},{20,16},{24,28},{28,24},{1,5},{5... | collective-permute-start | bytes 245768 | tf_op jit(solution)/shard_map/ppermute | solution.py:252
  42.7 17.2 %collective-permute-start.21 = (f32[16,1280]{1,0:T(8,128)S(1)}, f32[16,1280]{1,0:T(8,128)S(1)}, u32[]{:S(2)}, u32[]{:S(2)}) collective-permute-start(f32[16,1280]{1,0:T(8,128)S(1)} %collective-permute-done.17.refs_1_), channel_id=1, source_target_pairs={{0,4},{4,0},{8,12},{12,8},{16,20},{20,16},{24,28},{28,24},{1,5},{5... | collective-permute-start | bytes 245768 | tf_op jit(solution)/shard_map/ppermute | solution.py:252
  43.7 16.2 %collective-permute-start.22 = (f32[16,1280]{1,0:T(8,128)S(1)}, f32[16,1280]{1,0:T(8,128)S(1)}, u32[]{:S(2)}, u32[]{:S(2)}) collective-permute-start(f32[16,1280]{1,0:T(8,128)S(1)} %collective-permute-done.18.refs_2_), channel_id=1, source_target_pairs={{0,4},{4,0},{8,12},{12,8},{16,20},{20,16},{24,28},{28,24},{1,5},{5... | collective-permute-start | bytes 245768 | tf_op jit(solution)/shard_map/ppermute | solution.py:252
  47.2 12.7 %collective-permute-start.23 = (f32[16,1280]{1,0:T(8,128)S(1)}, f32[16,1280]{1,0:T(8,128)S(1)}, u32[]{:S(2)}, u32[]{:S(2)}) collective-permute-start(f32[16,1280]{1,0:T(8,128)S(1)} %collective-permute-done.19.refs_3_), channel_id=1, source_target_pairs={{0,4},{4,0},{8,12},{12,8},{16,20},{20,16},{24,28},{28,24},{1,5},{5... | collective-permute-start | bytes 245768 | tf_op jit(solution)/shard_map/ppermute | solution.py:252

commit v2 on v1

v2 whole, which is shorter than its diff:
```python
import functools
import math

import jax
import jax.numpy as jnp
from jax import lax
from jax.experimental import pallas as pl
from jax.experimental.pallas import tpu as pltpu
from jax.sharding import PartitionSpec as P

LEVELS = 4
XCOL_DEV = 4
SUB = 8
VMEM_LIMIT = 48 * 1024 * 1024
COST = pl.CostEstimate(flops=1, bytes_accessed=1, transcendentals=0)
F32 = jnp.float32
BF16 = jnp.bfloat16
LANES_BOTH = (((1,), (1,)), ((), ()))
ROWS_BOTH = (((0,), (0,)), ((), ()))
PLAIN = (((1,), (0,)), ((), ()))


def dot(a, b, dims):
    return lax.dot_general(a, b, dims, preferred_element_type=F32)


def split(x, parts):
    pieces = []
    for _ in range(parts - 1):
        piece = x.astype(BF16)
        pieces.append(piece)
        x = x - piece.astype(F32)
    pieces.append(x.astype(BF16))
    return pieces


def level_onehot(level_row):
    levels = lax.broadcasted_iota(jnp.int32, (SUB, level_row.shape[1]), 0)
    return (level_row == levels).astype(F32)


def by_level(level_row, columns):
    picked = jnp.where(level_row == 1, columns[1], columns[0])
    for level in range(2, LEVELS):
        picked = jnp.where(level_row == level, columns[level], picked)
    return picked


def pick_kernel(obs_ref, skip_ref, state_ref, out_ref, list_ref):
    rows = state_ref.shape[0]
    slots = out_ref.shape[0]
    row_first = lax.axis_index("rows") * rows
    skip = skip_ref[0]

    def visit(j, rank):
        row = obs_ref[j] - row_first
        list_ref[rank] = row
        return rank + ((row >= 0) & (row < rows)).astype(jnp.int32)

    total = lax.fori_loop(0, obs_ref.shape[0], visit, 0, unroll=8)
    held = jnp.clip(total - skip, 0, slots)

    def bring(slot, carry):
        out_ref[pl.ds(slot, 1), :] = state_ref[pl.ds(list_ref[skip + slot], 1), :]
        return carry

    def clear(slot, carry):
        out_ref[pl.ds(slot, 1), :] = jnp.zeros((1, out_ref.shape[1]), F32)
        return carry

    lax.fori_loop(0, held, bring, 0)
    lax.fori_loop(held, slots, clear, 0)


def pick(obs_row, skip, state, slots):
    smem = pl.BlockSpec(memory_space=pltpu.SMEM)
    vmem = pl.BlockSpec(memory_space=pltpu.VMEM)
    return pl.pallas_call(
        pick_kernel,
        out_shape=jax.ShapeDtypeStruct((slots, state.shape[1]), F32),
        in_specs=[smem, smem, vmem],
        out_specs=vmem,
        scratch_shapes=[pltpu.SMEM((obs_row.shape[0] + 1,), jnp.int32)],
        compiler_params=pltpu.CompilerParams(vmem_limit_bytes=VMEM_LIMIT),
        cost_estimate=COST,
        name="pick",
    )(obs_row, skip, state)


def center_kernel(level_ref, state_ref, sums_ref, high_ref, low_ref):
    level_row = level_ref[...]
    onehot = level_onehot(level_row)
    counts = jnp.sum(onehot, axis=1, keepdims=True)
    state = state_ref[...]
    hot = onehot.astype(BF16)
    sums = sum(dot(hot, piece, LANES_BOTH) for piece in split(state, 3))
    sums_ref[0:LEVELS, :] = sums[0:LEVELS, :]
    sums_ref[LEVELS:SUB, :] = jnp.broadcast_to(counts[0:LEVELS, :], (LEVELS, sums.shape[1]))
    means = jnp.transpose(sums / jnp.maximum(counts, 1.0))
    columns = [means[:, level : level + 1] for level in range(LEVELS)]
    high, low = split(state - by_level(level_row, columns), 2)
    high_ref[...] = high
    low_ref[...] = low


def center(level_row, state):
    rows, members = state.shape
    tall = math.gcd(rows, 128)
    return pl.pallas_call(
        center_kernel,
        out_shape=(
            jax.ShapeDtypeStruct((SUB, rows), F32),
            jax.ShapeDtypeStruct((rows, members), BF16),
            jax.ShapeDtypeStruct((rows, members), BF16),
        ),
        grid=(rows // tall,),
        in_specs=[
            pl.BlockSpec((1, members), lambda i: (0, 0)),
            pl.BlockSpec((tall, members), lambda i: (i, 0)),
        ],
        out_specs=(
            pl.BlockSpec((SUB, tall), lambda i: (0, i)),
            pl.BlockSpec((tall, members), lambda i: (i, 0)),
            pl.BlockSpec((tall, members), lambda i: (i, 0)),
        ),
        compiler_params=pltpu.CompilerParams(vmem_limit_bytes=VMEM_LIMIT),
        cost_estimate=COST,
        name="center",
    )(level_row, state)


def place_kernel(slots, rows, obs_ref, near_ref, far_ref, place_ref, rounds_ref, pair_ref):
    observed = obs_ref.shape[1]
    length = near_ref.shape[0]
    pair_ref[0:length, :] = near_ref[...]
    pair_ref[length : 2 * length, :] = far_ref[...]
    owner = lax.div(obs_ref[...], jnp.int32(rows))
    owner_row = owner.astype(F32)
    owner_down = jnp.transpose(jnp.broadcast_to(owner_row, (SUB, observed)))[:, 0:1]
    j_down = lax.broadcasted_iota(jnp.int32, (observed, observed), 0)
    j_row = lax.broadcasted_iota(jnp.int32, (observed, observed), 1)
    earlier = (owner_down == owner_row) & (j_down < j_row)
    rank = jnp.sum(earlier.astype(F32), axis=0, keepdims=True).astype(jnp.int32)
    place_ref[0:1, :] = owner
    place_ref[1:2, :] = rank
    place_ref[2:SUB, :] = jnp.zeros((SUB - 2, observed), jnp.int32)
    rounds_ref[0] = lax.div(jnp.max(rank), jnp.int32(slots)) + 1


def places(obs_row, near, far, rows, slots):
    observed = obs_row.shape[0]
    length, members = near.shape
    vmem = pl.BlockSpec(memory_space=pltpu.VMEM)
    smem = pl.BlockSpec(memory_space=pltpu.SMEM)
    return pl.pallas_call(
        functools.partial(place_kernel, slots, rows),
        out_shape=(
            jax.ShapeDtypeStruct((SUB, observed), jnp.int32),
            jax.ShapeDtypeStruct((1,), jnp.int32),
            jax.ShapeDtypeStruct((2 * length, members), F32),
        ),
        in_specs=[vmem] * 3,
        out_specs=(vmem, smem, vmem),
        compiler_params=pltpu.CompilerParams(vmem_limit_bytes=VMEM_LIMIT),
        name="places",
    )(obs_row[None, :], near, far)


def taper_kernel(radius, obs_ref, coords_ref, taper_ref):
    rows, observed = taper_ref.shape
    total = coords_ref.shape[1]
    chunk = math.gcd(total, 256)
    obs = obs_ref[...]

    def look(n, seen):
        at = pl.multiple_of(n * chunk, chunk)
        row = lax.broadcasted_iota(jnp.int32, (chunk, observed), 0) + at
        coords = coords_ref[:, pl.ds(at, chunk)].astype(F32).astype(BF16)
        return seen + dot(coords, (row == obs).astype(BF16), PLAIN)

    seen = lax.fori_loop(0, total // chunk, look, jnp.zeros((2, observed), F32), unroll=min(8, total // chunk))
    first = pl.multiple_of(lax.axis_index("rows") * rows, rows)
    own = coords_ref[:, pl.ds(first, rows)].astype(F32)
    own_x = jnp.transpose(jnp.broadcast_to(own[0:1, :], (SUB, rows)))[:, 0:1]
    own_y = jnp.transpose(jnp.broadcast_to(own[1:2, :], (SUB, rows)))[:, 0:1]
    offset_x = own_x - seen[0:1, :]
    offset_y = own_y - seen[1:2, :]
    distance = offset_x * offset_x + offset_y * offset_y
    reach = jnp.maximum(0.0, 1.0 - distance / float(radius * radius))
    taper_ref[...] = reach * reach


def tapers(obs_row, state_coords, rows, radius):
    vmem = pl.BlockSpec(memory_space=pltpu.VMEM)
    return pl.pallas_call(
        functools.partial(taper_kernel, radius),
        out_shape=jax.ShapeDtypeStruct((rows, obs_row.shape[0]), F32),
        in_specs=[vmem, vmem],
        out_specs=vmem,
        compiler_params=pltpu.CompilerParams(vmem_limit_bytes=VMEM_LIMIT),
        name="tapers",
    )(obs_row[None, :], state_coords)


def cross_kernel(number, slots, weight_ref, skip_ref, level_ref, place_ref, high_ref, low_ref, before_ref, *refs):
    blocks, (sums_ref, out_ref, o_high, o_low, p_ref, m_ref) = refs[: len(number)], refs[len(number) :]
    rows = high_ref.shape[0]
    me = lax.axis_index("rows")
    skip = skip_ref[0]
    level_row = level_ref[...]
    onehot = level_onehot(level_row)
    counts = jnp.maximum(jnp.sum(onehot, axis=1, keepdims=True), 1.0)
    total = sum(
        sums_ref[at + LEVELS : at + SUB, 0:128] for at in range(0, sums_ref.shape[0], SUB)
    )
    scales = [weight_ref[level] / (total[level, 0] - 1.0) for level in range(LEVELS)]
    member_scale = by_level(level_row, scales)
    owner, rank = place_ref[0:1, :], place_ref[1:2, :]
    padded = o_high.shape[0] // len(number)
    m_ref[...] = jnp.zeros_like(m_ref)
    for n, block_ref in enumerate(blocks):
        at = n * padded
        block = block_ref[...]
        columns = []
        for level in range(LEVELS):
            member = jnp.where(level_row == level, block, 0.0)
            columns.append(jnp.sum(member, axis=1, keepdims=True) / counts[level : level + 1, :])
            m_ref[at : at + slots, level : level + 1] = columns[level]
        high, low = split((block - by_level(level_row, columns)) * member_scale, 2)
        o_high[at : at + slots, :] = high
        o_low[at : at + slots, :] = low
        slot = lax.broadcasted_iota(jnp.int32, (slots, owner.shape[1]), 0)
        hit = (owner == (me ^ number[n])) & (rank - skip == slot)
        p_ref[at : at + slots, :] = hit.astype(BF16)
    by_slot = dot(high_ref[...], o_high[...], LANES_BOTH)
    by_slot += dot(high_ref[...], o_low[...], LANES_BOTH)
    by_slot += dot(low_ref[...], o_high[...], LANES_BOTH)
    place = p_ref[...]
    cross = sum(dot(piece, place, PLAIN) for piece in split(by_slot, 3))
    out_ref[0:rows, :] = before_ref[0:rows, :] + cross
    means = sum(dot(piece, place, ROWS_BOTH) for piece in split(m_ref[...], 3))
    out_ref[rows : rows + SUB, :] = before_ref[rows : rows + SUB, :] + means


def cross_part(level_weight, skip, level_row, place, high, low, before, blocks, sums, number):
    rows, members = high.shape
    slots = blocks[0].shape[0]
    smem = pl.BlockSpec(memory_space=pltpu.SMEM)
    vmem = pl.BlockSpec(memory_space=pltpu.VMEM)
    held = len(number) * slots
    return pl.pallas_call(
        functools.partial(cross_kernel, number, slots),
        out_shape=jax.ShapeDtypeStruct(before.shape, F32),
        in_specs=[smem, smem] + [vmem] * (6 + len(blocks)),
        out_specs=vmem,
        scratch_shapes=[
            pltpu.VMEM((held, members), BF16),
            pltpu.VMEM((held, members), BF16),
            pltpu.VMEM((held, before.shape[1]), BF16),
            pltpu.VMEM((held, SUB), F32),
        ],
        compiler_params=pltpu.CompilerParams(vmem_limit_bytes=VMEM_LIMIT),
        cost_estimate=COST,
        name="cross_part",
    )(level_weight, skip, level_row, place, high, low, before, *blocks, sums)


def final_kernel(number, mem, width, weight_ref, taper_ref, sums_ref, *refs):
    parts, refs = refs[:mem], refs[mem:]
    blocks, (out_ref, w_high, w_low, chunk, sem) = refs[: len(number)], refs[len(number) :]
    rows = taper_ref.shape[0]
    members = out_ref.shape[1]
    me = lax.axis_index("rows")

    for n, block_ref in enumerate(blocks):
        length = block_ref.shape[0] // 2
        for side in range(2):
            at = pl.multiple_of((me ^ number[n] ^ side) * length, length)
            high, low = split(block_ref[side * length : (side + 1) * length, :], 2)
            w_high[pl.ds(at, length), :] = high
            w_low[pl.ds(at, length), :] = low

    cross = sum(ref[0:rows, :] for ref in parts)
    places = range(0, mem * SUB, SUB)
    counts = [sums_ref[at + LEVELS : at + SUB, :] for at in places]
    sums = [sums_ref[at : at + LEVELS, :] for at in places]
    total = sum(counts)
    mean = sum(sums) / total
    level = lax.broadcasted_iota(jnp.int32, (LEVELS, 1), 0)
    scale = by_level(level, [weight_ref[k] for k in range(LEVELS)]) / (total - 1.0)
    seen = [ref[rows : rows + LEVELS, :] for ref in parts]
    seen_counts = [c[:, 0:1] for c in counts]
    seen_mean = sum(c * s for c, s in zip(seen_counts, seen)) / total[:, 0:1]
    left, right = [], []
    for d in range(mem):
        left.append(scale * (sums[d] - counts[d] * mean))
        right.append(jnp.where(seen_counts[d] > 0.0, seen[d] - seen_mean, 0.0))
    left = split(jnp.concatenate(left, axis=0), 2)
    right = split(jnp.concatenate(right, axis=0), 2)
    cross += dot(left[0], right[0], ROWS_BOTH)
    cross += dot(left[0], right[1], ROWS_BOTH)
    cross += dot(left[1], right[0], ROWS_BOTH)
    t_high, t_low = split(cross * taper_ref[...], 2)

    copies = []
    for n in range(members // width):
        at = n * width
        out = dot(t_high, w_high[:, at : at + width], PLAIN)
        out += dot(t_high, w_low[:, at : at + width], PLAIN)
        out += dot(t_low, w_high[:, at : at + width], PLAIN)
        chunk[n, :, :] = out
        copies.append(pltpu.make_async_copy(chunk.at[n], out_ref.at[:, pl.ds(at, width)], sem.at[n]))
        copies[-1].start()
    for copy in copies:
        copy.wait()


def final(level_weight, parts, sums, taper, blocks, number):
    rows, observed = taper.shape
    members = blocks[0].shape[1]
    width = math.gcd(members, 256)
    smem = pl.BlockSpec(memory_space=pltpu.SMEM)
    vmem = pl.BlockSpec(memory_space=pltpu.VMEM)
    return pl.pallas_call(
        functools.partial(final_kernel, number, len(parts), width),
        out_shape=jax.ShapeDtypeStruct((rows, members), F32),
        in_specs=[smem] + [vmem] * (2 + len(parts) + len(blocks)),
        out_specs=pl.BlockSpec(memory_space=pl.ANY),
        scratch_shapes=[
            pltpu.VMEM((observed, members), BF16),
            pltpu.VMEM((observed, members), BF16),
            pltpu.VMEM((members // width, rows, width), F32),
            pltpu.SemaphoreType.DMA((members // width,)),
        ],
        compiler_params=pltpu.CompilerParams(vmem_limit_bytes=VMEM_LIMIT),
        cost_estimate=COST,
        name="final",
    )(level_weight, taper, sums, *parts, *blocks)


def across(x, axis, bits):
    count = lax.axis_size(axis)
    return lax.ppermute(x, axis, [(i, i ^ bits) for i in range(count)])


def gather_line(x, bits):
    blocks = {0: x}
    for bit in bits:
        for distance in list(blocks):
            blocks[distance ^ bit] = across(blocks[distance], "rows", bit)
    return blocks


def after(x, *others):
    return lax.optimization_barrier((x, *others))[0]


def on_device(state, member_level, level_weight, obs_row, state_coords, weights):
    groups = lax.axis_size("rows")
    radius = XCOL_DEV * groups
    row_count = state.shape[0]
    observed = obs_row.shape[0]
    bits = [1 << n for n in range(groups.bit_length() - 2, 0, -1)]
    slots = min(observed, 16 * (-(-2 * observed // groups) // 16))

    none = jnp.zeros((1,), jnp.int32)
    own = pick(obs_row, none, state, slots)
    level_row = after(member_level, own)[None, :]
    sums, high, low = center(level_row, after(state, own))
    all_sums = sums
    for n in range(lax.axis_size("mem").bit_length() - 1):
        all_sums = jnp.concatenate([all_sums, across(all_sums, "mem", 1 << n)])
        if n == 0:
            first_sums = all_sums

    line = gather_line(own, bits)
    other = {b ^ 1: across(after(x, first_sums) if b == 2 else x, "rows", 1) for b, x in line.items()}
    blocks = line | other
    early = [b for b in blocks if b < bits[0]]
    late = [b for b in blocks if b >= bits[0]]

    weights_far = across(after(weights, other[1]), "rows", 1)
    place, rounds, weights_pair = places(
        after(obs_row, other[early[-1]], all_sums), weights, weights_far, row_count, slots
    )

    def cross(skip, part, high, low, held, number):
        return cross_part(level_weight, skip, level_row, place, high, low, part, held, all_sums, number)

    def more(carry):
        return carry[0] < rounds[0]

    def another(carry):
        turn, part = carry
        skip = (turn * slots)[None]
        again = after(state, turn)
        block = pick(obs_row, skip, again, slots)
        _, high, low = center(level_row, again)
        parcels = [lax.all_gather(x, "rows", axis=0) for x in jnp.split(block, slots // 16)]
        every = jnp.concatenate(parcels, axis=1)
        me = lax.axis_index("rows")
        part = cross(skip, part, high, low, [every[me ^ b] for b in early + late], early + late)
        return turn + 1, part

    empty = jnp.zeros((row_count + SUB, observed), F32)
    _, part = lax.while_loop(more, another, (jnp.int32(1), after(empty, other[bits[0] ^ 1])))
    half = cross(none, part, high, low, [blocks[b] for b in early], early)
    part = cross(none, half, high, low, [blocks[b] for b in late], late)
    parts = [part] + [across(part, "mem", b) for b in range(1, lax.axis_size("mem"))]

    far_pair = across(weights_pair, "rows", bits[0])
    weights_line = gather_line(after(weights_pair, half), bits[1:])
    weights_line |= {b ^ bits[0]: x for b, x in gather_line(after(far_pair, part), bits[1:]).items()}
    taper = tapers(after(obs_row, part), state_coords, row_count, radius)
    return final(level_weight, parts, all_sums, taper, list(weights_line.values()), list(weights_line))


def solution(mesh):
    in_specs = (P("rows", "mem"), P("mem"), P(), P(), P(), P("rows", "mem"))
    out_specs = P("rows", "mem")
    return jax.shard_map(
        on_device, mesh=mesh, in_specs=in_specs, out_specs=out_specs, check_vma=False
    )
```

time: 64 us -> 48.6 us (0.76)
  blocking collectives: 7.25 us -> 0 us
  between operations: 2.8 us -> 0.1 us
  starting transfers between devices: 23.3 us -> 20.8 us
  local copies, waits for them, and re-layouts: 4.32 us -> 2.26 us
  Pallas kernels: 13.6 us -> 11.7 us
  waiting for transfers between devices: 11.4 us -> 12.9 us
  other arithmetic: 1.06 us -> 0 us
  loops' own time: 0.01 us -> 0.69 us
    all_gather x1 -> x0, blocking collectives: 7.25 us -> none  [on_device(): parts = lax.all_gather(part, 'mem', axis=0)]
    ppermute x17 -> x16, starting transfers between devices: 23.3 us -> 20.8 us  [across(): return lax.ppermute(x, axis, [(i, i ^ bits) for i in range(count)])]
    pallas_call x1, Pallas kernels: 3.58 us -> 1.49 us  [center(): pl.pallas_call(center_kernel, out_shape=(jax.ShapeDtypeStruct((SUB, rows)...]
    gather x1 -> x0, local copies, waits for them, and re-layouts: 1.87 us -> none  [taper_rows(): observed_xy = jnp.take(state_coords, obs_row, axis=1)]
    ppermute x17 -> x16, waiting for transfers between devices: 11.4 us -> 12.9 us  [across(): return lax.ppermute(x, axis, [(i, i ^ bits) for i in range(count)])]
    pallas_call x2, Pallas kernels: 3.76 us -> 4.6 us  [cross_part(): pl.pallas_call(functools.partial(cross_kernel, number, slots), out_shape=...]
    broadcast_in_dim x1, local copies, waits for them, and re-layouts: 0.8 us -> 0.01 us  [on_device(): level_row = after(member_level, own)[None, :]]
    another operation x1, loops' own time: 0.01 us -> 0.69 us  [on_device(): lax.while_loop(more, another, (jnp.int32(1), after(empty, other[bits[0] ^...]
  transfers between devices with their start and end apart: 17 -> 16, of which waited for: 4 -> 8; matrix products, arithmetic and copies ran while one was open for 7% -> 1% of each run, Pallas kernels for 10% -> 15%
where the time goes in v2:
time: 48.6 us; the launch traced here: 48.4 us
  starting transfers between devices  20.8 us (43%)
  waiting for transfers between devices  12.9 us (27%)
  Pallas kernels  11.7 us (24%)
  local copies, waits for them, and re-layouts  2.26 us (5%)
  loops' own time  0.69 us (1%)
    ppermute x16, starting transfers between devices, across(): return lax.ppermute(x, axis, [(i, i ^ bits) for i in range(count)])  20.8 us
    ppermute x16, waiting for transfers between devices, across(): return lax.ppermute(x, axis, [(i, i ^ bits) for i in range(count)])  12.9 us
    pallas_call x2, Pallas kernels, cross_part(): pl.pallas_call(functools.partial(cross_kernel, number, slots), out_shape=...  4.6 us
    pallas_call x1, Pallas kernels, final(): pl.pallas_call(functools.partial(final_kernel, number, len(parts), width)...  2.3 us
    pallas_call x1, Pallas kernels, pick(): pl.pallas_call(pick_kernel, out_shape=jax.ShapeDtypeStruct((slots, state....  2.12 us
    unnamed x18, local copies, waits for them, and re-layouts  1.6 us
    pallas_call x1, Pallas kernels, center(): pl.pallas_call(center_kernel, out_shape=(jax.ShapeDtypeStruct((SUB, rows)...  1.49 us
  transfers between devices with their start and end apart: 16, of which 8 were waited for; matrix products, arithmetic and copies ran while one was open for 1% of the time, Pallas kernels for 15%

profile of v2, /device:TPU:0, one launch (start us, length us, event | category | flops | bytes accessed | tf_op | source)
XLA Modules:
  0.0 48.4 jit_solution(1837117921699127514)
XLA Ops:
  0.0 2.1 %pick.2.refs_0_ = f32[32,1280]{1,0:T(8,128)S(1)} custom-call(s32[128]{0:T(128)} %obs_ref.1, s32[1]{0:T(128)} %constant.14.clone.1.skip_ref, f32[256,1280]{1,0:T(8,128)} %state_ref.2), custom_call_target="tpu_custom_call" | custom-call | flops 1 | bytes 1 | tf_op jit(solution)/shard_map/pick/pallas_call | solution.py:78
  2.1 3.1 %collective-permute-start = (f32[32,1280]{1,0:T(8,128)S(1)}, f32[32,1280]{1,0:T(8,128)S(1)}, u32[]{:S(2)}, u32[]{:S(2)}) collective-permute-start(f32[32,1280]{1,0:T(8,128)S(1)} %pick.2.refs_0_), channel_id=1, source_target_pairs={{0,8},{4,12},{8,0},{12,4},{16,24},{20,28},{24,16},{28,20},{1,9},{5... | collective-permute-start | bytes 491528 | tf_op jit(solution)/shard_map/ppermute | solution.py:343
  5.2 1.5 %collective-permute-start.4 = (f32[32,1280]{1,0:T(8,128)S(1)}, f32[32,1280]{1,0:T(8,128)S(1)}, u32[]{:S(2)}, u32[]{:S(2)}) collective-permute-start(f32[32,1280]{1,0:T(8,128)S(1)} %pick.2.refs_0_), channel_id=1, source_target_pairs={{0,4},{4,0},{8,12},{12,8},{16,20},{20,16},{24,28},{28,24},{1,5},{5... | collective-permute-start | bytes 491528 | tf_op jit(solution)/shard_map/ppermute | solution.py:343
  6.8 2.6 %collective-permute-start.6 = (f32[32,1280]{1,0:T(8,128)S(1)}, f32[32,1280]{1,0:T(8,128)S(1)}, u32[]{:S(2)}, u32[]{:S(2)}) collective-permute-start(f32[32,1280]{1,0:T(8,128)S(1)} %pick.2.refs_0_), channel_id=1, source_target_pairs={{0,16},{4,20},{8,24},{12,28},{16,0},{20,4},{24,8},{28,12},{1,17},{... | collective-permute-start | bytes 491528 | tf_op jit(solution)/shard_map/ppermute | solution.py:343
  9.4 1.5 %center.2 = (f32[8,256]{1,0:T(8,128)S(1)}, bf16[256,1280]{1,0:T(8,128)(2,1)S(1)}, bf16[256,1280]{1,0:T(8,128)(2,1)S(1)}) custom-call(s32[1,1280]{1,0:T(1,128)S(1)} %broadcast_in_dim.15.level_ref, f32[256,1280]{1,0:T(8,128)S(1)} %copy-done.4), custom_call_target="tpu_custom_call" | custom-call | flops 1 | bytes 1 | tf_op jit(solution)/shard_map/center/pallas_call | solution.py:109
  10.9 1.1 %collective-permute-done.1 = f32[8,256]{1,0:T(8,128)S(1)} collective-permute-done((f32[8,256]{1,0:T(8,128)S(1)}, f32[8,256]{1,0:T(8,128)S(1)}, u32[]{:S(2)}, u32[]{:S(2)}) %collective-permute-start.1) | collective-permute-done | bytes 8224 | tf_op jit(solution)/shard_map/ppermute | solution.py:343
  12.1 2.0 %collective-permute-start.2 = (f32[32,1280]{1,0:T(8,128)S(1)}, f32[32,1280]{1,0:T(8,128)S(1)}, u32[]{:S(2)}, u32[]{:S(2)}) collective-permute-start(f32[32,1280]{1,0:T(8,128)S(1)} %collective-permute-done.refs_1_), channel_id=1, source_target_pairs={{0,4},{4,0},{8,12},{12,8},{16,20},{20,16},{24,28},{28,24},{1,5},{5... | collective-permute-start | bytes 491528 | tf_op jit(solution)/shard_map/ppermute | solution.py:343
  14.1 2.5 %collective-permute-done.6.refs_0_ = f32[32,1280]{1,0:T(8,128)S(1)} collective-permute-done((f32[32,1280]{1,0:T(8,128)S(1)}, f32[32,1280]{1,0:T(8,128)S(1)}, u32[]{:S(2)}, u32[]{:S(2)}) %collective-permute-start.6) | collective-permute-done | bytes 163872 | tf_op jit(solution)/shard_map/ppermute | solution.py:343
  16.5 0.6 %collective-permute-start.7 = (f32[32,1280]{1,0:T(8,128)S(1)}, f32[32,1280]{1,0:T(8,128)S(1)}, u32[]{:S(2)}, u32[]{:S(2)}) collective-permute-start(f32[32,1280]{1,0:T(8,128)S(1)} %collective-permute-done.6.refs_0_), channel_id=1, source_target_pairs={{0,4},{4,0},{8,12},{12,8},{16,20},{20,16},{24,28},{28,24},{1,5},{5... | collective-permute-start | bytes 491528 | tf_op jit(solution)/shard_map/ppermute | solution.py:343
  17.3 1.5 %collective-permute-start.3 = (f32[16,256]{1,0:T(8,128)S(1)}, f32[16,256]{1,0:T(8,128)S(1)}, u32[]{:S(2)}, u32[]{:S(2)}) collective-permute-start(f32[16,256]{1,0:T(8,128)S(1)} %get-tuple-element.116), channel_id=1, source_target_pairs={{0,2},{1,3},{2,0},{3,1},{4,6},{5,7},{6,4},{7,5},{8,10},{9,11},{10,... | collective-permute-start | bytes 49160 | tf_op jit(solution)/shard_map/ppermute | solution.py:343
  18.8 1.2 %collective-permute-start.5 = (f32[16,1280]{1,0:T(8,128)S(1)}, f32[16,1280]{1,0:T(8,128)S(1)}, u32[]{:S(2)}, u32[]{:S(2)}) collective-permute-start(f32[16,1280]{1,0:T(8,128)S(1)} %copy-done.2), channel_id=1, source_target_pairs={{0,4},{4,0},{8,12},{12,8},{16,20},{20,16},{24,28},{28,24},{1,5},{5... | collective-permute-start | bytes 245768 | tf_op jit(solution)/shard_map/ppermute | solution.py:343
  20.1 1.0 %collective-permute-done.3 = f32[16,256]{1,0:T(8,128)S(1)} collective-permute-done((f32[16,256]{1,0:T(8,128)S(1)}, f32[16,256]{1,0:T(8,128)S(1)}, u32[]{:S(2)}, u32[]{:S(2)}) %collective-permute-start.3) | collective-permute-done | bytes 16416 | tf_op jit(solution)/shard_map/ppermute | solution.py:343
  21.1 0.7 %copy-done = f32[32,1280]{1,0:T(8,128)} copy-done((f32[32,1280]{1,0:T(8,128)}, f32[32,1280]{1,0:T(8,128)S(1)}, u32[]{:S(2)}) %copy-start) | copy-done | bytes 163864
  21.8 1.0 %collective-permute-done.7.refs_2_ = f32[32,1280]{1,0:T(8,128)S(1)} collective-permute-done((f32[32,1280]{1,0:T(8,128)S(1)}, f32[32,1280]{1,0:T(8,128)S(1)}, u32[]{:S(2)}, u32[]{:S(2)}) %collective-permute-start.7) | collective-permute-done | bytes 163872 | tf_op jit(solution)/shard_map/ppermute | solution.py:343
  22.8 0.9 %collective-permute-done.5.far_ref = f32[16,1280]{1,0:T(8,128)S(1)} collective-permute-done((f32[16,1280]{1,0:T(8,128)S(1)}, f32[16,1280]{1,0:T(8,128)S(1)}, u32[]{:S(2)}, u32[]{:S(2)}) %collective-permute-start.5) | collective-permute-done | bytes 81952 | tf_op jit(solution)/shard_map/ppermute | solution.py:343
  23.6 0.9 %places.1 = (s32[8,128]{1,0:T(8,128)S(1)}, s32[1]{0:T(128)}, f32[32,1280]{1,0:T(8,128)S(1)}) custom-call(s32[1,128]{1,0:T(1,128)S(1)} %bitcast.37, f32[16,1280]{1,0:T(8,128)S(1)} %copy-done.2, f32[16,1280]{1,0:T(8,128)S(1)} %collective-permute-done.5.far_ref), custom_call_target="tpu_custom_call" | custom-call | tf_op jit(solution)/shard_map/places/pallas_call | solution.py:155
  24.5 2.5 %collective-permute-start.14 = (f32[32,1280]{1,0:T(8,128)S(1)}, f32[32,1280]{1,0:T(8,128)S(1)}, u32[]{:S(2)}, u32[]{:S(2)}) collective-permute-start(f32[32,1280]{1,0:T(8,128)S(1)} %get-tuple-element.85.refs_4_), channel_id=1, source_target_pairs={{0,16},{4,20},{8,24},{12,28},{16,0},{20,4},{24,8},{28,12},{1,17},{... | collective-permute-start | bytes 491528 | tf_op jit(solution)/shard_map/ppermute | solution.py:343
  27.1 1.5 %collective-permute-start.9 = (f32[32,1280]{1,0:T(8,128)}, f32[32,1280]{1,0:T(8,128)}, u32[]{:S(2)}, u32[]{:S(2)}) collective-permute-start(f32[32,1280]{1,0:T(8,128)} %collective-permute-done.8.refs_1_), channel_id=1, source_target_pairs={{0,4},{4,0},{8,12},{12,8},{16,20},{20,16},{24,28},{28,24},{1,5},{5... | collective-permute-start | bytes 491528 | tf_op jit(solution)/shard_map/ppermute | solution.py:343
  28.6 0.7 %broadcast_in_dim.17 = f32[264,128]{1,0:T(8,128)} broadcast(f32[]{:T(128)} %constant.31.clone.1), dimensions={} | broadcast | bytes 135172 | tf_op jit(solution)/shard_map/broadcast_in_dim | solution.py:405
  29.2 0.7 %while.10 = (s32[]{:T(128)}, f32[264,128]{1,0:T(8,128)}, s32[1]{0:T(128)}, f32[256,1280]{1,0:T(8,128)}, s32[1,1280]{1,0:T(1,128)S(1)}, /*index=5*/s32[128]{0:T(1...) while((s32[]{:T(128)}, f32[264,128]{1,0:T(8,128)}, ...), condition=%wide.region_1.0_spmd, body=%wide.region_0.0_spmd.sunk | while | flops 327720 | bytes 17031904 | solution.py:406
  29.9 0.9 %copy-done.1 = f32[32,1280]{1,0:T(8,128)S(1)} copy-done((f32[32,1280]{1,0:T(8,128)S(1)}, f32[32,1280]{1,0:T(8,128)}, u32[]{:S(2)}) %copy-start.1) | copy-done | bytes 163864
  30.9 2.3 %cross_part.3.before_ref = f32[264,128]{1,0:T(8,128)S(1)} custom-call(f32[4]{0:T(128)S(1)} %get-tuple-element.294, s32[1]{0:T(128)} %constant.14.clone.1.skip_ref, s32[1,1280]{1,0:T(1,128)S(1)} %get-tuple-element.291, s32[8,128]{1,0:T(8,128)S(1)} %get-tuple-element.292, bf16[256,1280]{1,0:T(8,128)(2,1)S(1)} %get-tuple-element.78.high_ref, ...), custom_call_target="tpu_custom_call" | custom-call | flops 1 | bytes 1 | tf_op jit(solution)/shard_map/cross_part/pallas_call | solution.py:251
  33.1 0.4 collective-permute-start.13
  33.5 2.3 %cross_part.4.refs_0_ = f32[264,128]{1,0:T(8,128)S(1)} custom-call(f32[4]{0:T(128)S(1)} %get-tuple-element.294, s32[1]{0:T(128)} %constant.14.clone.1.skip_ref, s32[1,1280]{1,0:T(1,128)S(1)} %get-tuple-element.291, s32[8,128]{1,0:T(8,128)S(1)} %get-tuple-element.292, bf16[256,1280]{1,0:T(8,128)(2,1)S(1)} %get-tuple-element.78.high_ref, ...), custom_call_target="tpu_custom_call" | custom-call | flops 1 | bytes 1 | tf_op jit(solution)/shard_map/cross_part/pallas_call | solution.py:251
  35.8 1.8 %collective-permute-start.15 = (f32[32,1280]{1,0:T(8,128)S(1)}, f32[32,1280]{1,0:T(8,128)S(1)}, u32[]{:S(2)}, u32[]{:S(2)}) collective-permute-start(f32[32,1280]{1,0:T(8,128)S(1)} %collective-permute-done.14.refs_6_), channel_id=1, source_target_pairs={{0,8},{4,12},{8,0},{12,4},{16,24},{20,28},{24,16},{28,20},{1,9},{5... | collective-permute-start | bytes 491528 | tf_op jit(solution)/shard_map/ppermute | solution.py:343
  37.6 0.5 %collective-permute-start.11 = (f32[264,128]{1,0:T(8,128)S(1)}, f32[264,128]{1,0:T(8,128)S(1)}, u32[]{:S(2)}, u32[]{:S(2)}) collective-permute-start(f32[264,128]{1,0:T(8,128)S(1)} %cross_part.4.refs_0_), channel_id=1, source_target_pairs={{0,2},{1,3},{2,0},{3,1},{4,6},{5,7},{6,4},{7,5},{8,10},{9,11},{10,... | collective-permute-start | bytes 405512 | tf_op jit(solution)/shard_map/ppermute | solution.py:343
  38.1 1.3 %collective-permute-start.12 = (f32[264,128]{1,0:T(8,128)S(1)}, f32[264,128]{1,0:T(8,128)S(1)}, u32[]{:S(2)}, u32[]{:S(2)}) collective-permute-start(f32[264,128]{1,0:T(8,128)S(1)} %cross_part.4.refs_0_), channel_id=1, source_target_pairs={{0,3},{1,2},{2,1},{3,0},{4,7},{5,6},{6,5},{7,4},{8,11},{9,10},{10,... | collective-permute-start | bytes 405512 | tf_op jit(solution)/shard_map/ppermute | solution.py:343
  39.5 0.3 tapers.1.taper_ref
  39.8 0.4 collective-permute-done.13.refs_5_
  40.2 3.8 %collective-permute-done.11.refs_2_ = f32[264,128]{1,0:T(8,128)S(1)} collective-permute-done((f32[264,128]{1,0:T(8,128)S(1)}, f32[264,128]{1,0:T(8,128)S(1)}, u32[]{:S(2)}, u32[]{:S(2)}) %collective-permute-start.11) | collective-permute-done | bytes 135200 | tf_op jit(solution)/shard_map/ppermute | solution.py:343
  44.0 2.1 %collective-permute-done.12.refs_3_ = f32[264,128]{1,0:T(8,128)S(1)} collective-permute-done((f32[264,128]{1,0:T(8,128)S(1)}, f32[264,128]{1,0:T(8,128)S(1)}, u32[]{:S(2)}, u32[]{:S(2)}) %collective-permute-start.12) | collective-permute-done | bytes 135200 | tf_op jit(solution)/shard_map/ppermute | solution.py:343
  46.1 2.3 %final.1 = f32[256,1280]{1,0:T(8,128)} custom-call(f32[4]{0:T(128)S(1)} %get-tuple-element.294, f32[256,128]{1,0:T(8,128)S(1)} %tapers.1.taper_ref, f32[32,256]{1,0:T(8,128)S(1)} %get-tuple-element.290, f32[264,128]{1,0:T(8,128)S(1)} %cross_part.4.refs_0_, f32[264,128]{1,0:T(8,128)S(1)} %collective-permute-done.10.refs_1_, ...), custom_call_target="tpu_custom_call" | custom-call | flops 1 | bytes 1 | tf_op jit(solution)/shard_map/final/pallas_call | solution.py:324
  (29 shorter events, 0.4 us)
Async XLA Ops:
  0.0 23.6 %copy-start.9 = (s32[128]{0:T(128)S(1)}, s32[128]{0:T(128)}, u32[]{:S(2)}) copy-start(s32[128]{0:T(128)} %obs_ref.1) | copy-start | bytes 1540
  0.0 9.4 %copy-start.4 = (f32[256,1280]{1,0:T(8,128)S(1)}, f32[256,1280]{1,0:T(8,128)}, u32[]{:S(2)}) copy-start(f32[256,1280]{1,0:T(8,128)} %state_ref.2) | copy-start | bytes 3932164
  0.0 9.3 %copy-start.11 = (s32[1280]{0:T(1024)S(1)}, s32[1280]{0:T(1024)}, u32[]{:S(2)}) copy-start(s32[1280]{0:T(1024)} %param.9) | copy-start | bytes 15364
  0.0 18.8 %copy-start.2 = (f32[16,1280]{1,0:T(8,128)S(1)}, f32[16,1280]{1,0:T(8,128)}, u32[]{:S(2)}) copy-start(f32[16,1280]{1,0:T(8,128)} %near_ref.1) | copy-start | bytes 245764
  0.0 29.2 %copy-start.10 = (f32[4]{0:T(128)S(1)}, f32[4]{0:T(128)}, u32[]{:S(2)}) copy-start(f32[4]{0:T(128)} %weight_ref.5) | copy-start | bytes 52
  2.1 10.0 %collective-permute-start = (f32[32,1280]{1,0:T(8,128)S(1)}, f32[32,1280]{1,0:T(8,128)S(1)}, u32[]{:S(2)}, u32[]{:S(2)}) collective-permute-start(f32[32,1280]{1,0:T(8,128)S(1)} %pick.2.refs_0_), channel_id=1, source_target_pairs={{0,8},{4,12},{8,0},{12,4},{16,24},{20,28},{24,16},{28,20},{1,9},{5... | collective-permute-start | bytes 491528 | tf_op jit(solution)/shard_map/ppermute | solution.py:343
  5.2 13.6 %collective-permute-start.4 = (f32[32,1280]{1,0:T(8,128)S(1)}, f32[32,1280]{1,0:T(8,128)S(1)}, u32[]{:S(2)}, u32[]{:S(2)}) collective-permute-start(f32[32,1280]{1,0:T(8,128)S(1)} %pick.2.refs_0_), channel_id=1, source_target_pairs={{0,4},{4,0},{8,12},{12,8},{16,20},{20,16},{24,28},{28,24},{1,5},{5... | collective-permute-start | bytes 491528 | tf_op jit(solution)/shard_map/ppermute | solution.py:343
  6.8 9.8 %collective-permute-start.6 = (f32[32,1280]{1,0:T(8,128)S(1)}, f32[32,1280]{1,0:T(8,128)S(1)}, u32[]{:S(2)}, u32[]{:S(2)}) collective-permute-start(f32[32,1280]{1,0:T(8,128)S(1)} %pick.2.refs_0_), channel_id=1, source_target_pairs={{0,16},{4,20},{8,24},{12,28},{16,0},{20,4},{24,8},{28,12},{1,17},{... | collective-permute-start | bytes 491528 | tf_op jit(solution)/shard_map/ppermute | solution.py:343
  10.9 1.2 %collective-permute-start.1 = (f32[8,256]{1,0:T(8,128)S(1)}, f32[8,256]{1,0:T(8,128)S(1)}, u32[]{:S(2)}, u32[]{:S(2)}) collective-permute-start(f32[8,256]{1,0:T(8,128)S(1)} %get-tuple-element.73), channel_id=1, source_target_pairs={{0,1},{1,0},{2,3},{3,2},{4,5},{5,4},{6,7},{7,6},{8,9},{9,8},{10,11... | collective-permute-start | bytes 24584 | tf_op jit(solution)/shard_map/ppermute | solution.py:343
  12.1 9.0 %collective-permute-start.2 = (f32[32,1280]{1,0:T(8,128)S(1)}, f32[32,1280]{1,0:T(8,128)S(1)}, u32[]{:S(2)}, u32[]{:S(2)}) collective-permute-start(f32[32,1280]{1,0:T(8,128)S(1)} %collective-permute-done.refs_1_), channel_id=1, source_target_pairs={{0,4},{4,0},{8,12},{12,8},{16,20},{20,16},{24,28},{28,24},{1,5},{5... | collective-permute-start | bytes 491528 | tf_op jit(solution)/shard_map/ppermute | solution.py:343
  16.5 6.2 %collective-permute-start.7 = (f32[32,1280]{1,0:T(8,128)S(1)}, f32[32,1280]{1,0:T(8,128)S(1)}, u32[]{:S(2)}, u32[]{:S(2)}) collective-permute-start(f32[32,1280]{1,0:T(8,128)S(1)} %collective-permute-done.6.refs_0_), channel_id=1, source_target_pairs={{0,4},{4,0},{8,12},{12,8},{16,20},{20,16},{24,28},{28,24},{1,5},{5... | collective-permute-start | bytes 491528 | tf_op jit(solution)/shard_map/ppermute | solution.py:343
  17.1 9.9 %collective-permute-start.8 = (f32[32,1280]{1,0:T(8,128)S(1)}, f32[32,1280]{1,0:T(8,128)}, u32[]{:S(2)}, u32[]{:S(2)}) collective-permute-start(f32[32,1280]{1,0:T(8,128)S(1)} %collective-permute-done.6.refs_0_), channel_id=1, source_target_pairs={{0,8},{4,12},{8,0},{12,4},{16,24},{20,28},{24,16},{28,20},{1,9},{5... | collective-permute-start | bytes 491528 | tf_op jit(solution)/shard_map/ppermute | solution.py:343
  17.3 3.7 %collective-permute-start.3 = (f32[16,256]{1,0:T(8,128)S(1)}, f32[16,256]{1,0:T(8,128)S(1)}, u32[]{:S(2)}, u32[]{:S(2)}) collective-permute-start(f32[16,256]{1,0:T(8,128)S(1)} %get-tuple-element.116), channel_id=1, source_target_pairs={{0,2},{1,3},{2,0},{3,1},{4,6},{5,7},{6,4},{7,5},{8,10},{9,11},{10,... | collective-permute-start | bytes 49160 | tf_op jit(solution)/shard_map/ppermute | solution.py:343
  18.8 4.8 %collective-permute-start.5 = (f32[16,1280]{1,0:T(8,128)S(1)}, f32[16,1280]{1,0:T(8,128)S(1)}, u32[]{:S(2)}, u32[]{:S(2)}) collective-permute-start(f32[16,1280]{1,0:T(8,128)S(1)} %copy-done.2), channel_id=1, source_target_pairs={{0,4},{4,0},{8,12},{12,8},{16,20},{20,16},{24,28},{28,24},{1,5},{5... | collective-permute-start | bytes 245768 | tf_op jit(solution)/shard_map/ppermute | solution.py:343
  21.1 0.7 %copy-start = (f32[32,1280]{1,0:T(8,128)}, f32[32,1280]{1,0:T(8,128)S(1)}, u32[]{:S(2)}) copy-start(f32[32,1280]{1,0:T(8,128)S(1)} %collective-permute-done.2.refs_3_) | copy-start | bytes 491524
  24.5 11.3 %collective-permute-start.14 = (f32[32,1280]{1,0:T(8,128)S(1)}, f32[32,1280]{1,0:T(8,128)S(1)}, u32[]{:S(2)}, u32[]{:S(2)}) collective-permute-start(f32[32,1280]{1,0:T(8,128)S(1)} %get-tuple-element.85.refs_4_), channel_id=1, source_target_pairs={{0,16},{4,20},{8,24},{12,28},{16,0},{20,4},{24,8},{28,12},{1,17},{... | collective-permute-start | bytes 491528 | tf_op jit(solution)/shard_map/ppermute | solution.py:343
  27.1 6.4 %collective-permute-start.9 = (f32[32,1280]{1,0:T(8,128)}, f32[32,1280]{1,0:T(8,128)}, u32[]{:S(2)}, u32[]{:S(2)}) collective-permute-start(f32[32,1280]{1,0:T(8,128)} %collective-permute-done.8.refs_1_), channel_id=1, source_target_pairs={{0,4},{4,0},{8,12},{12,8},{16,20},{20,16},{24,28},{28,24},{1,5},{5... | collective-permute-start | bytes 491528 | tf_op jit(solution)/shard_map/ppermute | solution.py:343
  29.9 0.9 %copy-start.1 = (f32[32,1280]{1,0:T(8,128)S(1)}, f32[32,1280]{1,0:T(8,128)}, u32[]{:S(2)}) copy-start(f32[32,1280]{1,0:T(8,128)} %copy-done) | copy-start | bytes 491524
  33.1 6.4 %copy-start.3 = (s32[2,2048]{1,0:T(2,128)S(1)}, s32[2,2048]{1,0:T(2,128)}, u32[]{:S(2)}) copy-start(s32[2,2048]{1,0:T(2,128)} %coords_ref.1) | copy-start | bytes 49156
  33.1 7.0 %collective-permute-start.13 = (f32[32,1280]{1,0:T(8,128)S(1)}, f32[32,1280]{1,0:T(8,128)S(1)}, u32[]{:S(2)}, u32[]{:S(2)}) collective-permute-start(f32[32,1280]{1,0:T(8,128)S(1)} %get-tuple-element.85.refs_4_), channel_id=1, source_target_pairs={{0,8},{4,12},{8,0},{12,4},{16,24},{20,28},{24,16},{28,20},{1,9},{5... | collective-permute-start | bytes 491528 | tf_op jit(solution)/shard_map/ppermute | solution.py:343
  35.8 10.3 %collective-permute-start.15 = (f32[32,1280]{1,0:T(8,128)S(1)}, f32[32,1280]{1,0:T(8,128)S(1)}, u32[]{:S(2)}, u32[]{:S(2)}) collective-permute-start(f32[32,1280]{1,0:T(8,128)S(1)} %collective-permute-done.14.refs_6_), channel_id=1, source_target_pairs={{0,8},{4,12},{8,0},{12,4},{16,24},{20,28},{24,16},{28,20},{1,9},{5... | collective-permute-start | bytes 491528 | tf_op jit(solution)/shard_map/ppermute | solution.py:343
  37.6 2.6 %collective-permute-start.10 = (f32[264,128]{1,0:T(8,128)S(1)}, f32[264,128]{1,0:T(8,128)S(1)}, u32[]{:S(2)}, u32[]{:S(2)}) collective-permute-start(f32[264,128]{1,0:T(8,128)S(1)} %cross_part.4.refs_0_), channel_id=1, source_target_pairs={{0,1},{1,0},{2,3},{3,2},{4,5},{5,4},{6,7},{7,6},{8,9},{9,8},{10,11... | collective-permute-start | bytes 405512 | tf_op jit(solution)/shard_map/ppermute | solution.py:343
  37.6 6.4 %collective-permute-start.11 = (f32[264,128]{1,0:T(8,128)S(1)}, f32[264,128]{1,0:T(8,128)S(1)}, u32[]{:S(2)}, u32[]{:S(2)}) collective-permute-start(f32[264,128]{1,0:T(8,128)S(1)} %cross_part.4.refs_0_), channel_id=1, source_target_pairs={{0,2},{1,3},{2,0},{3,1},{4,6},{5,7},{6,4},{7,5},{8,10},{9,11},{10,... | collective-permute-start | bytes 405512 | tf_op jit(solution)/shard_map/ppermute | solution.py:343
  38.1 8.0 %collective-permute-start.12 = (f32[264,128]{1,0:T(8,128)S(1)}, f32[264,128]{1,0:T(8,128)S(1)}, u32[]{:S(2)}, u32[]{:S(2)}) collective-permute-start(f32[264,128]{1,0:T(8,128)S(1)} %cross_part.4.refs_0_), channel_id=1, source_target_pairs={{0,3},{1,2},{2,1},{3,0},{4,7},{5,6},{6,5},{7,4},{8,11},{9,10},{10,... | collective-permute-start | bytes 405512 | tf_op jit(solution)/shard_map/ppermute | solution.py:343

commit v3 on v2

--- a/solution.py
+++ b/solution.py
@@ -46,11 +46,14 @@
     return picked
 
 
-def pick_kernel(obs_ref, skip_ref, state_ref, out_ref, list_ref):
+def pick_kernel(obs_ref, skip_ref, weights_ref, state_ref, out_ref, both_ref, list_ref, held_ref, sem):
     rows = state_ref.shape[0]
-    slots = out_ref.shape[0]
+    slots, members = out_ref.shape
     row_first = lax.axis_index("rows") * rows
     skip = skip_ref[0]
+    copy = pltpu.make_async_copy(state_ref, held_ref, sem)
+    copy.start()
+    both_ref[slots:, :] = weights_ref[...]
 
     def visit(j, rank):
         row = obs_ref[j] - row_first
@@ -59,32 +62,36 @@
 
     total = lax.fori_loop(0, obs_ref.shape[0], visit, 0, unroll=8)
     held = jnp.clip(total - skip, 0, slots)
-
-    def bring(slot, carry):
-        out_ref[pl.ds(slot, 1), :] = state_ref[pl.ds(list_ref[skip + slot], 1), :]
-        return carry
-
-    def clear(slot, carry):
-        out_ref[pl.ds(slot, 1), :] = jnp.zeros((1, out_ref.shape[1]), F32)
-        return carry
-
-    lax.fori_loop(0, held, bring, 0)
-    lax.fori_loop(held, slots, clear, 0)
-
-
-def pick(obs_row, skip, state, slots):
+    copy.wait()
+
+    for slot in range(slots):
+        row = jnp.clip(list_ref[skip + slot], 0, rows - 1)
+        value = jnp.where(slot < held, held_ref[pl.ds(row, 1), :], 0.0)
+        out_ref[slot : slot + 1, :] = value
+        both_ref[slot : slot + 1, :] = value
+
+
+def pick(obs_row, skip, weights, state, slots):
+    members = state.shape[1]
     smem = pl.BlockSpec(memory_space=pltpu.SMEM)
     vmem = pl.BlockSpec(memory_space=pltpu.VMEM)
     return pl.pallas_call(
         pick_kernel,
-        out_shape=jax.ShapeDtypeStruct((slots, state.shape[1]), F32),
-        in_specs=[smem, smem, vmem],
-        out_specs=vmem,
-        scratch_shapes=[pltpu.SMEM((obs_row.shape[0] + 1,), jnp.int32)],
+        out_shape=(
+            jax.ShapeDtypeStruct((slots, members), F32),
+            jax.ShapeDtypeStruct((slots + weights.shape[0], members), F32),
+        ),
+        in_specs=[smem, smem, vmem, pl.BlockSpec(memory_space=pl.ANY)],
+        out_specs=(vmem, vmem),
+        scratch_shapes=[
+            pltpu.SMEM((obs_row.shape[0] + slots + 1,), jnp.int32),
+            pltpu.VMEM(state.shape, F32),
+            pltpu.SemaphoreType.DMA(()),
+        ],
         compiler_params=pltpu.CompilerParams(vmem_limit_bytes=VMEM_LIMIT),
         cost_estimate=COST,
         name="pick",
-    )(obs_row, skip, state)
+    )(obs_row, skip, weights, state)
 
 
 def center_kernel(level_ref, state_ref, sums_ref, high_ref, low_ref):
@@ -129,11 +136,29 @@
     )(level_row, state)
 
 
-def place_kernel(slots, rows, obs_ref, near_ref, far_ref, place_ref, rounds_ref, pair_ref):
-    observed = obs_ref.shape[1]
+def pair_kernel(near_ref, far_ref, pair_ref):
     length = near_ref.shape[0]
     pair_ref[0:length, :] = near_ref[...]
-    pair_ref[length : 2 * length, :] = far_ref[...]
+    pair_ref[length : 2 * length, :] = far_ref[far_ref.shape[0] - length :, :]
+
+
+def pairs(near, far):
+    length, members = near.shape
+    vmem = pl.BlockSpec(memory_space=pltpu.VMEM)
+    return pl.pallas_call(
+        pair_kernel,
+        out_shape=jax.ShapeDtypeStruct((2 * length, members), F32),
+        in_specs=[vmem, vmem],
+        out_specs=vmem,
+        compiler_params=pltpu.CompilerParams(vmem_limit_bytes=VMEM_LIMIT),
+        cost_estimate=COST,
+        name="pairs",
+    )(near, far)
+
+
+def place_kernel(slots, rows, obs_ref, place_ref, rounds_ref, zero_ref):
+    observed = obs_ref.shape[1]
+    zero_ref[...] = jnp.zeros_like(zero_ref)
     owner = lax.div(obs_ref[...], jnp.int32(rows))
     owner_row = owner.astype(F32)
     owner_down = jnp.transpose(jnp.broadcast_to(owner_row, (SUB, observed)))[:, 0:1]
@@ -147,9 +172,8 @@
     rounds_ref[0] = lax.div(jnp.max(rank), jnp.int32(slots)) + 1
 
 
-def places(obs_row, near, far, rows, slots):
+def places(obs_row, rows, slots):
     observed = obs_row.shape[0]
-    length, members = near.shape
     vmem = pl.BlockSpec(memory_space=pltpu.VMEM)
     smem = pl.BlockSpec(memory_space=pltpu.SMEM)
     return pl.pallas_call(
@@ -157,13 +181,13 @@
         out_shape=(
             jax.ShapeDtypeStruct((SUB, observed), jnp.int32),
             jax.ShapeDtypeStruct((1,), jnp.int32),
-            jax.ShapeDtypeStruct((2 * length, members), F32),
+            jax.ShapeDtypeStruct((rows + SUB, observed), F32),
         ),
-        in_specs=[vmem] * 3,
+        in_specs=[vmem],
         out_specs=(vmem, smem, vmem),
         compiler_params=pltpu.CompilerParams(vmem_limit_bytes=VMEM_LIMIT),
         name="places",
-    )(obs_row[None, :], near, far)
+    )(obs_row[None, :])
 
 
 def taper_kernel(radius, obs_ref, coords_ref, taper_ref):
@@ -220,7 +244,7 @@
     m_ref[...] = jnp.zeros_like(m_ref)
     for n, block_ref in enumerate(blocks):
         at = n * padded
-        block = block_ref[...]
+        block = block_ref[0:slots, :]
         columns = []
         for level in range(LEVELS):
             member = jnp.where(level_row == level, block, 0.0)
@@ -242,9 +266,8 @@
     out_ref[rows : rows + SUB, :] = before_ref[rows : rows + SUB, :] + means
 
 
-def cross_part(level_weight, skip, level_row, place, high, low, before, blocks, sums, number):
+def cross_part(level_weight, skip, level_row, place, high, low, before, blocks, sums, slots, number):
     rows, members = high.shape
-    slots = blocks[0].shape[0]
     smem = pl.BlockSpec(memory_space=pltpu.SMEM)
     vmem = pl.BlockSpec(memory_space=pltpu.VMEM)
     held = len(number) * slots
@@ -364,28 +387,31 @@
     slots = min(observed, 16 * (-(-2 * observed // groups) // 16))
 
     none = jnp.zeros((1,), jnp.int32)
-    own = pick(obs_row, none, state, slots)
+    own, own_both = pick(obs_row, none, weights, state, slots)
     level_row = after(member_level, own)[None, :]
     sums, high, low = center(level_row, after(state, own))
-    all_sums = sums
-    for n in range(lax.axis_size("mem").bit_length() - 1):
+    near_far = across(own_both, "rows", 1)
+    near_sums = after(sums, near_far)
+    near_sums = jnp.concatenate([near_sums, across(near_sums, "mem", 1)])
+    place, rounds, empty = places(after(obs_row, own), row_count, slots)
+    first_far = across(own, "rows", bits[0])
+    line = gather_line(own, bits[1:])
+    line |= {
+        b ^ bits[0]: x for b, x in gather_line(after(first_far, near_sums, place), bits[1:]).items()
+    }
+    forward = {b: x for b, x in line.items()}
+    other = {b ^ 1: across(x, "rows", 1) if b else near_far for b, x in forward.items()}
+    all_sums = near_sums
+    for n in range(1, lax.axis_size("mem").bit_length() - 1):
         all_sums = jnp.concatenate([all_sums, across(all_sums, "mem", 1 << n)])
-        if n == 0:
-            first_sums = all_sums
-
-    line = gather_line(own, bits)
-    other = {b ^ 1: across(after(x, first_sums) if b == 2 else x, "rows", 1) for b, x in line.items()}
     blocks = line | other
     early = [b for b in blocks if b < bits[0]]
     late = [b for b in blocks if b >= bits[0]]
 
-    weights_far = across(after(weights, other[1]), "rows", 1)
-    place, rounds, weights_pair = places(
-        after(obs_row, other[early[-1]], all_sums), weights, weights_far, row_count, slots
-    )
+    weights_pair = pairs(weights, after(other[1], all_sums))
 
     def cross(skip, part, high, low, held, number):
-        return cross_part(level_weight, skip, level_row, place, high, low, part, held, all_sums, number)
+        return cross_part(level_weight, skip, level_row, place, high, low, part, held, all_sums, slots, number)
 
     def more(carry):
         return carry[0] < rounds[0]
@@ -394,7 +420,7 @@
         turn, part = carry
         skip = (turn * slots)[None]
         again = after(state, turn)
-        block = pick(obs_row, skip, again, slots)
+        block, _ = pick(obs_row, skip, weights, again, slots)
         _, high, low = center(level_row, again)
         parcels = [lax.all_gather(x, "rows", axis=0) for x in jnp.split(block, slots // 16)]
         every = jnp.concatenate(parcels, axis=1)
@@ -402,13 +428,12 @@
         part = cross(skip, part, high, low, [every[me ^ b] for b in early + late], early + late)
         return turn + 1, part
 
-    empty = jnp.zeros((row_count + SUB, observed), F32)
-    _, part = lax.while_loop(more, another, (jnp.int32(1), after(empty, other[bits[0] ^ 1])))
-    half = cross(none, part, high, low, [blocks[b] for b in early], early)
+    _, looped = lax.while_loop(more, another, (jnp.int32(1), empty))
+    half = cross(none, looped, high, low, [blocks[b] for b in early], early)
     part = cross(none, half, high, low, [blocks[b] for b in late], late)
     parts = [part] + [across(part, "mem", b) for b in range(1, lax.axis_size("mem"))]
 
-    far_pair = across(weights_pair, "rows", bits[0])
+    far_pair = across(after(weights_pair, looped), "rows", bits[0])
     weights_line = gather_line(after(weights_pair, half), bits[1:])
     weights_line |= {b ^ bits[0]: x for b, x in gather_line(after(far_pair, part), bits[1:]).items()}
     taper = tapers(after(obs_row, part), state_coords, row_count, radius)

time: 48.6 us -> 43.2 us (0.89)
  the two profiles are of different devices: /device:TPU:0 before, /device:TPU:17 now
where the time goes in v3:
time: 43.2 us; the launch traced here: 43 us
  starting transfers between devices  16.6 us (38%)
  Pallas kernels  13.8 us (32%)
  waiting for transfers between devices  11.7 us (27%)
  loops' own time  0.63 us (1%)
    ppermute x15, starting transfers between devices, across(): return lax.ppermute(x, axis, [(i, i ^ bits) for i in range(count)])  16.6 us
    ppermute x15, waiting for transfers between devices, across(): return lax.ppermute(x, axis, [(i, i ^ bits) for i in range(count)])  11.7 us
    pallas_call x2, Pallas kernels, cross_part(): pl.pallas_call(functools.partial(cross_kernel, number, slots), out_shape=...  4.16 us
    pallas_call x1, Pallas kernels, pick(): pl.pallas_call(pick_kernel, out_shape=(jax.ShapeDtypeStruct((slots, membe...  2.49 us
    pallas_call x1, Pallas kernels, final(): pl.pallas_call(functools.partial(final_kernel, number, len(parts), width)...  2.3 us
    pallas_call x1, Pallas kernels, places(): pl.pallas_call(functools.partial(place_kernel, slots, rows), out_shape=(j...  1.55 us
    pallas_call x1, Pallas kernels, center(): pl.pallas_call(center_kernel, out_shape=(jax.ShapeDtypeStruct((SUB, rows)...  1.49 us
    pallas_call x1, Pallas kernels, tapers(): pl.pallas_call(functools.partial(taper_kernel, radius), out_shape=jax.Sha...  0.93 us
  transfers between devices with their start and end apart: 15, of which 5 were waited for; matrix products, arithmetic and copies ran while one was open for 0% of the time, Pallas kernels for 21%

profile of v3, /device:TPU:17, one launch (start us, length us, event | category | flops | bytes accessed | tf_op | source)
XLA Modules:
  0.0 43.0 jit_solution(1893878280972751471)
XLA Ops:
  0.0 2.5 %pick.2 = (f32[32,1280]{1,0:T(8,128)S(1)}, f32[48,1280]{1,0:T(8,128)S(1)}) custom-call(s32[128]{0:T(128)} %obs_ref.1, s32[1]{0:T(128)} %constant.28.clone.1.skip_ref, f32[16,1280]{1,0:T(8,128)} %near_ref.1, f32[256,1280]{1,0:T(8,128)} %state_ref.2), custom_call_target="tpu_custom_call" | custom-call | flops 1 | bytes 1 | tf_op jit(solution)/shard_map/pick/pallas_call | solution.py:78
  2.5 1.3 %collective-permute-start = (f32[48,1280]{1,0:T(8,128)S(1)}, f32[48,1280]{1,0:T(8,128)S(1)}, u32[]{:S(2)}, u32[]{:S(2)}) collective-permute-start(f32[48,1280]{1,0:T(8,128)S(1)} %get-tuple-element.90), channel_id=1, source_target_pairs={{0,4},{4,0},{8,12},{12,8},{16,20},{20,16},{24,28},{28,24},{1,5},{5... | collective-permute-start | bytes 737288 | tf_op jit(solution)/shard_map/ppermute | solution.py:366
  3.8 1.3 %collective-permute-start.3 = (f32[32,1280]{1,0:T(8,128)S(1)}, f32[32,1280]{1,0:T(8,128)S(1)}, u32[]{:S(2)}, u32[]{:S(2)}) collective-permute-start(f32[32,1280]{1,0:T(8,128)S(1)} %get-tuple-element.80.refs_0_), channel_id=1, source_target_pairs={{0,8},{4,12},{8,0},{12,4},{16,24},{20,28},{24,16},{28,20},{1,9},{5... | collective-permute-start | bytes 491528 | tf_op jit(solution)/shard_map/ppermute | solution.py:366
  5.1 0.1 collective-permute-start.5
  5.2 1.5 %center.2 = (f32[8,256]{1,0:T(8,128)S(1)}, bf16[256,1280]{1,0:T(8,128)(2,1)S(1)}, bf16[256,1280]{1,0:T(8,128)(2,1)S(1)}) custom-call(s32[1,1280]{1,0:T(1,128)S(1)} %broadcast_in_dim.12.level_ref, f32[256,1280]{1,0:T(8,128)S(1)} %copy-done.1), custom_call_target="tpu_custom_call" | custom-call | flops 1 | bytes 1 | tf_op jit(solution)/shard_map/center/pallas_call | solution.py:116
  6.7 2.7 %collective-permute-done.refs_2_.far_ref = f32[48,1280]{1,0:T(8,128)S(1)} collective-permute-done((f32[48,1280]{1,0:T(8,128)S(1)}, f32[48,1280]{1,0:T(8,128)S(1)}, u32[]{:S(2)}, u32[]{:S(2)}) %collective-permute-start) | collective-permute-done | bytes 245792 | tf_op jit(solution)/shard_map/ppermute | solution.py:366
  9.4 1.5 %collective-permute-start.1 = (f32[8,256]{1,0:T(8,128)S(1)}, f32[8,256]{1,0:T(8,128)S(1)}, u32[]{:S(2)}, u32[]{:S(2)}) collective-permute-start(f32[8,256]{1,0:T(8,128)S(1)} %get-tuple-element.91), channel_id=1, source_target_pairs={{0,1},{1,0},{2,3},{3,2},{4,5},{5,4},{6,7},{7,6},{8,9},{9,8},{10,11... | collective-permute-start | bytes 24584 | tf_op jit(solution)/shard_map/ppermute | solution.py:366
  10.9 0.8 %collective-permute-done.1 = f32[8,256]{1,0:T(8,128)S(1)} collective-permute-done((f32[8,256]{1,0:T(8,128)S(1)}, f32[8,256]{1,0:T(8,128)S(1)}, u32[]{:S(2)}, u32[]{:S(2)}) %collective-permute-start.1) | collective-permute-done | bytes 8224 | tf_op jit(solution)/shard_map/ppermute | solution.py:366
  11.8 1.2 %collective-permute-start.2 = (f32[16,256]{1,0:T(8,128)S(1)}, f32[16,256]{1,0:T(8,128)S(1)}, u32[]{:S(2)}, u32[]{:S(2)}) collective-permute-start(f32[16,256]{1,0:T(8,128)S(1)} %get-tuple-element.129), channel_id=1, source_target_pairs={{0,2},{1,3},{2,0},{3,1},{4,6},{5,7},{6,4},{7,5},{8,10},{9,11},{10,... | collective-permute-start | bytes 49160 | tf_op jit(solution)/shard_map/ppermute | solution.py:366
  13.0 1.6 %places.1 = (s32[8,128]{1,0:T(8,128)}, s32[1]{0:T(128)}, f32[264,128]{1,0:T(8,128)}) custom-call(s32[1,128]{1,0:T(1,128)} %bitcast.12.obs_ref), custom_call_target="tpu_custom_call" | custom-call | tf_op jit(solution)/shard_map/places/pallas_call | solution.py:179
  14.5 0.0 collective-permute-done.3.refs_1_
  14.5 1.3 %collective-permute-start.4 = (f32[32,1280]{1,0:T(8,128)S(1)}, f32[32,1280]{1,0:T(8,128)S(1)}, u32[]{:S(2)}, u32[]{:S(2)}) collective-permute-start(f32[32,1280]{1,0:T(8,128)S(1)} %collective-permute-done.3.refs_1_), channel_id=1, source_target_pairs={{0,4},{4,0},{8,12},{12,8},{16,20},{20,16},{24,28},{28,24},{1,5},{5... | collective-permute-start | bytes 491528 | tf_op jit(solution)/shard_map/ppermute | solution.py:366
  15.9 1.3 %collective-permute-start.6 = (f32[32,1280]{1,0:T(8,128)S(1)}, f32[32,1280]{1,0:T(8,128)S(1)}, u32[]{:S(2)}, u32[]{:S(2)}) collective-permute-start(f32[32,1280]{1,0:T(8,128)S(1)} %collective-permute-done.5.refs_0_), channel_id=1, source_target_pairs={{0,8},{4,12},{8,0},{12,4},{16,24},{20,28},{24,16},{28,20},{1,9},{5... | collective-permute-start | bytes 491528 | tf_op jit(solution)/shard_map/ppermute | solution.py:366
  17.2 0.2 collective-permute-start.7
  17.4 0.0 collective-permute-done.2
  17.4 0.6 %while.10 = (s32[]{:T(128)}, f32[264,128]{1,0:T(8,128)}, s32[1]{0:T(128)}, f32[256,1280]{1,0:T(8,128)}, s32[1,1280]{1,0:T(1,128)}, /*index=5*/s32[128]{0:T(128)}...) while((s32[]{:T(128)}, f32[264,128]{1,0:T(8,128)}, ...), condition=%wide.region_1.0_spmd, body=%wide.region_0.0_spmd.sunk | while | flops 327720 | bytes 17068924 | solution.py:431
  18.0 0.0 copy-start.12
  18.1 0.9 %pairs.1.refs_4_ = f32[32,1280]{1,0:T(8,128)S(1)} custom-call(f32[16,1280]{1,0:T(8,128)} %near_ref.1, f32[48,1280]{1,0:T(8,128)S(1)} %collective-permute-done.refs_2_.far_ref), custom_call_target="tpu_custom_call" | custom-call | flops 1 | bytes 1 | tf_op jit(solution)/shard_map/pairs/pallas_call | solution.py:148
  19.0 1.7 %collective-permute-done.6.refs_1_ = f32[32,1280]{1,0:T(8,128)S(1)} collective-permute-done((f32[32,1280]{1,0:T(8,128)S(1)}, f32[32,1280]{1,0:T(8,128)S(1)}, u32[]{:S(2)}, u32[]{:S(2)}) %collective-permute-start.6) | collective-permute-done | bytes 163872 | tf_op jit(solution)/shard_map/ppermute | solution.py:366
  20.7 0.2 collective-permute-start.8
  20.9 0.1 collective-permute-start.13
  20.9 2.3 %cross_part.3.before_ref = f32[264,128]{1,0:T(8,128)S(1)} custom-call(f32[4]{0:T(128)} %get-tuple-element.319, s32[1]{0:T(128)} %constant.28.clone.1.skip_ref, s32[1,1280]{1,0:T(1,128)} %get-tuple-element.317, s32[8,128]{1,0:T(8,128)} %get-tuple-element.318, bf16[256,1280]{1,0:T(8,128)(2,1)S(1)} %get-tuple-element.85.high_ref, ...), custom_call_target="tpu_custom_call" | custom-call | flops 1 | bytes 1 | tf_op jit(solution)/shard_map/cross_part/pallas_call | solution.py:274
  23.2 1.4 %collective-permute-start.12 = (f32[32,1280]{1,0:T(8,128)S(1)}, f32[32,1280]{1,0:T(8,128)S(1)}, u32[]{:S(2)}, u32[]{:S(2)}) collective-permute-start(f32[32,1280]{1,0:T(8,128)S(1)} %pairs.1.refs_4_), channel_id=1, source_target_pairs={{0,8},{4,12},{8,0},{12,4},{16,24},{20,28},{24,16},{28,20},{1,9},{5... | collective-permute-start | bytes 491528 | tf_op jit(solution)/shard_map/ppermute | solution.py:366
  24.6 0.0 collective-permute-done.7.refs_2_
  24.6 1.9 %collective-permute-done.8.refs_3_ = f32[32,1280]{1,0:T(8,128)S(1)} collective-permute-done((f32[32,1280]{1,0:T(8,128)S(1)}, f32[32,1280]{1,0:T(8,128)S(1)}, u32[]{:S(2)}, u32[]{:S(2)}) %collective-permute-start.8) | collective-permute-done | bytes 163872 | tf_op jit(solution)/shard_map/ppermute | solution.py:366
  26.5 1.9 %cross_part.4.refs_0_ = f32[264,128]{1,0:T(8,128)S(1)} custom-call(f32[4]{0:T(128)S(1)} %copy-done.12, s32[1]{0:T(128)} %constant.28.clone.1.skip_ref, s32[1,1280]{1,0:T(1,128)S(1)} %copy-done.8, s32[8,128]{1,0:T(8,128)S(1)} %copy-done.10, bf16[256,1280]{1,0:T(8,128)(2,1)S(1)} %get-tuple-element.85.high_ref, ...), custom_call_target="tpu_custom_call" | custom-call | flops 1 | bytes 1 | tf_op jit(solution)/shard_map/cross_part/pallas_call | solution.py:274
  28.4 3.4 %collective-permute-start.14 = (f32[32,1280]{1,0:T(8,128)S(1)}, f32[32,1280]{1,0:T(8,128)S(1)}, u32[]{:S(2)}, u32[]{:S(2)}) collective-permute-start(f32[32,1280]{1,0:T(8,128)S(1)} %collective-permute-done.13.refs_6_), channel_id=1, source_target_pairs={{0,8},{4,12},{8,0},{12,4},{16,24},{20,28},{24,16},{28,20},{1,9},{5... | collective-permute-start | bytes 491528 | tf_op jit(solution)/shard_map/ppermute | solution.py:366
  31.8 0.3 collective-permute-start.10
  32.0 3.1 %collective-permute-start.11 = (f32[264,128]{1,0:T(8,128)S(1)}, f32[264,128]{1,0:T(8,128)S(1)}, u32[]{:S(2)}, u32[]{:S(2)}) collective-permute-start(f32[264,128]{1,0:T(8,128)S(1)} %cross_part.4.refs_0_), channel_id=1, source_target_pairs={{0,3},{1,2},{2,1},{3,0},{4,7},{5,6},{6,5},{7,4},{8,11},{9,10},{10,... | collective-permute-start | bytes 405512 | tf_op jit(solution)/shard_map/ppermute | solution.py:366
  35.1 0.9 %tapers.1.taper_ref = f32[256,128]{1,0:T(8,128)S(1)} custom-call(s32[1,128]{1,0:T(1,128)} %bitcast.13.obs_ref, s32[2,2048]{1,0:T(2,128)S(1)} %copy-done), custom_call_target="tpu_custom_call" | custom-call | tf_op jit(solution)/shard_map/tapers/pallas_call | solution.py:219
  36.1 4.6 %collective-permute-done.11.refs_3_ = f32[264,128]{1,0:T(8,128)S(1)} collective-permute-done((f32[264,128]{1,0:T(8,128)S(1)}, f32[264,128]{1,0:T(8,128)S(1)}, u32[]{:S(2)}, u32[]{:S(2)}) %collective-permute-start.11) | collective-permute-done | bytes 135200 | tf_op jit(solution)/shard_map/ppermute | solution.py:366
  40.7 2.3 %final.1 = f32[256,1280]{1,0:T(8,128)} custom-call(f32[4]{0:T(128)S(1)} %copy-done.12, f32[256,128]{1,0:T(8,128)S(1)} %tapers.1.taper_ref, f32[32,256]{1,0:T(8,128)S(1)} %get-tuple-element.316, f32[264,128]{1,0:T(8,128)S(1)} %cross_part.4.refs_0_, f32[264,128]{1,0:T(8,128)S(1)} %collective-permute-done.9.refs_1_, ...), custom_call_target="tpu_custom_call" | custom-call | flops 1 | bytes 1 | tf_op jit(solution)/shard_map/final/pallas_call | solution.py:347
  (25 shorter events, 0.1 us)
Async XLA Ops:
  0.0 5.2 %copy-start.1 = (f32[256,1280]{1,0:T(8,128)S(1)}, f32[256,1280]{1,0:T(8,128)}, u32[]{:S(2)}) copy-start(f32[256,1280]{1,0:T(8,128)} %state_ref.2) | copy-start | bytes 3932164
  0.0 5.2 %copy-start.13 = (s32[1280]{0:T(1024)S(1)}, s32[1280]{0:T(1024)}, u32[]{:S(2)}) copy-start(s32[1280]{0:T(1024)} %param.9) | copy-start | bytes 15364
  2.5 6.9 %collective-permute-start = (f32[48,1280]{1,0:T(8,128)S(1)}, f32[48,1280]{1,0:T(8,128)S(1)}, u32[]{:S(2)}, u32[]{:S(2)}) collective-permute-start(f32[48,1280]{1,0:T(8,128)S(1)} %get-tuple-element.90), channel_id=1, source_target_pairs={{0,4},{4,0},{8,12},{12,8},{16,20},{20,16},{24,28},{28,24},{1,5},{5... | collective-permute-start | bytes 737288 | tf_op jit(solution)/shard_map/ppermute | solution.py:366
  3.8 10.7 %collective-permute-start.3 = (f32[32,1280]{1,0:T(8,128)S(1)}, f32[32,1280]{1,0:T(8,128)S(1)}, u32[]{:S(2)}, u32[]{:S(2)}) collective-permute-start(f32[32,1280]{1,0:T(8,128)S(1)} %get-tuple-element.80.refs_0_), channel_id=1, source_target_pairs={{0,8},{4,12},{8,0},{12,4},{16,24},{20,28},{24,16},{28,20},{1,9},{5... | collective-permute-start | bytes 491528 | tf_op jit(solution)/shard_map/ppermute | solution.py:366
  5.1 10.8 %collective-permute-start.5 = (f32[32,1280]{1,0:T(8,128)S(1)}, f32[32,1280]{1,0:T(8,128)S(1)}, u32[]{:S(2)}, u32[]{:S(2)}) collective-permute-start(f32[32,1280]{1,0:T(8,128)S(1)} %get-tuple-element.80.refs_0_), channel_id=1, source_target_pairs={{0,16},{4,20},{8,24},{12,28},{16,0},{20,4},{24,8},{28,12},{1,17},{... | collective-permute-start | bytes 491528 | tf_op jit(solution)/shard_map/ppermute | solution.py:366
  5.2 10.7 %copy-start.6 = (s32[1,1280]{1,0:T(1,128)}, s32[1,1280]{1,0:T(1,128)S(1)}, u32[]{:S(2)}) copy-start(s32[1,1280]{1,0:T(1,128)S(1)} %broadcast_in_dim.12.level_ref) | copy-start | bytes 15364
  9.4 2.4 %collective-permute-start.1 = (f32[8,256]{1,0:T(8,128)S(1)}, f32[8,256]{1,0:T(8,128)S(1)}, u32[]{:S(2)}, u32[]{:S(2)}) collective-permute-start(f32[8,256]{1,0:T(8,128)S(1)} %get-tuple-element.91), channel_id=1, source_target_pairs={{0,1},{1,0},{2,3},{3,2},{4,5},{5,4},{6,7},{7,6},{8,9},{9,8},{10,11... | collective-permute-start | bytes 24584 | tf_op jit(solution)/shard_map/ppermute | solution.py:366
  11.8 5.6 %collective-permute-start.2 = (f32[16,256]{1,0:T(8,128)S(1)}, f32[16,256]{1,0:T(8,128)S(1)}, u32[]{:S(2)}, u32[]{:S(2)}) collective-permute-start(f32[16,256]{1,0:T(8,128)S(1)} %get-tuple-element.129), channel_id=1, source_target_pairs={{0,2},{1,3},{2,0},{3,1},{4,6},{5,7},{6,4},{7,5},{8,10},{9,11},{10,... | collective-permute-start | bytes 49160 | tf_op jit(solution)/shard_map/ppermute | solution.py:366
  14.5 6.4 %collective-permute-start.4 = (f32[32,1280]{1,0:T(8,128)S(1)}, f32[32,1280]{1,0:T(8,128)S(1)}, u32[]{:S(2)}, u32[]{:S(2)}) collective-permute-start(f32[32,1280]{1,0:T(8,128)S(1)} %collective-permute-done.3.refs_1_), channel_id=1, source_target_pairs={{0,4},{4,0},{8,12},{12,8},{16,20},{20,16},{24,28},{28,24},{1,5},{5... | collective-permute-start | bytes 491528 | tf_op jit(solution)/shard_map/ppermute | solution.py:366
  15.9 4.8 %collective-permute-start.6 = (f32[32,1280]{1,0:T(8,128)S(1)}, f32[32,1280]{1,0:T(8,128)S(1)}, u32[]{:S(2)}, u32[]{:S(2)}) collective-permute-start(f32[32,1280]{1,0:T(8,128)S(1)} %collective-permute-done.5.refs_0_), channel_id=1, source_target_pairs={{0,8},{4,12},{8,0},{12,4},{16,24},{20,28},{24,16},{28,20},{1,9},{5... | collective-permute-start | bytes 491528 | tf_op jit(solution)/shard_map/ppermute | solution.py:366
  17.2 7.4 %collective-permute-start.7 = (f32[32,1280]{1,0:T(8,128)S(1)}, f32[32,1280]{1,0:T(8,128)S(1)}, u32[]{:S(2)}, u32[]{:S(2)}) collective-permute-start(f32[32,1280]{1,0:T(8,128)S(1)} %collective-permute-done.5.refs_0_), channel_id=1, source_target_pairs={{0,4},{4,0},{8,12},{12,8},{16,20},{20,16},{24,28},{28,24},{1,5},{5... | collective-permute-start | bytes 491528 | tf_op jit(solution)/shard_map/ppermute | solution.py:366
  18.0 8.5 %copy-start.8 = (s32[1,1280]{1,0:T(1,128)S(1)}, s32[1,1280]{1,0:T(1,128)}, u32[]{:S(2)}) copy-start(s32[1,1280]{1,0:T(1,128)} %get-tuple-element.317) | copy-start | bytes 15364
  18.0 8.5 %copy-start.10 = (s32[8,128]{1,0:T(8,128)S(1)}, s32[8,128]{1,0:T(8,128)}, u32[]{:S(2)}) copy-start(s32[8,128]{1,0:T(8,128)} %get-tuple-element.318) | copy-start | bytes 12292
  18.0 8.5 %copy-start.12 = (f32[4]{0:T(128)S(1)}, f32[4]{0:T(128)}, u32[]{:S(2)}) copy-start(f32[4]{0:T(128)} %get-tuple-element.319) | copy-start | bytes 52
  20.7 5.8 %collective-permute-start.8 = (f32[32,1280]{1,0:T(8,128)S(1)}, f32[32,1280]{1,0:T(8,128)S(1)}, u32[]{:S(2)}, u32[]{:S(2)}) collective-permute-start(f32[32,1280]{1,0:T(8,128)S(1)} %collective-permute-done.6.refs_1_), channel_id=1, source_target_pairs={{0,4},{4,0},{8,12},{12,8},{16,20},{20,16},{24,28},{28,24},{1,5},{5... | collective-permute-start | bytes 491528 | tf_op jit(solution)/shard_map/ppermute | solution.py:366
  20.9 7.5 %collective-permute-start.13 = (f32[32,1280]{1,0:T(8,128)S(1)}, f32[32,1280]{1,0:T(8,128)S(1)}, u32[]{:S(2)}, u32[]{:S(2)}) collective-permute-start(f32[32,1280]{1,0:T(8,128)S(1)} %pairs.1.refs_4_), channel_id=1, source_target_pairs={{0,16},{4,20},{8,24},{12,28},{16,0},{20,4},{24,8},{28,12},{1,17},{... | collective-permute-start | bytes 491528 | tf_op jit(solution)/shard_map/ppermute | solution.py:366
  23.2 11.9 %copy-start = (s32[2,2048]{1,0:T(2,128)S(1)}, s32[2,2048]{1,0:T(2,128)}, u32[]{:S(2)}) copy-start(s32[2,2048]{1,0:T(2,128)} %coords_ref.1) | copy-start | bytes 49156
  23.2 12.8 %collective-permute-start.12 = (f32[32,1280]{1,0:T(8,128)S(1)}, f32[32,1280]{1,0:T(8,128)S(1)}, u32[]{:S(2)}, u32[]{:S(2)}) collective-permute-start(f32[32,1280]{1,0:T(8,128)S(1)} %pairs.1.refs_4_), channel_id=1, source_target_pairs={{0,8},{4,12},{8,0},{12,4},{16,24},{20,28},{24,16},{28,20},{1,9},{5... | collective-permute-start | bytes 491528 | tf_op jit(solution)/shard_map/ppermute | solution.py:366
  28.4 12.3 %collective-permute-start.14 = (f32[32,1280]{1,0:T(8,128)S(1)}, f32[32,1280]{1,0:T(8,128)S(1)}, u32[]{:S(2)}, u32[]{:S(2)}) collective-permute-start(f32[32,1280]{1,0:T(8,128)S(1)} %collective-permute-done.13.refs_6_), channel_id=1, source_target_pairs={{0,8},{4,12},{8,0},{12,4},{16,24},{20,28},{24,16},{28,20},{1,9},{5... | collective-permute-start | bytes 491528 | tf_op jit(solution)/shard_map/ppermute | solution.py:366
  31.8 4.3 %collective-permute-start.10 = (f32[264,128]{1,0:T(8,128)S(1)}, f32[264,128]{1,0:T(8,128)S(1)}, u32[]{:S(2)}, u32[]{:S(2)}) collective-permute-start(f32[264,128]{1,0:T(8,128)S(1)} %cross_part.4.refs_0_), channel_id=1, source_target_pairs={{0,2},{1,3},{2,0},{3,1},{4,6},{5,7},{6,4},{7,5},{8,10},{9,11},{10,... | collective-permute-start | bytes 405512 | tf_op jit(solution)/shard_map/ppermute | solution.py:366
  32.0 8.6 %collective-permute-start.11 = (f32[264,128]{1,0:T(8,128)S(1)}, f32[264,128]{1,0:T(8,128)S(1)}, u32[]{:S(2)}, u32[]{:S(2)}) collective-permute-start(f32[264,128]{1,0:T(8,128)S(1)} %cross_part.4.refs_0_), channel_id=1, source_target_pairs={{0,3},{1,2},{2,1},{3,0},{4,7},{5,6},{6,5},{7,4},{8,11},{9,10},{10,... | collective-permute-start | bytes 405512 | tf_op jit(solution)/shard_map/ppermute | solution.py:366
  35.1 5.5 %collective-permute-start.9 = (f32[264,128]{1,0:T(8,128)S(1)}, f32[264,128]{1,0:T(8,128)S(1)}, u32[]{:S(2)}, u32[]{:S(2)}) collective-permute-start(f32[264,128]{1,0:T(8,128)S(1)} %cross_part.4.refs_0_), channel_id=1, source_target_pairs={{0,1},{1,0},{2,3},{3,2},{4,5},{5,4},{6,7},{7,6},{8,9},{9,8},{10,11... | collective-permute-start | bytes 405512 | tf_op jit(solution)/shard_map/ppermute | solution.py:366

commit v4 on v3

--- a/solution.py
+++ b/solution.py
@@ -34,6 +34,16 @@
     return pieces
 
 
+def packing(slots, members):
+    lanes = members // 128
+    full = slots - slots % SUB
+    pieces = [(n * full, full, 0, n * 128) for n in range(lanes)] if full else []
+    tail = slots - full
+    if tail:
+        pieces += [(lanes * full + n * tail, tail, full, n * 128) for n in range(lanes)]
+    return pieces
+
+
 def level_onehot(level_row):
     levels = lax.broadcasted_iota(jnp.int32, (SUB, level_row.shape[1]), 0)
     return (level_row == levels).astype(F32)
@@ -46,14 +56,12 @@
     return picked
 
 
-def pick_kernel(obs_ref, skip_ref, weights_ref, state_ref, out_ref, both_ref, list_ref, held_ref, sem):
-    rows = state_ref.shape[0]
-    slots, members = out_ref.shape
+def pick_kernel(slots, obs_ref, skip_ref, state_ref, out_ref, list_ref, held_ref, row_ref, sem):
+    rows, members = state_ref.shape
     row_first = lax.axis_index("rows") * rows
     skip = skip_ref[0]
     copy = pltpu.make_async_copy(state_ref, held_ref, sem)
     copy.start()
-    both_ref[slots:, :] = weights_ref[...]
 
     def visit(j, rank):
         row = obs_ref[j] - row_first
@@ -67,34 +75,58 @@
     for slot in range(slots):
         row = jnp.clip(list_ref[skip + slot], 0, rows - 1)
         value = jnp.where(slot < held, held_ref[pl.ds(row, 1), :], 0.0)
-        out_ref[slot : slot + 1, :] = value
-        both_ref[slot : slot + 1, :] = value
-
-
-def pick(obs_row, skip, weights, state, slots):
-    members = state.shape[1]
+        row_ref[slot : slot + 1, :] = value
+    for at, tall, row, lane in packing(slots, members):
+        out_ref[at : at + tall, :] = row_ref[row : row + tall, lane : lane + 128]
+
+
+def pick(obs_row, skip, state, slots):
     smem = pl.BlockSpec(memory_space=pltpu.SMEM)
-    vmem = pl.BlockSpec(memory_space=pltpu.VMEM)
-    return pl.pallas_call(
-        pick_kernel,
-        out_shape=(
-            jax.ShapeDtypeStruct((slots, members), F32),
-            jax.ShapeDtypeStruct((slots + weights.shape[0], members), F32),
-        ),
-        in_specs=[smem, smem, vmem, pl.BlockSpec(memory_space=pl.ANY)],
-        out_specs=(vmem, vmem),
+    return pl.pallas_call(
+        functools.partial(pick_kernel, slots),
+        out_shape=jax.ShapeDtypeStruct((slots * (state.shape[1] // 128), 128), F32),
+        in_specs=[smem, smem, pl.BlockSpec(memory_space=pl.ANY)],
+        out_specs=pl.BlockSpec(memory_space=pltpu.VMEM),
         scratch_shapes=[
             pltpu.SMEM((obs_row.shape[0] + slots + 1,), jnp.int32),
             pltpu.VMEM(state.shape, F32),
+            pltpu.VMEM((-(-slots // SUB) * SUB, state.shape[1]), F32),
             pltpu.SemaphoreType.DMA(()),
         ],
         compiler_params=pltpu.CompilerParams(vmem_limit_bytes=VMEM_LIMIT),
         cost_estimate=COST,
         name="pick",
-    )(obs_row, skip, weights, state)
-
-
-def center_kernel(level_ref, state_ref, sums_ref, high_ref, low_ref):
+    )(obs_row, skip, state)
+
+
+def place(slots, rows, obs_ref, place_ref, rounds_ref):
+    observed = obs_ref.shape[1]
+    owner = lax.div(obs_ref[...], jnp.int32(rows))
+    owner_row = owner.astype(F32)
+    owner_down = jnp.transpose(jnp.broadcast_to(owner_row, (SUB, observed)))[:, 0:1]
+    j_down = lax.broadcasted_iota(jnp.int32, (observed, observed), 0)
+    j_row = lax.broadcasted_iota(jnp.int32, (observed, observed), 1)
+    earlier = (owner_down == owner_row) & (j_down < j_row)
+    rank = jnp.sum(earlier.astype(F32), axis=0, keepdims=True).astype(jnp.int32)
+    place_ref[0:1, :] = owner
+    place_ref[1:2, :] = rank
+    place_ref[2:SUB, :] = jnp.zeros((SUB - 2, observed), jnp.int32)
+    rounds_ref[0] = lax.div(jnp.max(rank), jnp.int32(slots)) + 1
+
+
+def center_kernel(
+    slots, rows, obs_ref, own_ref, weights_ref, level_ref, state_ref, sums_ref, high_ref, low_ref,
+    both_ref, place_ref, zero_ref, rounds_ref,
+):
+    @pl.when(pl.program_id(0) == 0)
+    def _():
+        held, (length, members) = own_ref.shape[0], weights_ref.shape
+        both_ref[0:held, :] = own_ref[...]
+        for at, tall, row, lane in packing(length, members):
+            both_ref[held + at : held + at + tall, :] = weights_ref[row : row + tall, lane : lane + 128]
+        place(slots, rows, obs_ref, place_ref, rounds_ref)
+        zero_ref[...] = jnp.zeros_like(zero_ref)
+
     level_row = level_ref[...]
     onehot = level_onehot(level_row)
     counts = jnp.sum(onehot, axis=1, keepdims=True)
@@ -110,36 +142,54 @@
     low_ref[...] = low
 
 
-def center(level_row, state):
+def center(obs_row, own, weights, level_row, state):
     rows, members = state.shape
+    observed = obs_row.shape[0]
+    slots = own.shape[0] // (members // 128)
     tall = math.gcd(rows, 128)
-    return pl.pallas_call(
-        center_kernel,
+    whole = lambda *shape: pl.BlockSpec(shape, lambda i: (0, 0))
+    both = (own.shape[0] + weights.shape[0] * (members // 128), 128)
+    return pl.pallas_call(
+        functools.partial(center_kernel, slots, rows),
         out_shape=(
             jax.ShapeDtypeStruct((SUB, rows), F32),
             jax.ShapeDtypeStruct((rows, members), BF16),
             jax.ShapeDtypeStruct((rows, members), BF16),
+            jax.ShapeDtypeStruct(both, F32),
+            jax.ShapeDtypeStruct((SUB, observed), jnp.int32),
+            jax.ShapeDtypeStruct((rows + SUB, observed), F32),
+            jax.ShapeDtypeStruct((1,), jnp.int32),
         ),
         grid=(rows // tall,),
         in_specs=[
-            pl.BlockSpec((1, members), lambda i: (0, 0)),
+            whole(1, observed),
+            whole(*own.shape),
+            whole(*weights.shape),
+            whole(1, members),
             pl.BlockSpec((tall, members), lambda i: (i, 0)),
         ],
         out_specs=(
             pl.BlockSpec((SUB, tall), lambda i: (0, i)),
             pl.BlockSpec((tall, members), lambda i: (i, 0)),
             pl.BlockSpec((tall, members), lambda i: (i, 0)),
+            whole(*both),
+            whole(SUB, observed),
+            whole(rows + SUB, observed),
+            pl.BlockSpec(memory_space=pltpu.SMEM),
         ),
         compiler_params=pltpu.CompilerParams(vmem_limit_bytes=VMEM_LIMIT),
         cost_estimate=COST,
         name="center",
-    )(level_row, state)
+    )(obs_row[None, :], own, weights, level_row, state)
 
 
 def pair_kernel(near_ref, far_ref, pair_ref):
     length = near_ref.shape[0]
     pair_ref[0:length, :] = near_ref[...]
-    pair_ref[length : 2 * length, :] = far_ref[far_ref.shape[0] - length :, :]
+    members = near_ref.shape[1]
+    held = far_ref.shape[0] - length * (members // 128)
+    for at, tall, row, lane in packing(length, members):
+        pair_ref[length + row : length + row + tall, lane : lane + 128] = far_ref[held + at : held + at + tall, :]
 
 
 def pairs(near, far):
@@ -154,40 +204,6 @@
         cost_estimate=COST,
         name="pairs",
     )(near, far)
-
-
-def place_kernel(slots, rows, obs_ref, place_ref, rounds_ref, zero_ref):
-    observed = obs_ref.shape[1]
-    zero_ref[...] = jnp.zeros_like(zero_ref)
-    owner = lax.div(obs_ref[...], jnp.int32(rows))
-    owner_row = owner.astype(F32)
-    owner_down = jnp.transpose(jnp.broadcast_to(owner_row, (SUB, observed)))[:, 0:1]
-    j_down = lax.broadcasted_iota(jnp.int32, (observed, observed), 0)
-    j_row = lax.broadcasted_iota(jnp.int32, (observed, observed), 1)
-    earlier = (owner_down == owner_row) & (j_down < j_row)
-    rank = jnp.sum(earlier.astype(F32), axis=0, keepdims=True).astype(jnp.int32)
-    place_ref[0:1, :] = owner
-    place_ref[1:2, :] = rank
-    place_ref[2:SUB, :] = jnp.zeros((SUB - 2, observed), jnp.int32)
-    rounds_ref[0] = lax.div(jnp.max(rank), jnp.int32(slots)) + 1
-
-
-def places(obs_row, rows, slots):
-    observed = obs_row.shape[0]
-    vmem = pl.BlockSpec(memory_space=pltpu.VMEM)
-    smem = pl.BlockSpec(memory_space=pltpu.SMEM)
-    return pl.pallas_call(
-        functools.partial(place_kernel, slots, rows),
-        out_shape=(
-            jax.ShapeDtypeStruct((SUB, observed), jnp.int32),
-            jax.ShapeDtypeStruct((1,), jnp.int32),
-            jax.ShapeDtypeStruct((rows + SUB, observed), F32),
-        ),
-        in_specs=[vmem],
-        out_specs=(vmem, smem, vmem),
-        compiler_params=pltpu.CompilerParams(vmem_limit_bytes=VMEM_LIMIT),
-        name="places",
-    )(obs_row[None, :])
 
 
 def taper_kernel(radius, obs_ref, coords_ref, taper_ref):
@@ -227,7 +243,7 @@
 
 
 def cross_kernel(number, slots, weight_ref, skip_ref, level_ref, place_ref, high_ref, low_ref, before_ref, *refs):
-    blocks, (sums_ref, out_ref, o_high, o_low, p_ref, m_ref) = refs[: len(number)], refs[len(number) :]
+    blocks, (sums_ref, out_ref, o_high, o_low, p_ref, m_ref, raw_ref) = refs[: len(number)], refs[len(number) :]
     rows = high_ref.shape[0]
     me = lax.axis_index("rows")
     skip = skip_ref[0]
@@ -244,18 +260,21 @@
     m_ref[...] = jnp.zeros_like(m_ref)
     for n, block_ref in enumerate(blocks):
         at = n * padded
-        block = block_ref[0:slots, :]
+        raw_ref[at + padded - SUB : at + padded, :] = jnp.zeros((SUB, raw_ref.shape[1]), F32)
+        for start, tall, row, lane in packing(slots, raw_ref.shape[1]):
+            raw_ref[at + row : at + row + tall, lane : lane + 128] = block_ref[start : start + tall, :]
+        block = raw_ref[at : at + padded, :]
         columns = []
         for level in range(LEVELS):
             member = jnp.where(level_row == level, block, 0.0)
             columns.append(jnp.sum(member, axis=1, keepdims=True) / counts[level : level + 1, :])
-            m_ref[at : at + slots, level : level + 1] = columns[level]
+            m_ref[at : at + padded, level : level + 1] = columns[level]
         high, low = split((block - by_level(level_row, columns)) * member_scale, 2)
-        o_high[at : at + slots, :] = high
-        o_low[at : at + slots, :] = low
-        slot = lax.broadcasted_iota(jnp.int32, (slots, owner.shape[1]), 0)
-        hit = (owner == (me ^ number[n])) & (rank - skip == slot)
-        p_ref[at : at + slots, :] = hit.astype(BF16)
+        o_high[at : at + padded, :] = high
+        o_low[at : at + padded, :] = low
+        slot = lax.broadcasted_iota(jnp.int32, (padded, owner.shape[1]), 0)
+        hit = (owner == (me ^ number[n])) & (rank - skip == slot) & (slot < slots)
+        p_ref[at : at + padded, :] = hit.astype(BF16)
     by_slot = dot(high_ref[...], o_high[...], LANES_BOTH)
     by_slot += dot(high_ref[...], o_low[...], LANES_BOTH)
     by_slot += dot(low_ref[...], o_high[...], LANES_BOTH)
@@ -270,7 +289,7 @@
     rows, members = high.shape
     smem = pl.BlockSpec(memory_space=pltpu.SMEM)
     vmem = pl.BlockSpec(memory_space=pltpu.VMEM)
-    held = len(number) * slots
+    held = len(number) * -(-slots // 16) * 16
     return pl.pallas_call(
         functools.partial(cross_kernel, number, slots),
         out_shape=jax.ShapeDtypeStruct(before.shape, F32),
@@ -281,6 +300,7 @@
             pltpu.VMEM((held, members), BF16),
             pltpu.VMEM((held, before.shape[1]), BF16),
             pltpu.VMEM((held, SUB), F32),
+            pltpu.VMEM((held, members), F32),
         ],
         compiler_params=pltpu.CompilerParams(vmem_limit_bytes=VMEM_LIMIT),
         cost_estimate=COST,
@@ -384,30 +404,29 @@
     row_count = state.shape[0]
     observed = obs_row.shape[0]
     bits = [1 << n for n in range(groups.bit_length() - 2, 0, -1)]
-    slots = min(observed, 16 * (-(-2 * observed // groups) // 16))
+    mean = -(-observed // groups)
+    slots = min(observed, 4 * math.ceil((mean + 3 * math.sqrt(mean)) / 4))
+    if slots % SUB * (state.shape[1] // 128) % SUB:
+        slots += SUB - slots % SUB
 
     none = jnp.zeros((1,), jnp.int32)
-    own, own_both = pick(obs_row, none, weights, state, slots)
+    own = pick(obs_row, none, state, slots)
+    first_far = across(own, "rows", bits[0])
     level_row = after(member_level, own)[None, :]
-    sums, high, low = center(level_row, after(state, own))
-    near_far = across(own_both, "rows", 1)
-    near_sums = after(sums, near_far)
-    near_sums = jnp.concatenate([near_sums, across(near_sums, "mem", 1)])
-    place, rounds, empty = places(after(obs_row, own), row_count, slots)
-    first_far = across(own, "rows", bits[0])
-    line = gather_line(own, bits[1:])
-    line |= {
-        b ^ bits[0]: x for b, x in gather_line(after(first_far, near_sums, place), bits[1:]).items()
-    }
-    forward = {b: x for b, x in line.items()}
-    other = {b ^ 1: across(x, "rows", 1) if b else near_far for b, x in forward.items()}
-    all_sums = near_sums
-    for n in range(1, lax.axis_size("mem").bit_length() - 1):
+    sums, high, low, own_both, place, empty, rounds = center(
+        after(obs_row, own), own, weights, level_row, after(state, own)
+    )
+    all_sums = sums
+    for n in range(lax.axis_size("mem").bit_length() - 1):
         all_sums = jnp.concatenate([all_sums, across(all_sums, "mem", 1 << n)])
+
+    line = gather_line(after(own, sums), bits[1:])
+    line |= {b ^ bits[0]: x for b, x in gather_line(first_far, bits[1:]).items()}
+    forward = line | {0: own_both}
+    other = {b ^ 1: across(x, "rows", 1) for b, x in forward.items()}
     blocks = line | other
     early = [b for b in blocks if b < bits[0]]
     late = [b for b in blocks if b >= bits[0]]
-
     weights_pair = pairs(weights, after(other[1], all_sums))
 
     def cross(skip, part, high, low, held, number):
@@ -420,9 +439,11 @@
         turn, part = carry
         skip = (turn * slots)[None]
         again = after(state, turn)
-        block, _ = pick(obs_row, skip, weights, again, slots)
-        _, high, low = center(level_row, again)
-        parcels = [lax.all_gather(x, "rows", axis=0) for x in jnp.split(block, slots // 16)]
+        block = pick(obs_row, skip, again, slots)
+        _, high, low, *_ = center(obs_row, block, weights, level_row, again)
+        parcels = [
+            lax.all_gather(block[at : at + 64], "rows", axis=0) for at in range(0, block.shape[0], 64)
+        ]
         every = jnp.concatenate(parcels, axis=1)
         me = lax.axis_index("rows")
         part = cross(skip, part, high, low, [every[me ^ b] for b in early + late], early + late)

time: 43.2 us -> 41.5 us (0.961)
  the two profiles are of different devices: /device:TPU:17 before, /device:TPU:0 now
where the time goes in v4:
time: 41.5 us; the launch traced here: 41.4 us
  starting transfers between devices  16 us (39%)
  waiting for transfers between devices  14 us (34%)
  Pallas kernels  10.6 us (26%)
  loops' own time  0.68 us (2%)
    ppermute x15, starting transfers between devices, across(): return lax.ppermute(x, axis, [(i, i ^ bits) for i in range(count)])  16 us
    ppermute x15, waiting for transfers between devices, across(): return lax.ppermute(x, axis, [(i, i ^ bits) for i in range(count)])  14 us
    pallas_call x2, Pallas kernels, cross_part(): pl.pallas_call(functools.partial(cross_kernel, number, slots), out_shape=...  3.82 us
    pallas_call x1, Pallas kernels, final(): pl.pallas_call(functools.partial(final_kernel, number, len(parts), width)...  2.3 us
    pallas_call x1, Pallas kernels, pick(): pl.pallas_call(functools.partial(pick_kernel, slots), out_shape=jax.Shape...  2.24 us
    pallas_call x1, Pallas kernels, center(): pl.pallas_call(functools.partial(center_kernel, slots, rows), out_shape=(...  1.9 us
  transfers between devices with their start and end apart: 15, of which 7 were waited for; matrix products, arithmetic and copies ran while one was open for 0% of the time, Pallas kernels for 15%

profile of v4, /device:TPU:0, one launch (start us, length us, event | category | flops | bytes accessed | tf_op | source)
XLA Modules:
  0.0 41.4 jit_solution(931056460098311496)
XLA Ops:
  0.0 2.2 %pick.2.own_ref.refs_0_ = f32[280,128]{1,0:T(8,128)S(1)} custom-call(s32[128]{0:T(128)} %obs_ref.1, s32[1]{0:T(128)} %constant.28.clone.1.skip_ref, f32[256,1280]{1,0:T(8,128)} %state_ref.2), custom_call_target="tpu_custom_call" | custom-call | flops 1 | bytes 1 | tf_op jit(solution)/shard_map/pick/pallas_call | solution.py:85
  2.3 0.0 copy-start.5
  2.3 4.1 %collective-permute-start.5 = (f32[280,128]{1,0:T(8,128)S(1)}, f32[280,128]{1,0:T(8,128)S(1)}, u32[]{:S(2)}, u32[]{:S(2)}) collective-permute-start(f32[280,128]{1,0:T(8,128)S(1)} %pick.2.own_ref.refs_0_), channel_id=1, source_target_pairs={{0,16},{4,20},{8,24},{12,28},{16,0},{20,4},{24,8},{28,12},{1,17},{... | collective-permute-start | bytes 430088 | tf_op jit(solution)/shard_map/ppermute | solution.py:386
  6.4 1.9 %center.2 = (f32[8,256]{1,0:T(8,128)S(1)}, bf16[256,1280]{1,0:T(8,128)(2,1)S(1)}, bf16[256,1280]{1,0:T(8,128)(2,1)S(1)}, f32[440,128]{1,0:T(8,128)S(1)}, s32[8,1...) custom-call(s32[1,128]{1,0:T(1,128)S(1)} %bitcast.48, f32[280,128]{1,0:T(8,128)S(1)} %pick.2.own_ref.refs_0_, ...), custom_call_target="tpu_custom_call" | custom-call | flops 1 | bytes 1 | tf_op jit(solution)/shard_map/center/pallas_call | solution.py:152
  8.3 0.1 collective-permute-start
  8.4 1.6 %collective-permute-start.3 = (f32[440,128]{1,0:T(8,128)S(1)}, f32[440,128]{1,0:T(8,128)S(1)}, u32[]{:S(2)}, u32[]{:S(2)}) collective-permute-start(f32[440,128]{1,0:T(8,128)S(1)} %get-tuple-element.88), channel_id=1, source_target_pairs={{0,4},{4,0},{8,12},{12,8},{16,20},{20,16},{24,28},{28,24},{1,5},{5... | collective-permute-start | bytes 675848 | tf_op jit(solution)/shard_map/ppermute | solution.py:386
  10.0 1.6 %collective-permute-start.2 = (f32[280,128]{1,0:T(8,128)S(1)}, f32[280,128]{1,0:T(8,128)S(1)}, u32[]{:S(2)}, u32[]{:S(2)}) collective-permute-start(f32[280,128]{1,0:T(8,128)S(1)} %pick.2.own_ref.refs_0_), channel_id=1, source_target_pairs={{0,8},{4,12},{8,0},{12,4},{16,24},{20,28},{24,16},{28,20},{1,9},{5... | collective-permute-start | bytes 430088 | tf_op jit(solution)/shard_map/ppermute | solution.py:386
  11.6 0.0 collective-permute-done
  11.6 1.6 %collective-permute-start.1 = (f32[16,256]{1,0:T(8,128)S(1)}, f32[16,256]{1,0:T(8,128)S(1)}, u32[]{:S(2)}, u32[]{:S(2)}) collective-permute-start(f32[16,256]{1,0:T(8,128)S(1)} %pad_maximum_fusion), channel_id=1, source_target_pairs={{0,2},{1,3},{2,0},{3,1},{4,6},{5,7},{6,4},{7,5},{8,10},{9,11},{10,... | collective-permute-start | bytes 49160 | tf_op jit(solution)/shard_map/ppermute | solution.py:386
  13.1 2.2 %collective-permute-done.1 = f32[16,256]{1,0:T(8,128)S(1)} collective-permute-done((f32[16,256]{1,0:T(8,128)S(1)}, f32[16,256]{1,0:T(8,128)S(1)}, u32[]{:S(2)}, u32[]{:S(2)}) %collective-permute-start.1) | collective-permute-done | bytes 16416 | tf_op jit(solution)/shard_map/ppermute | solution.py:386
  15.4 0.0 collective-permute-done.5.refs_0_
  15.4 0.5 %collective-permute-start.6 = (f32[280,128]{1,0:T(8,128)S(1)}, f32[280,128]{1,0:T(8,128)S(1)}, u32[]{:S(2)}, u32[]{:S(2)}) collective-permute-start(f32[280,128]{1,0:T(8,128)S(1)} %collective-permute-done.5.refs_0_), channel_id=1, source_target_pairs={{0,8},{4,12},{8,0},{12,4},{16,24},{20,28},{24,16},{28,20},{1,9},{5... | collective-permute-start | bytes 430088 | tf_op jit(solution)/shard_map/ppermute | solution.py:386
  15.8 0.7 %while.10 = (s32[]{:T(128)}, f32[264,128]{1,0:T(8,128)S(1)}, s32[1]{0:T(128)}, s32[128]{0:T(128)S(1)}, f32[256,1280]{1,0:T(8,128)}, /*index=5*/f32[16,1280]{1,0:...) while((s32[]{:T(128)}, f32[264,128]{1,0:T(8,128)S(1)}, ...), condition=%wide.region_1.0_spmd, body=%wide.region_0.0_spmd.sunk | while | flops 40 | bytes 11678356 | solution.py:452
  16.5 0.0 collective-permute-done.3.refs_2_.far_ref
  16.6 1.7 %collective-permute-start.13 = (f32[32,1280]{1,0:T(8,128)S(1)}, f32[32,1280]{1,0:T(8,128)S(1)}, u32[]{:S(2)}, u32[]{:S(2)}) collective-permute-start(f32[32,1280]{1,0:T(8,128)S(1)} %pairs.1.refs_4_), channel_id=1, source_target_pairs={{0,16},{4,20},{8,24},{12,28},{16,0},{20,4},{24,8},{28,12},{1,17},{... | collective-permute-start | bytes 491528 | tf_op jit(solution)/shard_map/ppermute | solution.py:386
  18.2 1.5 %collective-permute-start.4 = (f32[280,128]{1,0:T(8,128)S(1)}, f32[280,128]{1,0:T(8,128)S(1)}, u32[]{:S(2)}, u32[]{:S(2)}) collective-permute-start(f32[280,128]{1,0:T(8,128)S(1)} %collective-permute-done.2.refs_1_), channel_id=1, source_target_pairs={{0,4},{4,0},{8,12},{12,8},{16,20},{20,16},{24,28},{28,24},{1,5},{5... | collective-permute-start | bytes 430088 | tf_op jit(solution)/shard_map/ppermute | solution.py:386
  19.7 0.5 %collective-permute-start.7 = (f32[280,128]{1,0:T(8,128)S(1)}, f32[280,128]{1,0:T(8,128)S(1)}, u32[]{:S(2)}, u32[]{:S(2)}) collective-permute-start(f32[280,128]{1,0:T(8,128)S(1)} %collective-permute-done.5.refs_0_), channel_id=1, source_target_pairs={{0,4},{4,0},{8,12},{12,8},{16,20},{20,16},{24,28},{28,24},{1,5},{5... | collective-permute-start | bytes 430088 | tf_op jit(solution)/shard_map/ppermute | solution.py:386
  20.3 1.4 %collective-permute-done.6.refs_1_ = f32[280,128]{1,0:T(8,128)S(1)} collective-permute-done((f32[280,128]{1,0:T(8,128)S(1)}, f32[280,128]{1,0:T(8,128)S(1)}, u32[]{:S(2)}, u32[]{:S(2)}) %collective-permute-start.6) | collective-permute-done | bytes 143392 | tf_op jit(solution)/shard_map/ppermute | solution.py:386
  21.7 0.1 collective-permute-start.8
  21.8 3.1 %collective-permute-done.4.refs_3_ = f32[280,128]{1,0:T(8,128)S(1)} collective-permute-done((f32[280,128]{1,0:T(8,128)S(1)}, f32[280,128]{1,0:T(8,128)S(1)}, u32[]{:S(2)}, u32[]{:S(2)}) %collective-permute-start.4) | collective-permute-done | bytes 143392 | tf_op jit(solution)/shard_map/ppermute | solution.py:386
  24.9 1.9 %cross_part.3.before_ref = f32[264,128]{1,0:T(8,128)S(1)} custom-call(f32[4]{0:T(128)S(1)} %get-tuple-element.317, s32[1]{0:T(128)} %constant.28.clone.1.skip_ref, s32[1,1280]{1,0:T(1,128)S(1)} %get-tuple-element.313, s32[8,128]{1,0:T(8,128)S(1)} %get-tuple-element.314, bf16[256,1280]{1,0:T(8,128)(2,1)S(1)} %get-tuple-element.81.high_ref, ...), custom_call_target="tpu_custom_call" | custom-call | flops 1 | bytes 1 | tf_op jit(solution)/shard_map/cross_part/pallas_call | solution.py:293
  26.8 0.4 collective-permute-start.12
  27.2 0.7 %collective-permute-done.7.refs_2_ = f32[280,128]{1,0:T(8,128)S(1)} collective-permute-done((f32[280,128]{1,0:T(8,128)S(1)}, f32[280,128]{1,0:T(8,128)S(1)}, u32[]{:S(2)}, u32[]{:S(2)}) %collective-permute-start.7) | collective-permute-done | bytes 143392 | tf_op jit(solution)/shard_map/ppermute | solution.py:386
  27.9 1.5 %collective-permute-done.8.refs_3_ = f32[280,128]{1,0:T(8,128)S(1)} collective-permute-done((f32[280,128]{1,0:T(8,128)S(1)}, f32[280,128]{1,0:T(8,128)S(1)}, u32[]{:S(2)}, u32[]{:S(2)}) %collective-permute-start.8) | collective-permute-done | bytes 143392 | tf_op jit(solution)/shard_map/ppermute | solution.py:386
  29.4 1.9 %cross_part.4.refs_0_ = f32[264,128]{1,0:T(8,128)S(1)} custom-call(f32[4]{0:T(128)S(1)} %get-tuple-element.317, s32[1]{0:T(128)} %constant.28.clone.1.skip_ref, s32[1,1280]{1,0:T(1,128)S(1)} %get-tuple-element.313, s32[8,128]{1,0:T(8,128)S(1)} %get-tuple-element.314, bf16[256,1280]{1,0:T(8,128)(2,1)S(1)} %get-tuple-element.81.high_ref, ...), custom_call_target="tpu_custom_call" | custom-call | flops 1 | bytes 1 | tf_op jit(solution)/shard_map/cross_part/pallas_call | solution.py:293
  31.3 0.3 collective-permute-start.14
  31.7 1.5 %collective-permute-start.10 = (f32[264,128]{1,0:T(8,128)S(1)}, f32[264,128]{1,0:T(8,128)S(1)}, u32[]{:S(2)}, u32[]{:S(2)}) collective-permute-start(f32[264,128]{1,0:T(8,128)S(1)} %cross_part.4.refs_0_), channel_id=1, source_target_pairs={{0,2},{1,3},{2,0},{3,1},{4,6},{5,7},{6,4},{7,5},{8,10},{9,11},{10,... | collective-permute-start | bytes 405512 | tf_op jit(solution)/shard_map/ppermute | solution.py:386
  33.2 0.6 %collective-permute-start.9 = (f32[264,128]{1,0:T(8,128)S(1)}, f32[264,128]{1,0:T(8,128)S(1)}, u32[]{:S(2)}, u32[]{:S(2)}) collective-permute-start(f32[264,128]{1,0:T(8,128)S(1)} %cross_part.4.refs_0_), channel_id=1, source_target_pairs={{0,1},{1,0},{2,3},{3,2},{4,5},{5,4},{6,7},{7,6},{8,9},{9,8},{10,11... | collective-permute-start | bytes 405512 | tf_op jit(solution)/shard_map/ppermute | solution.py:386
  33.8 0.3 tapers.1.taper_ref
  34.1 3.1 %collective-permute-done.10.refs_2_ = f32[264,128]{1,0:T(8,128)S(1)} collective-permute-done((f32[264,128]{1,0:T(8,128)S(1)}, f32[264,128]{1,0:T(8,128)S(1)}, u32[]{:S(2)}, u32[]{:S(2)}) %collective-permute-start.10) | collective-permute-done | bytes 135200 | tf_op jit(solution)/shard_map/ppermute | solution.py:386
  37.2 1.8 %collective-permute-done.11.refs_3_ = f32[264,128]{1,0:T(8,128)S(1)} collective-permute-done((f32[264,128]{1,0:T(8,128)S(1)}, f32[264,128]{1,0:T(8,128)S(1)}, u32[]{:S(2)}, u32[]{:S(2)}) %collective-permute-start.11) | collective-permute-done | bytes 135200 | tf_op jit(solution)/shard_map/ppermute | solution.py:386
  39.1 2.3 %final.1 = f32[256,1280]{1,0:T(8,128)} custom-call(f32[4]{0:T(128)S(1)} %get-tuple-element.317, f32[256,128]{1,0:T(8,128)S(1)} %tapers.1.taper_ref, f32[32,256]{1,0:T(8,128)S(1)} %get-tuple-element.312, f32[264,128]{1,0:T(8,128)S(1)} %cross_part.4.refs_0_, f32[264,128]{1,0:T(8,128)S(1)} %collective-permute-done.9.refs_1_, ...), custom_call_target="tpu_custom_call" | custom-call | flops 1 | bytes 1 | tf_op jit(solution)/shard_map/final/pallas_call | solution.py:367
  (23 shorter events, 0.1 us)
Async XLA Ops:
  0.0 6.4 %copy-start.4 = (s32[128]{0:T(128)S(1)}, s32[128]{0:T(128)}, u32[]{:S(2)}) copy-start(s32[128]{0:T(128)} %obs_ref.1) | copy-start | bytes 1540
  0.0 6.4 %copy-start.1 = (f32[256,1280]{1,0:T(8,128)S(1)}, f32[256,1280]{1,0:T(8,128)}, u32[]{:S(2)}) copy-start(f32[256,1280]{1,0:T(8,128)} %state_ref.2) | copy-start | bytes 3932164
  0.0 6.4 %copy-start.6 = (s32[1280]{0:T(1024)S(1)}, s32[1280]{0:T(1024)}, u32[]{:S(2)}) copy-start(s32[1280]{0:T(1024)} %param.9) | copy-start | bytes 15364
  0.0 6.4 %copy-start.3 = (f32[16,1280]{1,0:T(8,128)S(1)}, f32[16,1280]{1,0:T(8,128)}, u32[]{:S(2)}) copy-start(f32[16,1280]{1,0:T(8,128)} %near_ref.1) | copy-start | bytes 245764
  2.3 13.6 %copy-start.5 = (f32[4]{0:T(128)S(1)}, f32[4]{0:T(128)}, u32[]{:S(2)}) copy-start(f32[4]{0:T(128)} %weight_ref.5) | copy-start | bytes 52
  2.3 13.1 %collective-permute-start.5 = (f32[280,128]{1,0:T(8,128)S(1)}, f32[280,128]{1,0:T(8,128)S(1)}, u32[]{:S(2)}, u32[]{:S(2)}) collective-permute-start(f32[280,128]{1,0:T(8,128)S(1)} %pick.2.own_ref.refs_0_), channel_id=1, source_target_pairs={{0,16},{4,20},{8,24},{12,28},{16,0},{20,4},{24,8},{28,12},{1,17},{... | collective-permute-start | bytes 430088 | tf_op jit(solution)/shard_map/ppermute | solution.py:386
  8.3 3.2 %collective-permute-start = (f32[8,256]{1,0:T(8,128)S(1)}, f32[8,256]{1,0:T(8,128)S(1)}, u32[]{:S(2)}, u32[]{:S(2)}) collective-permute-start(f32[8,256]{1,0:T(8,128)S(1)} %get-tuple-element.85), channel_id=1, source_target_pairs={{0,1},{1,0},{2,3},{3,2},{4,5},{5,4},{6,7},{7,6},{8,9},{9,8},{10,11... | collective-permute-start | bytes 24584 | tf_op jit(solution)/shard_map/ppermute | solution.py:386
  8.4 8.1 %collective-permute-start.3 = (f32[440,128]{1,0:T(8,128)S(1)}, f32[440,128]{1,0:T(8,128)S(1)}, u32[]{:S(2)}, u32[]{:S(2)}) collective-permute-start(f32[440,128]{1,0:T(8,128)S(1)} %get-tuple-element.88), channel_id=1, source_target_pairs={{0,4},{4,0},{8,12},{12,8},{16,20},{20,16},{24,28},{28,24},{1,5},{5... | collective-permute-start | bytes 675848 | tf_op jit(solution)/shard_map/ppermute | solution.py:386
  10.0 8.2 %collective-permute-start.2 = (f32[280,128]{1,0:T(8,128)S(1)}, f32[280,128]{1,0:T(8,128)S(1)}, u32[]{:S(2)}, u32[]{:S(2)}) collective-permute-start(f32[280,128]{1,0:T(8,128)S(1)} %pick.2.own_ref.refs_0_), channel_id=1, source_target_pairs={{0,8},{4,12},{8,0},{12,4},{16,24},{20,28},{24,16},{28,20},{1,9},{5... | collective-permute-start | bytes 430088 | tf_op jit(solution)/shard_map/ppermute | solution.py:386
  11.6 3.8 %collective-permute-start.1 = (f32[16,256]{1,0:T(8,128)S(1)}, f32[16,256]{1,0:T(8,128)S(1)}, u32[]{:S(2)}, u32[]{:S(2)}) collective-permute-start(f32[16,256]{1,0:T(8,128)S(1)} %pad_maximum_fusion), channel_id=1, source_target_pairs={{0,2},{1,3},{2,0},{3,1},{4,6},{5,7},{6,4},{7,5},{8,10},{9,11},{10,... | collective-permute-start | bytes 49160 | tf_op jit(solution)/shard_map/ppermute | solution.py:386
  15.4 6.3 %collective-permute-start.6 = (f32[280,128]{1,0:T(8,128)S(1)}, f32[280,128]{1,0:T(8,128)S(1)}, u32[]{:S(2)}, u32[]{:S(2)}) collective-permute-start(f32[280,128]{1,0:T(8,128)S(1)} %collective-permute-done.5.refs_0_), channel_id=1, source_target_pairs={{0,8},{4,12},{8,0},{12,4},{16,24},{20,28},{24,16},{28,20},{1,9},{5... | collective-permute-start | bytes 430088 | tf_op jit(solution)/shard_map/ppermute | solution.py:386
  16.6 14.8 %collective-permute-start.13 = (f32[32,1280]{1,0:T(8,128)S(1)}, f32[32,1280]{1,0:T(8,128)S(1)}, u32[]{:S(2)}, u32[]{:S(2)}) collective-permute-start(f32[32,1280]{1,0:T(8,128)S(1)} %pairs.1.refs_4_), channel_id=1, source_target_pairs={{0,16},{4,20},{8,24},{12,28},{16,0},{20,4},{24,8},{28,12},{1,17},{... | collective-permute-start | bytes 491528 | tf_op jit(solution)/shard_map/ppermute | solution.py:386
  18.2 6.7 %collective-permute-start.4 = (f32[280,128]{1,0:T(8,128)S(1)}, f32[280,128]{1,0:T(8,128)S(1)}, u32[]{:S(2)}, u32[]{:S(2)}) collective-permute-start(f32[280,128]{1,0:T(8,128)S(1)} %collective-permute-done.2.refs_1_), channel_id=1, source_target_pairs={{0,4},{4,0},{8,12},{12,8},{16,20},{20,16},{24,28},{28,24},{1,5},{5... | collective-permute-start | bytes 430088 | tf_op jit(solution)/shard_map/ppermute | solution.py:386
  19.7 8.1 %collective-permute-start.7 = (f32[280,128]{1,0:T(8,128)S(1)}, f32[280,128]{1,0:T(8,128)S(1)}, u32[]{:S(2)}, u32[]{:S(2)}) collective-permute-start(f32[280,128]{1,0:T(8,128)S(1)} %collective-permute-done.5.refs_0_), channel_id=1, source_target_pairs={{0,4},{4,0},{8,12},{12,8},{16,20},{20,16},{24,28},{28,24},{1,5},{5... | collective-permute-start | bytes 430088 | tf_op jit(solution)/shard_map/ppermute | solution.py:386
  21.7 7.7 %collective-permute-start.8 = (f32[280,128]{1,0:T(8,128)S(1)}, f32[280,128]{1,0:T(8,128)S(1)}, u32[]{:S(2)}, u32[]{:S(2)}) collective-permute-start(f32[280,128]{1,0:T(8,128)S(1)} %collective-permute-done.6.refs_1_), channel_id=1, source_target_pairs={{0,4},{4,0},{8,12},{12,8},{16,20},{20,16},{24,28},{28,24},{1,5},{5... | collective-permute-start | bytes 430088 | tf_op jit(solution)/shard_map/ppermute | solution.py:386
  26.8 7.0 %copy-start = (s32[2,2048]{1,0:T(2,128)S(1)}, s32[2,2048]{1,0:T(2,128)}, u32[]{:S(2)}) copy-start(s32[2,2048]{1,0:T(2,128)} %coords_ref.1) | copy-start | bytes 49156
  26.8 7.3 %collective-permute-start.12 = (f32[32,1280]{1,0:T(8,128)S(1)}, f32[32,1280]{1,0:T(8,128)S(1)}, u32[]{:S(2)}, u32[]{:S(2)}) collective-permute-start(f32[32,1280]{1,0:T(8,128)S(1)} %pairs.1.refs_4_), channel_id=1, source_target_pairs={{0,8},{4,12},{8,0},{12,4},{16,24},{20,28},{24,16},{28,20},{1,9},{5... | collective-permute-start | bytes 491528 | tf_op jit(solution)/shard_map/ppermute | solution.py:386
  31.3 7.7 %collective-permute-start.14 = (f32[32,1280]{1,0:T(8,128)S(1)}, f32[32,1280]{1,0:T(8,128)S(1)}, u32[]{:S(2)}, u32[]{:S(2)}) collective-permute-start(f32[32,1280]{1,0:T(8,128)S(1)} %collective-permute-done.13.refs_6_), channel_id=1, source_target_pairs={{0,8},{4,12},{8,0},{12,4},{16,24},{20,28},{24,16},{28,20},{1,9},{5... | collective-permute-start | bytes 491528 | tf_op jit(solution)/shard_map/ppermute | solution.py:386
  31.7 5.5 %collective-permute-start.10 = (f32[264,128]{1,0:T(8,128)S(1)}, f32[264,128]{1,0:T(8,128)S(1)}, u32[]{:S(2)}, u32[]{:S(2)}) collective-permute-start(f32[264,128]{1,0:T(8,128)S(1)} %cross_part.4.refs_0_), channel_id=1, source_target_pairs={{0,2},{1,3},{2,0},{3,1},{4,6},{5,7},{6,4},{7,5},{8,10},{9,11},{10,... | collective-permute-start | bytes 405512 | tf_op jit(solution)/shard_map/ppermute | solution.py:386
  33.2 5.9 %collective-permute-start.11 = (f32[264,128]{1,0:T(8,128)S(1)}, f32[264,128]{1,0:T(8,128)S(1)}, u32[]{:S(2)}, u32[]{:S(2)}) collective-permute-start(f32[264,128]{1,0:T(8,128)S(1)} %cross_part.4.refs_0_), channel_id=1, source_target_pairs={{0,3},{1,2},{2,1},{3,0},{4,7},{5,6},{6,5},{7,4},{8,11},{9,10},{10,... | collective-permute-start | bytes 405512 | tf_op jit(solution)/shard_map/ppermute | solution.py:386
  33.2 5.9 %collective-permute-start.9 = (f32[264,128]{1,0:T(8,128)S(1)}, f32[264,128]{1,0:T(8,128)S(1)}, u32[]{:S(2)}, u32[]{:S(2)}) collective-permute-start(f32[264,128]{1,0:T(8,128)S(1)} %cross_part.4.refs_0_), channel_id=1, source_target_pairs={{0,1},{1,0},{2,3},{3,2},{4,5},{5,4},{6,7},{7,6},{8,9},{9,8},{10,11... | collective-permute-start | bytes 405512 | tf_op jit(solution)/shard_map/ppermute | solution.py:386

commit v5 on v4

--- a/solution.py
+++ b/solution.py
@@ -243,7 +243,7 @@
 
 
 def cross_kernel(number, slots, weight_ref, skip_ref, level_ref, place_ref, high_ref, low_ref, before_ref, *refs):
-    blocks, (sums_ref, out_ref, o_high, o_low, p_ref, m_ref, raw_ref) = refs[: len(number)], refs[len(number) :]
+    blocks, (sums_ref, out_ref, o_ref, p_ref, m_ref, raw_ref) = refs[: len(number)], refs[len(number) :]
     rows = high_ref.shape[0]
     me = lax.axis_index("rows")
     skip = skip_ref[0]
@@ -256,7 +256,8 @@
     scales = [weight_ref[level] / (total[level, 0] - 1.0) for level in range(LEVELS)]
     member_scale = by_level(level_row, scales)
     owner, rank = place_ref[0:1, :], place_ref[1:2, :]
-    padded = o_high.shape[0] // len(number)
+    held = o_ref.shape[0] // 2
+    padded = held // len(number)
     m_ref[...] = jnp.zeros_like(m_ref)
     for n, block_ref in enumerate(blocks):
         at = n * padded
@@ -270,14 +271,14 @@
             columns.append(jnp.sum(member, axis=1, keepdims=True) / counts[level : level + 1, :])
             m_ref[at : at + padded, level : level + 1] = columns[level]
         high, low = split((block - by_level(level_row, columns)) * member_scale, 2)
-        o_high[at : at + padded, :] = high
-        o_low[at : at + padded, :] = low
+        o_ref[at : at + padded, :] = high
+        o_ref[held + at : held + at + padded, :] = low
         slot = lax.broadcasted_iota(jnp.int32, (padded, owner.shape[1]), 0)
         hit = (owner == (me ^ number[n])) & (rank - skip == slot) & (slot < slots)
         p_ref[at : at + padded, :] = hit.astype(BF16)
-    by_slot = dot(high_ref[...], o_high[...], LANES_BOTH)
-    by_slot += dot(high_ref[...], o_low[...], LANES_BOTH)
-    by_slot += dot(low_ref[...], o_high[...], LANES_BOTH)
+    by_piece = dot(high_ref[...], o_ref[...], LANES_BOTH)
+    by_slot = by_piece[:, 0:held] + by_piece[:, held:]
+    by_slot += dot(low_ref[...], o_ref[0:held, :], LANES_BOTH)
     place = p_ref[...]
     cross = sum(dot(piece, place, PLAIN) for piece in split(by_slot, 3))
     out_ref[0:rows, :] = before_ref[0:rows, :] + cross
@@ -296,8 +297,7 @@
         in_specs=[smem, smem] + [vmem] * (6 + len(blocks)),
         out_specs=vmem,
         scratch_shapes=[
-            pltpu.VMEM((held, members), BF16),
-            pltpu.VMEM((held, members), BF16),
+            pltpu.VMEM((2 * held, members), BF16),
             pltpu.VMEM((held, before.shape[1]), BF16),
             pltpu.VMEM((held, SUB), F32),
             pltpu.VMEM((held, members), F32),
@@ -310,8 +310,8 @@
 
 def final_kernel(number, mem, width, weight_ref, taper_ref, sums_ref, *refs):
     parts, refs = refs[:mem], refs[mem:]
-    blocks, (out_ref, w_high, w_low, chunk, sem) = refs[: len(number)], refs[len(number) :]
-    rows = taper_ref.shape[0]
+    blocks, (out_ref, w_ref, chunk, sem) = refs[: len(number)], refs[len(number) :]
+    rows, observed = taper_ref.shape
     members = out_ref.shape[1]
     me = lax.axis_index("rows")
 
@@ -320,8 +320,9 @@
         for side in range(2):
             at = pl.multiple_of((me ^ number[n] ^ side) * length, length)
             high, low = split(block_ref[side * length : (side + 1) * length, :], 2)
-            w_high[pl.ds(at, length), :] = high
-            w_low[pl.ds(at, length), :] = low
+            w_ref[pl.ds(at, length), :] = high
+            w_ref[pl.ds(observed + at, length), :] = low
+            w_ref[pl.ds(2 * observed + at, length), :] = high
 
     cross = sum(ref[0:rows, :] for ref in parts)
     places = range(0, mem * SUB, SUB)
@@ -344,14 +345,12 @@
     cross += dot(left[0], right[1], ROWS_BOTH)
     cross += dot(left[1], right[0], ROWS_BOTH)
     t_high, t_low = split(cross * taper_ref[...], 2)
+    stacked = jnp.concatenate([t_high, t_high, t_low], axis=1)
 
     copies = []
     for n in range(members // width):
         at = n * width
-        out = dot(t_high, w_high[:, at : at + width], PLAIN)
-        out += dot(t_high, w_low[:, at : at + width], PLAIN)
-        out += dot(t_low, w_high[:, at : at + width], PLAIN)
-        chunk[n, :, :] = out
+        chunk[n, :, :] = dot(stacked, w_ref[:, at : at + width], PLAIN)
         copies.append(pltpu.make_async_copy(chunk.at[n], out_ref.at[:, pl.ds(at, width)], sem.at[n]))
         copies[-1].start()
     for copy in copies:
@@ -370,8 +369,7 @@
         in_specs=[smem] + [vmem] * (2 + len(parts) + len(blocks)),
         out_specs=pl.BlockSpec(memory_space=pl.ANY),
         scratch_shapes=[
-            pltpu.VMEM((observed, members), BF16),
-            pltpu.VMEM((observed, members), BF16),
+            pltpu.VMEM((3 * observed, members), BF16),
             pltpu.VMEM((members // width, rows, width), F32),
             pltpu.SemaphoreType.DMA((members // width,)),
         ],

time: 41.5 us -> 41.1 us (level)
  Pallas kernels: 10.6 us -> 9.93 us
    pallas_call x2, Pallas kernels: 3.82 us -> 3.34 us  [cross_part(): pl.pallas_call(functools.partial(cross_kernel, number, slots), out_shape=...]
  transfers between devices with their start and end apart: 15 -> 15, of which waited for: 7 -> 7; matrix products, arithmetic and copies ran while one was open for 0% -> 0% of each run, Pallas kernels for 15% -> 13%
where the time goes in v5:
time: 41.1 us; the launch traced here: 41 us
  starting transfers between devices  16 us (39%)
  waiting for transfers between devices  14.2 us (35%)
  Pallas kernels  9.93 us (24%)
  loops' own time  0.68 us (2%)
    ppermute x15, starting transfers between devices, across(): return lax.ppermute(x, axis, [(i, i ^ bits) for i in range(count)])  16 us
    ppermute x15, waiting for transfers between devices, across(): return lax.ppermute(x, axis, [(i, i ^ bits) for i in range(count)])  14.2 us
    pallas_call x2, Pallas kernels, cross_part(): pl.pallas_call(functools.partial(cross_kernel, number, slots), out_shape=...  3.34 us
    pallas_call x1, Pallas kernels, pick(): pl.pallas_call(functools.partial(pick_kernel, slots), out_shape=jax.Shape...  2.24 us
    pallas_call x1, Pallas kernels, final(): pl.pallas_call(functools.partial(final_kernel, number, len(parts), width)...  2.15 us
    pallas_call x1, Pallas kernels, center(): pl.pallas_call(functools.partial(center_kernel, slots, rows), out_shape=(...  1.9 us
  transfers between devices with their start and end apart: 15, of which 7 were waited for; matrix products, arithmetic and copies ran while one was open for 0% of the time, Pallas kernels for 13%

profile of v5, /device:TPU:0, one launch (start us, length us, event | category | flops | bytes accessed | tf_op | source)
XLA Modules:
  0.0 41.0 jit_solution(12769280651638973381)
XLA Ops:
  0.0 2.2 %pick.2.own_ref.refs_0_ = f32[280,128]{1,0:T(8,128)S(1)} custom-call(s32[128]{0:T(128)} %obs_ref.1, s32[1]{0:T(128)} %constant.28.clone.1.skip_ref, f32[256,1280]{1,0:T(8,128)} %state_ref.2), custom_call_target="tpu_custom_call" | custom-call | flops 1 | bytes 1 | tf_op jit(solution)/shard_map/pick/pallas_call | solution.py:85
  2.3 0.0 copy-start.5
  2.3 4.1 %collective-permute-start.5 = (f32[280,128]{1,0:T(8,128)S(1)}, f32[280,128]{1,0:T(8,128)S(1)}, u32[]{:S(2)}, u32[]{:S(2)}) collective-permute-start(f32[280,128]{1,0:T(8,128)S(1)} %pick.2.own_ref.refs_0_), channel_id=1, source_target_pairs={{0,16},{4,20},{8,24},{12,28},{16,0},{20,4},{24,8},{28,12},{1,17},{... | collective-permute-start | bytes 430088 | tf_op jit(solution)/shard_map/ppermute | solution.py:384
  6.4 1.9 %center.2 = (f32[8,256]{1,0:T(8,128)S(1)}, bf16[256,1280]{1,0:T(8,128)(2,1)S(1)}, bf16[256,1280]{1,0:T(8,128)(2,1)S(1)}, f32[440,128]{1,0:T(8,128)S(1)}, s32[8,1...) custom-call(s32[1,128]{1,0:T(1,128)S(1)} %bitcast.48, f32[280,128]{1,0:T(8,128)S(1)} %pick.2.own_ref.refs_0_, ...), custom_call_target="tpu_custom_call" | custom-call | flops 1 | bytes 1 | tf_op jit(solution)/shard_map/center/pallas_call | solution.py:152
  8.3 0.1 collective-permute-start
  8.4 1.6 %collective-permute-start.3 = (f32[440,128]{1,0:T(8,128)S(1)}, f32[440,128]{1,0:T(8,128)S(1)}, u32[]{:S(2)}, u32[]{:S(2)}) collective-permute-start(f32[440,128]{1,0:T(8,128)S(1)} %get-tuple-element.88), channel_id=1, source_target_pairs={{0,4},{4,0},{8,12},{12,8},{16,20},{20,16},{24,28},{28,24},{1,5},{5... | collective-permute-start | bytes 675848 | tf_op jit(solution)/shard_map/ppermute | solution.py:384
  10.0 1.6 %collective-permute-start.2 = (f32[280,128]{1,0:T(8,128)S(1)}, f32[280,128]{1,0:T(8,128)S(1)}, u32[]{:S(2)}, u32[]{:S(2)}) collective-permute-start(f32[280,128]{1,0:T(8,128)S(1)} %pick.2.own_ref.refs_0_), channel_id=1, source_target_pairs={{0,8},{4,12},{8,0},{12,4},{16,24},{20,28},{24,16},{28,20},{1,9},{5... | collective-permute-start | bytes 430088 | tf_op jit(solution)/shard_map/ppermute | solution.py:384
  11.6 1.6 %collective-permute-start.1 = (f32[16,256]{1,0:T(8,128)S(1)}, f32[16,256]{1,0:T(8,128)S(1)}, u32[]{:S(2)}, u32[]{:S(2)}) collective-permute-start(f32[16,256]{1,0:T(8,128)S(1)} %pad_maximum_fusion), channel_id=1, source_target_pairs={{0,2},{1,3},{2,0},{3,1},{4,6},{5,7},{6,4},{7,5},{8,10},{9,11},{10,... | collective-permute-start | bytes 49160 | tf_op jit(solution)/shard_map/ppermute | solution.py:384
  13.1 2.2 %collective-permute-done.1 = f32[16,256]{1,0:T(8,128)S(1)} collective-permute-done((f32[16,256]{1,0:T(8,128)S(1)}, f32[16,256]{1,0:T(8,128)S(1)}, u32[]{:S(2)}, u32[]{:S(2)}) %collective-permute-start.1) | collective-permute-done | bytes 16416 | tf_op jit(solution)/shard_map/ppermute | solution.py:384
  15.4 0.5 %collective-permute-start.6 = (f32[280,128]{1,0:T(8,128)S(1)}, f32[280,128]{1,0:T(8,128)S(1)}, u32[]{:S(2)}, u32[]{:S(2)}) collective-permute-start(f32[280,128]{1,0:T(8,128)S(1)} %collective-permute-done.5.refs_0_), channel_id=1, source_target_pairs={{0,8},{4,12},{8,0},{12,4},{16,24},{20,28},{24,16},{28,20},{1,9},{5... | collective-permute-start | bytes 430088 | tf_op jit(solution)/shard_map/ppermute | solution.py:384
  15.8 0.7 %while.10 = (s32[]{:T(128)}, f32[264,128]{1,0:T(8,128)S(1)}, s32[1]{0:T(128)}, s32[128]{0:T(128)S(1)}, f32[256,1280]{1,0:T(8,128)}, /*index=5*/f32[16,1280]{1,0:...) while((s32[]{:T(128)}, f32[264,128]{1,0:T(8,128)S(1)}, ...), condition=%wide.region_1.0_spmd, body=%wide.region_0.0_spmd.sunk | while | flops 40 | bytes 11678356 | solution.py:450
  16.5 0.0 collective-permute-done.3.refs_2_.far_ref
  16.6 1.7 %collective-permute-start.13 = (f32[32,1280]{1,0:T(8,128)S(1)}, f32[32,1280]{1,0:T(8,128)S(1)}, u32[]{:S(2)}, u32[]{:S(2)}) collective-permute-start(f32[32,1280]{1,0:T(8,128)S(1)} %pairs.1.refs_4_), channel_id=1, source_target_pairs={{0,16},{4,20},{8,24},{12,28},{16,0},{20,4},{24,8},{28,12},{1,17},{... | collective-permute-start | bytes 491528 | tf_op jit(solution)/shard_map/ppermute | solution.py:384
  18.2 0.0 collective-permute-done.2.refs_1_
  18.2 1.5 %collective-permute-start.4 = (f32[280,128]{1,0:T(8,128)S(1)}, f32[280,128]{1,0:T(8,128)S(1)}, u32[]{:S(2)}, u32[]{:S(2)}) collective-permute-start(f32[280,128]{1,0:T(8,128)S(1)} %collective-permute-done.2.refs_1_), channel_id=1, source_target_pairs={{0,4},{4,0},{8,12},{12,8},{16,20},{20,16},{24,28},{28,24},{1,5},{5... | collective-permute-start | bytes 430088 | tf_op jit(solution)/shard_map/ppermute | solution.py:384
  19.7 0.5 %collective-permute-start.7 = (f32[280,128]{1,0:T(8,128)S(1)}, f32[280,128]{1,0:T(8,128)S(1)}, u32[]{:S(2)}, u32[]{:S(2)}) collective-permute-start(f32[280,128]{1,0:T(8,128)S(1)} %collective-permute-done.5.refs_0_), channel_id=1, source_target_pairs={{0,4},{4,0},{8,12},{12,8},{16,20},{20,16},{24,28},{28,24},{1,5},{5... | collective-permute-start | bytes 430088 | tf_op jit(solution)/shard_map/ppermute | solution.py:384
  20.3 1.4 %collective-permute-done.6.refs_1_ = f32[280,128]{1,0:T(8,128)S(1)} collective-permute-done((f32[280,128]{1,0:T(8,128)S(1)}, f32[280,128]{1,0:T(8,128)S(1)}, u32[]{:S(2)}, u32[]{:S(2)}) %collective-permute-start.6) | collective-permute-done | bytes 143392 | tf_op jit(solution)/shard_map/ppermute | solution.py:384
  21.7 0.1 collective-permute-start.8
  21.8 3.1 %collective-permute-done.4.refs_3_ = f32[280,128]{1,0:T(8,128)S(1)} collective-permute-done((f32[280,128]{1,0:T(8,128)S(1)}, f32[280,128]{1,0:T(8,128)S(1)}, u32[]{:S(2)}, u32[]{:S(2)}) %collective-permute-start.4) | collective-permute-done | bytes 143392 | tf_op jit(solution)/shard_map/ppermute | solution.py:384
  24.9 1.7 %cross_part.3.before_ref = f32[264,128]{1,0:T(8,128)S(1)} custom-call(f32[4]{0:T(128)S(1)} %get-tuple-element.317, s32[1]{0:T(128)} %constant.28.clone.1.skip_ref, s32[1,1280]{1,0:T(1,128)S(1)} %get-tuple-element.313, s32[8,128]{1,0:T(8,128)S(1)} %get-tuple-element.314, bf16[256,1280]{1,0:T(8,128)(2,1)S(1)} %get-tuple-element.81.high_ref, ...), custom_call_target="tpu_custom_call" | custom-call | flops 1 | bytes 1 | tf_op jit(solution)/shard_map/cross_part/pallas_call | solution.py:294
  26.6 0.0 copy-start
  26.6 0.4 collective-permute-start.12
  27.0 0.9 %collective-permute-done.7.refs_2_ = f32[280,128]{1,0:T(8,128)S(1)} collective-permute-done((f32[280,128]{1,0:T(8,128)S(1)}, f32[280,128]{1,0:T(8,128)S(1)}, u32[]{:S(2)}, u32[]{:S(2)}) %collective-permute-start.7) | collective-permute-done | bytes 143392 | tf_op jit(solution)/shard_map/ppermute | solution.py:384
  27.9 1.5 %collective-permute-done.8.refs_3_ = f32[280,128]{1,0:T(8,128)S(1)} collective-permute-done((f32[280,128]{1,0:T(8,128)S(1)}, f32[280,128]{1,0:T(8,128)S(1)}, u32[]{:S(2)}, u32[]{:S(2)}) %collective-permute-start.8) | collective-permute-done | bytes 143392 | tf_op jit(solution)/shard_map/ppermute | solution.py:384
  29.4 1.7 %cross_part.4.refs_0_ = f32[264,128]{1,0:T(8,128)S(1)} custom-call(f32[4]{0:T(128)S(1)} %get-tuple-element.317, s32[1]{0:T(128)} %constant.28.clone.1.skip_ref, s32[1,1280]{1,0:T(1,128)S(1)} %get-tuple-element.313, s32[8,128]{1,0:T(8,128)S(1)} %get-tuple-element.314, bf16[256,1280]{1,0:T(8,128)(2,1)S(1)} %get-tuple-element.81.high_ref, ...), custom_call_target="tpu_custom_call" | custom-call | flops 1 | bytes 1 | tf_op jit(solution)/shard_map/cross_part/pallas_call | solution.py:294
  31.1 0.3 collective-permute-start.14
  31.5 1.5 %collective-permute-start.10 = (f32[264,128]{1,0:T(8,128)S(1)}, f32[264,128]{1,0:T(8,128)S(1)}, u32[]{:S(2)}, u32[]{:S(2)}) collective-permute-start(f32[264,128]{1,0:T(8,128)S(1)} %cross_part.4.refs_0_), channel_id=1, source_target_pairs={{0,2},{1,3},{2,0},{3,1},{4,6},{5,7},{6,4},{7,5},{8,10},{9,11},{10,... | collective-permute-start | bytes 405512 | tf_op jit(solution)/shard_map/ppermute | solution.py:384
  33.0 0.6 %collective-permute-start.9 = (f32[264,128]{1,0:T(8,128)S(1)}, f32[264,128]{1,0:T(8,128)S(1)}, u32[]{:S(2)}, u32[]{:S(2)}) collective-permute-start(f32[264,128]{1,0:T(8,128)S(1)} %cross_part.4.refs_0_), channel_id=1, source_target_pairs={{0,1},{1,0},{2,3},{3,2},{4,5},{5,4},{6,7},{7,6},{8,9},{9,8},{10,11... | collective-permute-start | bytes 405512 | tf_op jit(solution)/shard_map/ppermute | solution.py:384
  33.6 0.3 tapers.1.taper_ref
  33.9 3.1 %collective-permute-done.10.refs_2_ = f32[264,128]{1,0:T(8,128)S(1)} collective-permute-done((f32[264,128]{1,0:T(8,128)S(1)}, f32[264,128]{1,0:T(8,128)S(1)}, u32[]{:S(2)}, u32[]{:S(2)}) %collective-permute-start.10) | collective-permute-done | bytes 135200 | tf_op jit(solution)/shard_map/ppermute | solution.py:384
  37.0 1.8 %collective-permute-done.11.refs_3_ = f32[264,128]{1,0:T(8,128)S(1)} collective-permute-done((f32[264,128]{1,0:T(8,128)S(1)}, f32[264,128]{1,0:T(8,128)S(1)}, u32[]{:S(2)}, u32[]{:S(2)}) %collective-permute-start.11) | collective-permute-done | bytes 135200 | tf_op jit(solution)/shard_map/ppermute | solution.py:384
  38.8 2.2 %final.1 = f32[256,1280]{1,0:T(8,128)} custom-call(f32[4]{0:T(128)S(1)} %get-tuple-element.317, f32[256,128]{1,0:T(8,128)S(1)} %tapers.1.taper_ref, f32[32,256]{1,0:T(8,128)S(1)} %get-tuple-element.312, f32[264,128]{1,0:T(8,128)S(1)} %cross_part.4.refs_0_, f32[264,128]{1,0:T(8,128)S(1)} %collective-permute-done.9.refs_1_, ...), custom_call_target="tpu_custom_call" | custom-call | flops 1 | bytes 1 | tf_op jit(solution)/shard_map/final/pallas_call | solution.py:366
  (23 shorter events, 0.1 us)
Async XLA Ops:
  0.0 6.4 %copy-start.4 = (s32[128]{0:T(128)S(1)}, s32[128]{0:T(128)}, u32[]{:S(2)}) copy-start(s32[128]{0:T(128)} %obs_ref.1) | copy-start | bytes 1540
  0.0 6.4 %copy-start.1 = (f32[256,1280]{1,0:T(8,128)S(1)}, f32[256,1280]{1,0:T(8,128)}, u32[]{:S(2)}) copy-start(f32[256,1280]{1,0:T(8,128)} %state_ref.2) | copy-start | bytes 3932164
  0.0 6.4 %copy-start.6 = (s32[1280]{0:T(1024)S(1)}, s32[1280]{0:T(1024)}, u32[]{:S(2)}) copy-start(s32[1280]{0:T(1024)} %param.9) | copy-start | bytes 15364
  0.0 6.4 %copy-start.3 = (f32[16,1280]{1,0:T(8,128)S(1)}, f32[16,1280]{1,0:T(8,128)}, u32[]{:S(2)}) copy-start(f32[16,1280]{1,0:T(8,128)} %near_ref.1) | copy-start | bytes 245764
  2.3 13.6 %copy-start.5 = (f32[4]{0:T(128)S(1)}, f32[4]{0:T(128)}, u32[]{:S(2)}) copy-start(f32[4]{0:T(128)} %weight_ref.5) | copy-start | bytes 52
  2.3 13.1 %collective-permute-start.5 = (f32[280,128]{1,0:T(8,128)S(1)}, f32[280,128]{1,0:T(8,128)S(1)}, u32[]{:S(2)}, u32[]{:S(2)}) collective-permute-start(f32[280,128]{1,0:T(8,128)S(1)} %pick.2.own_ref.refs_0_), channel_id=1, source_target_pairs={{0,16},{4,20},{8,24},{12,28},{16,0},{20,4},{24,8},{28,12},{1,17},{... | collective-permute-start | bytes 430088 | tf_op jit(solution)/shard_map/ppermute | solution.py:384
  8.3 3.2 %collective-permute-start = (f32[8,256]{1,0:T(8,128)S(1)}, f32[8,256]{1,0:T(8,128)S(1)}, u32[]{:S(2)}, u32[]{:S(2)}) collective-permute-start(f32[8,256]{1,0:T(8,128)S(1)} %get-tuple-element.85), channel_id=1, source_target_pairs={{0,1},{1,0},{2,3},{3,2},{4,5},{5,4},{6,7},{7,6},{8,9},{9,8},{10,11... | collective-permute-start | bytes 24584 | tf_op jit(solution)/shard_map/ppermute | solution.py:384
  8.4 8.1 %collective-permute-start.3 = (f32[440,128]{1,0:T(8,128)S(1)}, f32[440,128]{1,0:T(8,128)S(1)}, u32[]{:S(2)}, u32[]{:S(2)}) collective-permute-start(f32[440,128]{1,0:T(8,128)S(1)} %get-tuple-element.88), channel_id=1, source_target_pairs={{0,4},{4,0},{8,12},{12,8},{16,20},{20,16},{24,28},{28,24},{1,5},{5... | collective-permute-start | bytes 675848 | tf_op jit(solution)/shard_map/ppermute | solution.py:384
  10.0 8.2 %collective-permute-start.2 = (f32[280,128]{1,0:T(8,128)S(1)}, f32[280,128]{1,0:T(8,128)S(1)}, u32[]{:S(2)}, u32[]{:S(2)}) collective-permute-start(f32[280,128]{1,0:T(8,128)S(1)} %pick.2.own_ref.refs_0_), channel_id=1, source_target_pairs={{0,8},{4,12},{8,0},{12,4},{16,24},{20,28},{24,16},{28,20},{1,9},{5... | collective-permute-start | bytes 430088 | tf_op jit(solution)/shard_map/ppermute | solution.py:384
  11.6 3.8 %collective-permute-start.1 = (f32[16,256]{1,0:T(8,128)S(1)}, f32[16,256]{1,0:T(8,128)S(1)}, u32[]{:S(2)}, u32[]{:S(2)}) collective-permute-start(f32[16,256]{1,0:T(8,128)S(1)} %pad_maximum_fusion), channel_id=1, source_target_pairs={{0,2},{1,3},{2,0},{3,1},{4,6},{5,7},{6,4},{7,5},{8,10},{9,11},{10,... | collective-permute-start | bytes 49160 | tf_op jit(solution)/shard_map/ppermute | solution.py:384
  15.4 6.3 %collective-permute-start.6 = (f32[280,128]{1,0:T(8,128)S(1)}, f32[280,128]{1,0:T(8,128)S(1)}, u32[]{:S(2)}, u32[]{:S(2)}) collective-permute-start(f32[280,128]{1,0:T(8,128)S(1)} %collective-permute-done.5.refs_0_), channel_id=1, source_target_pairs={{0,8},{4,12},{8,0},{12,4},{16,24},{20,28},{24,16},{28,20},{1,9},{5... | collective-permute-start | bytes 430088 | tf_op jit(solution)/shard_map/ppermute | solution.py:384
  16.6 14.5 %collective-permute-start.13 = (f32[32,1280]{1,0:T(8,128)S(1)}, f32[32,1280]{1,0:T(8,128)S(1)}, u32[]{:S(2)}, u32[]{:S(2)}) collective-permute-start(f32[32,1280]{1,0:T(8,128)S(1)} %pairs.1.refs_4_), channel_id=1, source_target_pairs={{0,16},{4,20},{8,24},{12,28},{16,0},{20,4},{24,8},{28,12},{1,17},{... | collective-permute-start | bytes 491528 | tf_op jit(solution)/shard_map/ppermute | solution.py:384
  18.2 6.7 %collective-permute-start.4 = (f32[280,128]{1,0:T(8,128)S(1)}, f32[280,128]{1,0:T(8,128)S(1)}, u32[]{:S(2)}, u32[]{:S(2)}) collective-permute-start(f32[280,128]{1,0:T(8,128)S(1)} %collective-permute-done.2.refs_1_), channel_id=1, source_target_pairs={{0,4},{4,0},{8,12},{12,8},{16,20},{20,16},{24,28},{28,24},{1,5},{5... | collective-permute-start | bytes 430088 | tf_op jit(solution)/shard_map/ppermute | solution.py:384
  19.7 8.1 %collective-permute-start.7 = (f32[280,128]{1,0:T(8,128)S(1)}, f32[280,128]{1,0:T(8,128)S(1)}, u32[]{:S(2)}, u32[]{:S(2)}) collective-permute-start(f32[280,128]{1,0:T(8,128)S(1)} %collective-permute-done.5.refs_0_), channel_id=1, source_target_pairs={{0,4},{4,0},{8,12},{12,8},{16,20},{20,16},{24,28},{28,24},{1,5},{5... | collective-permute-start | bytes 430088 | tf_op jit(solution)/shard_map/ppermute | solution.py:384
  21.7 7.7 %collective-permute-start.8 = (f32[280,128]{1,0:T(8,128)S(1)}, f32[280,128]{1,0:T(8,128)S(1)}, u32[]{:S(2)}, u32[]{:S(2)}) collective-permute-start(f32[280,128]{1,0:T(8,128)S(1)} %collective-permute-done.6.refs_1_), channel_id=1, source_target_pairs={{0,4},{4,0},{8,12},{12,8},{16,20},{20,16},{24,28},{28,24},{1,5},{5... | collective-permute-start | bytes 430088 | tf_op jit(solution)/shard_map/ppermute | solution.py:384
  26.6 7.0 %copy-start = (s32[2,2048]{1,0:T(2,128)S(1)}, s32[2,2048]{1,0:T(2,128)}, u32[]{:S(2)}) copy-start(s32[2,2048]{1,0:T(2,128)} %coords_ref.1) | copy-start | bytes 49156
  26.6 7.3 %collective-permute-start.12 = (f32[32,1280]{1,0:T(8,128)S(1)}, f32[32,1280]{1,0:T(8,128)S(1)}, u32[]{:S(2)}, u32[]{:S(2)}) collective-permute-start(f32[32,1280]{1,0:T(8,128)S(1)} %pairs.1.refs_4_), channel_id=1, source_target_pairs={{0,8},{4,12},{8,0},{12,4},{16,24},{20,28},{24,16},{28,20},{1,9},{5... | collective-permute-start | bytes 491528 | tf_op jit(solution)/shard_map/ppermute | solution.py:384
  31.1 7.7 %collective-permute-start.14 = (f32[32,1280]{1,0:T(8,128)S(1)}, f32[32,1280]{1,0:T(8,128)S(1)}, u32[]{:S(2)}, u32[]{:S(2)}) collective-permute-start(f32[32,1280]{1,0:T(8,128)S(1)} %collective-permute-done.13.refs_6_), channel_id=1, source_target_pairs={{0,8},{4,12},{8,0},{12,4},{16,24},{20,28},{24,16},{28,20},{1,9},{5... | collective-permute-start | bytes 491528 | tf_op jit(solution)/shard_map/ppermute | solution.py:384
  31.5 5.6 %collective-permute-start.10 = (f32[264,128]{1,0:T(8,128)S(1)}, f32[264,128]{1,0:T(8,128)S(1)}, u32[]{:S(2)}, u32[]{:S(2)}) collective-permute-start(f32[264,128]{1,0:T(8,128)S(1)} %cross_part.4.refs_0_), channel_id=1, source_target_pairs={{0,2},{1,3},{2,0},{3,1},{4,6},{5,7},{6,4},{7,5},{8,10},{9,11},{10,... | collective-permute-start | bytes 405512 | tf_op jit(solution)/shard_map/ppermute | solution.py:384
  33.0 5.9 %collective-permute-start.11 = (f32[264,128]{1,0:T(8,128)S(1)}, f32[264,128]{1,0:T(8,128)S(1)}, u32[]{:S(2)}, u32[]{:S(2)}) collective-permute-start(f32[264,128]{1,0:T(8,128)S(1)} %cross_part.4.refs_0_), channel_id=1, source_target_pairs={{0,3},{1,2},{2,1},{3,0},{4,7},{5,6},{6,5},{7,4},{8,11},{9,10},{10,... | collective-permute-start | bytes 405512 | tf_op jit(solution)/shard_map/ppermute | solution.py:384
  33.0 5.9 %collective-permute-start.9 = (f32[264,128]{1,0:T(8,128)S(1)}, f32[264,128]{1,0:T(8,128)S(1)}, u32[]{:S(2)}, u32[]{:S(2)}) collective-permute-start(f32[264,128]{1,0:T(8,128)S(1)} %cross_part.4.refs_0_), channel_id=1, source_target_pairs={{0,1},{1,0},{2,3},{3,2},{4,5},{5,4},{6,7},{7,6},{8,9},{9,8},{10,11... | collective-permute-start | bytes 405512 | tf_op jit(solution)/shard_map/ppermute | solution.py:384

commit v6 on v5

--- a/solution.py
+++ b/solution.py
@@ -423,8 +423,8 @@
     forward = line | {0: own_both}
     other = {b ^ 1: across(x, "rows", 1) for b, x in forward.items()}
     blocks = line | other
-    early = [b for b in blocks if b < bits[0]]
-    late = [b for b in blocks if b >= bits[0]]
+    early = [b for b in blocks if b % 2 == 0 or b in (1, bits[0] ^ 1)]
+    late = [b for b in blocks if b not in early]
     weights_pair = pairs(weights, after(other[1], all_sums))
 
     def cross(skip, part, high, low, held, number):

time: 41.1 us -> 41 us (level)
    ppermute x15, waiting for transfers between devices: 14.2 us -> 13.8 us  [across(): return lax.ppermute(x, axis, [(i, i ^ bits) for i in range(count)])]
  transfers between devices with their start and end apart: 15 -> 15, of which waited for: 7 -> 7; matrix products, arithmetic and copies ran while one was open for 0% -> 0% of each run, Pallas kernels for 13% -> 14%
where the time goes in v6:
time: 41 us; the launch traced here: 40.9 us
  starting transfers between devices  16 us (39%)
  waiting for transfers between devices  13.8 us (34%)
  Pallas kernels  10.3 us (25%)
  loops' own time  0.68 us (2%)
    ppermute x15, starting transfers between devices, across(): return lax.ppermute(x, axis, [(i, i ^ bits) for i in range(count)])  16 us
    ppermute x15, waiting for transfers between devices, across(): return lax.ppermute(x, axis, [(i, i ^ bits) for i in range(count)])  13.8 us
    pallas_call x2, Pallas kernels, cross_part(): pl.pallas_call(functools.partial(cross_kernel, number, slots), out_shape=...  3.68 us
    pallas_call x1, Pallas kernels, pick(): pl.pallas_call(functools.partial(pick_kernel, slots), out_shape=jax.Shape...  2.24 us
    pallas_call x1, Pallas kernels, final(): pl.pallas_call(functools.partial(final_kernel, number, len(parts), width)...  2.15 us
    pallas_call x1, Pallas kernels, center(): pl.pallas_call(functools.partial(center_kernel, slots, rows), out_shape=(...  1.9 us
  transfers between devices with their start and end apart: 15, of which 7 were waited for; matrix products, arithmetic and copies ran while one was open for 0% of the time, Pallas kernels for 14%

profile of v6, /device:TPU:0, one launch (start us, length us, event | category | flops | bytes accessed | tf_op | source)
XLA Modules:
  0.0 40.9 jit_solution(16056150699035391419)
XLA Ops:
  0.0 2.2 %pick.2.own_ref.refs_0_ = f32[280,128]{1,0:T(8,128)S(1)} custom-call(s32[128]{0:T(128)} %obs_ref.1, s32[1]{0:T(128)} %constant.28.clone.1.skip_ref, f32[256,1280]{1,0:T(8,128)} %state_ref.2), custom_call_target="tpu_custom_call" | custom-call | flops 1 | bytes 1 | tf_op jit(solution)/shard_map/pick/pallas_call | solution.py:85
  2.3 0.0 copy-start.5
  2.3 4.1 %collective-permute-start.3 = (f32[280,128]{1,0:T(8,128)S(1)}, f32[280,128]{1,0:T(8,128)S(1)}, u32[]{:S(2)}, u32[]{:S(2)}) collective-permute-start(f32[280,128]{1,0:T(8,128)S(1)} %pick.2.own_ref.refs_0_), channel_id=1, source_target_pairs={{0,16},{4,20},{8,24},{12,28},{16,0},{20,4},{24,8},{28,12},{1,17},{... | collective-permute-start | bytes 430088 | tf_op jit(solution)/shard_map/ppermute | solution.py:384
  6.4 1.9 %center.2 = (f32[8,256]{1,0:T(8,128)S(1)}, bf16[256,1280]{1,0:T(8,128)(2,1)S(1)}, bf16[256,1280]{1,0:T(8,128)(2,1)S(1)}, f32[440,128]{1,0:T(8,128)S(1)}, s32[8,1...) custom-call(s32[1,128]{1,0:T(1,128)S(1)} %bitcast.48, f32[280,128]{1,0:T(8,128)S(1)} %pick.2.own_ref.refs_0_, ...), custom_call_target="tpu_custom_call" | custom-call | flops 1 | bytes 1 | tf_op jit(solution)/shard_map/center/pallas_call | solution.py:152
  8.3 0.1 collective-permute-start
  8.4 1.6 %collective-permute-start.5 = (f32[440,128]{1,0:T(8,128)S(1)}, f32[440,128]{1,0:T(8,128)S(1)}, u32[]{:S(2)}, u32[]{:S(2)}) collective-permute-start(f32[440,128]{1,0:T(8,128)S(1)} %get-tuple-element.88), channel_id=1, source_target_pairs={{0,4},{4,0},{8,12},{12,8},{16,20},{20,16},{24,28},{28,24},{1,5},{5... | collective-permute-start | bytes 675848 | tf_op jit(solution)/shard_map/ppermute | solution.py:384
  10.0 1.6 %collective-permute-start.2 = (f32[280,128]{1,0:T(8,128)S(1)}, f32[280,128]{1,0:T(8,128)S(1)}, u32[]{:S(2)}, u32[]{:S(2)}) collective-permute-start(f32[280,128]{1,0:T(8,128)S(1)} %pick.2.own_ref.refs_0_), channel_id=1, source_target_pairs={{0,8},{4,12},{8,0},{12,4},{16,24},{20,28},{24,16},{28,20},{1,9},{5... | collective-permute-start | bytes 430088 | tf_op jit(solution)/shard_map/ppermute | solution.py:384
  11.6 1.6 %collective-permute-start.1 = (f32[16,256]{1,0:T(8,128)S(1)}, f32[16,256]{1,0:T(8,128)S(1)}, u32[]{:S(2)}, u32[]{:S(2)}) collective-permute-start(f32[16,256]{1,0:T(8,128)S(1)} %pad_maximum_fusion), channel_id=1, source_target_pairs={{0,2},{1,3},{2,0},{3,1},{4,6},{5,7},{6,4},{7,5},{8,10},{9,11},{10,... | collective-permute-start | bytes 49160 | tf_op jit(solution)/shard_map/ppermute | solution.py:384
  13.1 2.2 %collective-permute-done.1 = f32[16,256]{1,0:T(8,128)S(1)} collective-permute-done((f32[16,256]{1,0:T(8,128)S(1)}, f32[16,256]{1,0:T(8,128)S(1)}, u32[]{:S(2)}, u32[]{:S(2)}) %collective-permute-start.1) | collective-permute-done | bytes 16416 | tf_op jit(solution)/shard_map/ppermute | solution.py:384
  15.4 0.5 %collective-permute-start.4 = (f32[280,128]{1,0:T(8,128)S(1)}, f32[280,128]{1,0:T(8,128)S(1)}, u32[]{:S(2)}, u32[]{:S(2)}) collective-permute-start(f32[280,128]{1,0:T(8,128)S(1)} %collective-permute-done.3.refs_2_), channel_id=1, source_target_pairs={{0,8},{4,12},{8,0},{12,4},{16,24},{20,28},{24,16},{28,20},{1,9},{5... | collective-permute-start | bytes 430088 | tf_op jit(solution)/shard_map/ppermute | solution.py:384
  15.8 0.7 %while.10 = (s32[]{:T(128)}, f32[264,128]{1,0:T(8,128)S(1)}, s32[1]{0:T(128)}, s32[128]{0:T(128)S(1)}, f32[256,1280]{1,0:T(8,128)}, /*index=5*/f32[16,1280]{1,0:...) while((s32[]{:T(128)}, f32[264,128]{1,0:T(8,128)S(1)}, ...), condition=%wide.region_1.0_spmd, body=%wide.region_0.0_spmd.sunk | while | flops 40 | bytes 11678356 | solution.py:450
  16.5 0.0 collective-permute-done.5.refs_4_.far_ref
  16.6 1.7 %collective-permute-start.13 = (f32[32,1280]{1,0:T(8,128)S(1)}, f32[32,1280]{1,0:T(8,128)S(1)}, u32[]{:S(2)}, u32[]{:S(2)}) collective-permute-start(f32[32,1280]{1,0:T(8,128)S(1)} %pairs.1.refs_4_), channel_id=1, source_target_pairs={{0,16},{4,20},{8,24},{12,28},{16,0},{20,4},{24,8},{28,12},{1,17},{... | collective-permute-start | bytes 491528 | tf_op jit(solution)/shard_map/ppermute | solution.py:384
  18.2 1.5 %collective-permute-start.6 = (f32[280,128]{1,0:T(8,128)S(1)}, f32[280,128]{1,0:T(8,128)S(1)}, u32[]{:S(2)}, u32[]{:S(2)}) collective-permute-start(f32[280,128]{1,0:T(8,128)S(1)} %collective-permute-done.3.refs_2_), channel_id=1, source_target_pairs={{0,4},{4,0},{8,12},{12,8},{16,20},{20,16},{24,28},{28,24},{1,5},{5... | collective-permute-start | bytes 430088 | tf_op jit(solution)/shard_map/ppermute | solution.py:384
  19.7 0.5 %collective-permute-start.7 = (f32[280,128]{1,0:T(8,128)S(1)}, f32[280,128]{1,0:T(8,128)S(1)}, u32[]{:S(2)}, u32[]{:S(2)}) collective-permute-start(f32[280,128]{1,0:T(8,128)S(1)} %collective-permute-done.2.refs_1_), channel_id=1, source_target_pairs={{0,4},{4,0},{8,12},{12,8},{16,20},{20,16},{24,28},{28,24},{1,5},{5... | collective-permute-start | bytes 430088 | tf_op jit(solution)/shard_map/ppermute | solution.py:384
  20.3 1.4 %collective-permute-done.4.refs_3_ = f32[280,128]{1,0:T(8,128)S(1)} collective-permute-done((f32[280,128]{1,0:T(8,128)S(1)}, f32[280,128]{1,0:T(8,128)S(1)}, u32[]{:S(2)}, u32[]{:S(2)}) %collective-permute-start.4) | collective-permute-done | bytes 143392 | tf_op jit(solution)/shard_map/ppermute | solution.py:384
  21.7 0.1 collective-permute-start.8
  21.8 3.1 %collective-permute-done.6.refs_5_ = f32[280,128]{1,0:T(8,128)S(1)} collective-permute-done((f32[280,128]{1,0:T(8,128)S(1)}, f32[280,128]{1,0:T(8,128)S(1)}, u32[]{:S(2)}, u32[]{:S(2)}) %collective-permute-start.6) | collective-permute-done | bytes 143392 | tf_op jit(solution)/shard_map/ppermute | solution.py:384
  24.9 2.1 %cross_part.3.before_ref = f32[264,128]{1,0:T(8,128)S(1)} custom-call(f32[4]{0:T(128)S(1)} %get-tuple-element.316, s32[1]{0:T(128)} %constant.28.clone.1.skip_ref, s32[1,1280]{1,0:T(1,128)S(1)} %get-tuple-element.313, s32[8,128]{1,0:T(8,128)S(1)} %get-tuple-element.314, bf16[256,1280]{1,0:T(8,128)(2,1)S(1)} %get-tuple-element.81.high_ref, ...), custom_call_target="tpu_custom_call" | custom-call | flops 1 | bytes 1 | tf_op jit(solution)/shard_map/cross_part/pallas_call | solution.py:294
  27.0 0.4 collective-permute-start.12
  27.4 0.5 %collective-permute-done.7.refs_0_ = f32[280,128]{1,0:T(8,128)S(1)} collective-permute-done((f32[280,128]{1,0:T(8,128)S(1)}, f32[280,128]{1,0:T(8,128)S(1)}, u32[]{:S(2)}, u32[]{:S(2)}) %collective-permute-start.7) | collective-permute-done | bytes 143392 | tf_op jit(solution)/shard_map/ppermute | solution.py:384
  27.9 1.5 %collective-permute-done.8.refs_1_ = f32[280,128]{1,0:T(8,128)S(1)} collective-permute-done((f32[280,128]{1,0:T(8,128)S(1)}, f32[280,128]{1,0:T(8,128)S(1)}, u32[]{:S(2)}, u32[]{:S(2)}) %collective-permute-start.8) | collective-permute-done | bytes 143392 | tf_op jit(solution)/shard_map/ppermute | solution.py:384
  29.4 1.6 %cross_part.4.refs_0_ = f32[264,128]{1,0:T(8,128)S(1)} custom-call(f32[4]{0:T(128)S(1)} %get-tuple-element.316, s32[1]{0:T(128)} %constant.28.clone.1.skip_ref, s32[1,1280]{1,0:T(1,128)S(1)} %get-tuple-element.313, s32[8,128]{1,0:T(8,128)S(1)} %get-tuple-element.314, bf16[256,1280]{1,0:T(8,128)(2,1)S(1)} %get-tuple-element.81.high_ref, ...), custom_call_target="tpu_custom_call" | custom-call | flops 1 | bytes 1 | tf_op jit(solution)/shard_map/cross_part/pallas_call | solution.py:294
  31.0 0.0 collective-permute-done.13.refs_6_
  31.0 0.3 collective-permute-start.14
  31.3 1.5 %collective-permute-start.10 = (f32[264,128]{1,0:T(8,128)S(1)}, f32[264,128]{1,0:T(8,128)S(1)}, u32[]{:S(2)}, u32[]{:S(2)}) collective-permute-start(f32[264,128]{1,0:T(8,128)S(1)} %cross_part.4.refs_0_), channel_id=1, source_target_pairs={{0,2},{1,3},{2,0},{3,1},{4,6},{5,7},{6,4},{7,5},{8,10},{9,11},{10,... | collective-permute-start | bytes 405512 | tf_op jit(solution)/shard_map/ppermute | solution.py:384
  32.8 0.0 collective-permute-start.11
  32.8 0.6 %collective-permute-start.9 = (f32[264,128]{1,0:T(8,128)S(1)}, f32[264,128]{1,0:T(8,128)S(1)}, u32[]{:S(2)}, u32[]{:S(2)}) collective-permute-start(f32[264,128]{1,0:T(8,128)S(1)} %cross_part.4.refs_0_), channel_id=1, source_target_pairs={{0,1},{1,0},{2,3},{3,2},{4,5},{5,4},{6,7},{7,6},{8,9},{9,8},{10,11... | collective-permute-start | bytes 405512 | tf_op jit(solution)/shard_map/ppermute | solution.py:384
  33.5 0.3 tapers.1.taper_ref
  33.8 3.1 %collective-permute-done.10.refs_2_ = f32[264,128]{1,0:T(8,128)S(1)} collective-permute-done((f32[264,128]{1,0:T(8,128)S(1)}, f32[264,128]{1,0:T(8,128)S(1)}, u32[]{:S(2)}, u32[]{:S(2)}) %collective-permute-start.10) | collective-permute-done | bytes 135200 | tf_op jit(solution)/shard_map/ppermute | solution.py:384
  36.9 1.8 %collective-permute-done.11.refs_3_ = f32[264,128]{1,0:T(8,128)S(1)} collective-permute-done((f32[264,128]{1,0:T(8,128)S(1)}, f32[264,128]{1,0:T(8,128)S(1)}, u32[]{:S(2)}, u32[]{:S(2)}) %collective-permute-start.11) | collective-permute-done | bytes 135200 | tf_op jit(solution)/shard_map/ppermute | solution.py:384
  38.7 2.1 %final.1 = f32[256,1280]{1,0:T(8,128)} custom-call(f32[4]{0:T(128)S(1)} %get-tuple-element.316, f32[256,128]{1,0:T(8,128)S(1)} %tapers.1.taper_ref, f32[32,256]{1,0:T(8,128)S(1)} %get-tuple-element.312, f32[264,128]{1,0:T(8,128)S(1)} %cross_part.4.refs_0_, f32[264,128]{1,0:T(8,128)S(1)} %collective-permute-done.9.refs_1_, ...), custom_call_target="tpu_custom_call" | custom-call | flops 1 | bytes 1 | tf_op jit(solution)/shard_map/final/pallas_call | solution.py:366
  (23 shorter events, 0.1 us)
Async XLA Ops:
  0.0 6.4 %copy-start.4 = (s32[128]{0:T(128)S(1)}, s32[128]{0:T(128)}, u32[]{:S(2)}) copy-start(s32[128]{0:T(128)} %obs_ref.1) | copy-start | bytes 1540
  0.0 6.4 %copy-start.1 = (f32[256,1280]{1,0:T(8,128)S(1)}, f32[256,1280]{1,0:T(8,128)}, u32[]{:S(2)}) copy-start(f32[256,1280]{1,0:T(8,128)} %state_ref.2) | copy-start | bytes 3932164
  0.0 6.4 %copy-start.6 = (s32[1280]{0:T(1024)S(1)}, s32[1280]{0:T(1024)}, u32[]{:S(2)}) copy-start(s32[1280]{0:T(1024)} %param.9) | copy-start | bytes 15364
  0.0 6.4 %copy-start.3 = (f32[16,1280]{1,0:T(8,128)S(1)}, f32[16,1280]{1,0:T(8,128)}, u32[]{:S(2)}) copy-start(f32[16,1280]{1,0:T(8,128)} %near_ref.1) | copy-start | bytes 245764
  2.3 13.6 %copy-start.5 = (f32[4]{0:T(128)S(1)}, f32[4]{0:T(128)}, u32[]{:S(2)}) copy-start(f32[4]{0:T(128)} %weight_ref.5) | copy-start | bytes 52
  2.3 13.1 %collective-permute-start.3 = (f32[280,128]{1,0:T(8,128)S(1)}, f32[280,128]{1,0:T(8,128)S(1)}, u32[]{:S(2)}, u32[]{:S(2)}) collective-permute-start(f32[280,128]{1,0:T(8,128)S(1)} %pick.2.own_ref.refs_0_), channel_id=1, source_target_pairs={{0,16},{4,20},{8,24},{12,28},{16,0},{20,4},{24,8},{28,12},{1,17},{... | collective-permute-start | bytes 430088 | tf_op jit(solution)/shard_map/ppermute | solution.py:384
  8.3 3.2 %collective-permute-start = (f32[8,256]{1,0:T(8,128)S(1)}, f32[8,256]{1,0:T(8,128)S(1)}, u32[]{:S(2)}, u32[]{:S(2)}) collective-permute-start(f32[8,256]{1,0:T(8,128)S(1)} %get-tuple-element.85), channel_id=1, source_target_pairs={{0,1},{1,0},{2,3},{3,2},{4,5},{5,4},{6,7},{7,6},{8,9},{9,8},{10,11... | collective-permute-start | bytes 24584 | tf_op jit(solution)/shard_map/ppermute | solution.py:384
  8.4 8.1 %collective-permute-start.5 = (f32[440,128]{1,0:T(8,128)S(1)}, f32[440,128]{1,0:T(8,128)S(1)}, u32[]{:S(2)}, u32[]{:S(2)}) collective-permute-start(f32[440,128]{1,0:T(8,128)S(1)} %get-tuple-element.88), channel_id=1, source_target_pairs={{0,4},{4,0},{8,12},{12,8},{16,20},{20,16},{24,28},{28,24},{1,5},{5... | collective-permute-start | bytes 675848 | tf_op jit(solution)/shard_map/ppermute | solution.py:384
  10.0 9.8 %collective-permute-start.2 = (f32[280,128]{1,0:T(8,128)S(1)}, f32[280,128]{1,0:T(8,128)S(1)}, u32[]{:S(2)}, u32[]{:S(2)}) collective-permute-start(f32[280,128]{1,0:T(8,128)S(1)} %pick.2.own_ref.refs_0_), channel_id=1, source_target_pairs={{0,8},{4,12},{8,0},{12,4},{16,24},{20,28},{24,16},{28,20},{1,9},{5... | collective-permute-start | bytes 430088 | tf_op jit(solution)/shard_map/ppermute | solution.py:384
  11.6 3.8 %collective-permute-start.1 = (f32[16,256]{1,0:T(8,128)S(1)}, f32[16,256]{1,0:T(8,128)S(1)}, u32[]{:S(2)}, u32[]{:S(2)}) collective-permute-start(f32[16,256]{1,0:T(8,128)S(1)} %pad_maximum_fusion), channel_id=1, source_target_pairs={{0,2},{1,3},{2,0},{3,1},{4,6},{5,7},{6,4},{7,5},{8,10},{9,11},{10,... | collective-permute-start | bytes 49160 | tf_op jit(solution)/shard_map/ppermute | solution.py:384
  15.4 6.3 %collective-permute-start.4 = (f32[280,128]{1,0:T(8,128)S(1)}, f32[280,128]{1,0:T(8,128)S(1)}, u32[]{:S(2)}, u32[]{:S(2)}) collective-permute-start(f32[280,128]{1,0:T(8,128)S(1)} %collective-permute-done.3.refs_2_), channel_id=1, source_target_pairs={{0,8},{4,12},{8,0},{12,4},{16,24},{20,28},{24,16},{28,20},{1,9},{5... | collective-permute-start | bytes 430088 | tf_op jit(solution)/shard_map/ppermute | solution.py:384
  16.6 14.4 %collective-permute-start.13 = (f32[32,1280]{1,0:T(8,128)S(1)}, f32[32,1280]{1,0:T(8,128)S(1)}, u32[]{:S(2)}, u32[]{:S(2)}) collective-permute-start(f32[32,1280]{1,0:T(8,128)S(1)} %pairs.1.refs_4_), channel_id=1, source_target_pairs={{0,16},{4,20},{8,24},{12,28},{16,0},{20,4},{24,8},{28,12},{1,17},{... | collective-permute-start | bytes 491528 | tf_op jit(solution)/shard_map/ppermute | solution.py:384
  18.2 6.7 %collective-permute-start.6 = (f32[280,128]{1,0:T(8,128)S(1)}, f32[280,128]{1,0:T(8,128)S(1)}, u32[]{:S(2)}, u32[]{:S(2)}) collective-permute-start(f32[280,128]{1,0:T(8,128)S(1)} %collective-permute-done.3.refs_2_), channel_id=1, source_target_pairs={{0,4},{4,0},{8,12},{12,8},{16,20},{20,16},{24,28},{28,24},{1,5},{5... | collective-permute-start | bytes 430088 | tf_op jit(solution)/shard_map/ppermute | solution.py:384
  19.7 8.1 %collective-permute-start.7 = (f32[280,128]{1,0:T(8,128)S(1)}, f32[280,128]{1,0:T(8,128)S(1)}, u32[]{:S(2)}, u32[]{:S(2)}) collective-permute-start(f32[280,128]{1,0:T(8,128)S(1)} %collective-permute-done.2.refs_1_), channel_id=1, source_target_pairs={{0,4},{4,0},{8,12},{12,8},{16,20},{20,16},{24,28},{28,24},{1,5},{5... | collective-permute-start | bytes 430088 | tf_op jit(solution)/shard_map/ppermute | solution.py:384
  21.7 7.7 %collective-permute-start.8 = (f32[280,128]{1,0:T(8,128)S(1)}, f32[280,128]{1,0:T(8,128)S(1)}, u32[]{:S(2)}, u32[]{:S(2)}) collective-permute-start(f32[280,128]{1,0:T(8,128)S(1)} %collective-permute-done.4.refs_3_), channel_id=1, source_target_pairs={{0,4},{4,0},{8,12},{12,8},{16,20},{20,16},{24,28},{28,24},{1,5},{5... | collective-permute-start | bytes 430088 | tf_op jit(solution)/shard_map/ppermute | solution.py:384
  27.0 6.4 %copy-start = (s32[2,2048]{1,0:T(2,128)S(1)}, s32[2,2048]{1,0:T(2,128)}, u32[]{:S(2)}) copy-start(s32[2,2048]{1,0:T(2,128)} %coords_ref.1) | copy-start | bytes 49156
  27.0 6.7 %collective-permute-start.12 = (f32[32,1280]{1,0:T(8,128)S(1)}, f32[32,1280]{1,0:T(8,128)S(1)}, u32[]{:S(2)}, u32[]{:S(2)}) collective-permute-start(f32[32,1280]{1,0:T(8,128)S(1)} %pairs.1.refs_4_), channel_id=1, source_target_pairs={{0,8},{4,12},{8,0},{12,4},{16,24},{20,28},{24,16},{28,20},{1,9},{5... | collective-permute-start | bytes 491528 | tf_op jit(solution)/shard_map/ppermute | solution.py:384
  31.0 7.7 %collective-permute-start.14 = (f32[32,1280]{1,0:T(8,128)S(1)}, f32[32,1280]{1,0:T(8,128)S(1)}, u32[]{:S(2)}, u32[]{:S(2)}) collective-permute-start(f32[32,1280]{1,0:T(8,128)S(1)} %collective-permute-done.13.refs_6_), channel_id=1, source_target_pairs={{0,8},{4,12},{8,0},{12,4},{16,24},{20,28},{24,16},{28,20},{1,9},{5... | collective-permute-start | bytes 491528 | tf_op jit(solution)/shard_map/ppermute | solution.py:384
  31.3 5.5 %collective-permute-start.10 = (f32[264,128]{1,0:T(8,128)S(1)}, f32[264,128]{1,0:T(8,128)S(1)}, u32[]{:S(2)}, u32[]{:S(2)}) collective-permute-start(f32[264,128]{1,0:T(8,128)S(1)} %cross_part.4.refs_0_), channel_id=1, source_target_pairs={{0,2},{1,3},{2,0},{3,1},{4,6},{5,7},{6,4},{7,5},{8,10},{9,11},{10,... | collective-permute-start | bytes 405512 | tf_op jit(solution)/shard_map/ppermute | solution.py:384
  32.8 5.9 %collective-permute-start.11 = (f32[264,128]{1,0:T(8,128)S(1)}, f32[264,128]{1,0:T(8,128)S(1)}, u32[]{:S(2)}, u32[]{:S(2)}) collective-permute-start(f32[264,128]{1,0:T(8,128)S(1)} %cross_part.4.refs_0_), channel_id=1, source_target_pairs={{0,3},{1,2},{2,1},{3,0},{4,7},{5,6},{6,5},{7,4},{8,11},{9,10},{10,... | collective-permute-start | bytes 405512 | tf_op jit(solution)/shard_map/ppermute | solution.py:384
  32.8 5.9 %collective-permute-start.9 = (f32[264,128]{1,0:T(8,128)S(1)}, f32[264,128]{1,0:T(8,128)S(1)}, u32[]{:S(2)}, u32[]{:S(2)}) collective-permute-start(f32[264,128]{1,0:T(8,128)S(1)} %cross_part.4.refs_0_), channel_id=1, source_target_pairs={{0,1},{1,0},{2,3},{3,2},{4,5},{5,4},{6,7},{7,6},{8,9},{9,8},{10,11... | collective-permute-start | bytes 405512 | tf_op jit(solution)/shard_map/ppermute | solution.py:384
